TPU v7x, 512 devices: a whole 4x4x16 slice. The times are simulated.
512 devices in a mesh: row: 32 (over z_hi, x, y), col: 16 (over z_lo, core).
Axes of the slice: x: 4, y: 4, z: 16 (z_hi: 2, z_lo: 8; z = z_hi * 8 + z_lo), core: 2. Of those that a mesh axis runs over, the one named last changes fastest.
Arguments:
- a_blocks: float32 [128, 32, 128, 128], P('row', 'col'), may hold values from -0.09375 to 0.09375
- b_blocks: float32 [32, 64, 128, 128], P('row', 'col'), may hold values from -6 to 6
- a_occupied: int32 [128, 32], P('row', 'col'), may hold values from 0 to 1, as said below
- b_occupied: int32 [32, 64], P('row', 'col'), may hold values 0 or 1
- c_filter: int32 [128, 64], P('row', 'col'), may hold values 0 or 1
- row_sizes: int32 [128], P('row'), may hold values from 32 to 128, as said below
- k_sizes: int32 [32], replicated, may hold values from 32 to 128, as said below
- col_sizes: int32 [64], P('col'), may hold values from 32 to 128, as said below
Outputs:
- c_product: float32 [128, 64, 128, 128], P('row', 'col')
Inputs may be any that keep to these rules, and one draw needn't show every extreme that they name: `a_occupied`: at most 6 of the 4 x 2 blocks that one device holds are occupied, and some device holds exactly 6. `row_sizes`: some block row uses all 128 rows. `k_sizes`: some inner block index uses all 128 rows. `col_sizes`: some block column uses all 128 columns.
All inputs are finite; a program needn't handle non-finite values. No bound on the sum of `b_occupied` or of `c_filter` on one device may be relied on, other than what follows from the above.
Results may differ from a plain program's by a relative error of at most 0.00007.
Values sent between devices are 32-bit elements; how exact they have to be, the bound alone decides.
No kernel may reach another device: no remote copies, remote signals or barrier semaphores. Data moves between devices by JAX's collectives and lax.ppermute only.
A program may use at most 64 MiB of HBM per device.

v0:
```python
import jax
import jax.numpy as jnp
from jax import lax
from jax.sharding import PartitionSpec as P


def masked_blocks(blocks, occupied, row_used, col_used):
    size = blocks.shape[-1]
    line = jnp.arange(size, dtype=jnp.int32)
    rows_fine = line[None, None, :, None] < row_used[:, None, None, None]
    cols_fine = line[None, None, None, :] < col_used[None, :, None, None]
    keep = (occupied[:, :, None, None] > 0) & rows_fine & cols_fine
    return jnp.where(keep, blocks, jnp.zeros_like(blocks))


def on_device(a_blocks, b_blocks, a_occupied, b_occupied, c_filter, row_sizes, k_sizes, col_sizes):
    k_local = a_blocks.shape[1]
    k_rows = b_blocks.shape[0]
    left_used = lax.dynamic_slice_in_dim(k_sizes, lax.axis_index("col") * k_local, k_local)
    right_used = lax.dynamic_slice_in_dim(k_sizes, lax.axis_index("row") * k_rows, k_rows)
    left = masked_blocks(a_blocks, a_occupied, row_sizes, left_used)
    right = masked_blocks(b_blocks, b_occupied, right_used, col_sizes)
    right_panel = lax.all_gather(right, "row", axis=0, tiled=True)
    product = jnp.einsum(
        "ikab,kjbc->ijac",
        lax.all_gather(left, "col", axis=1, tiled=True),
        right_panel,
        precision=lax.Precision.HIGHEST,
    )
    return jnp.where(c_filter[:, :, None, None] > 0, product, jnp.zeros_like(product))


def solution(mesh):
    placed = (
        P("row", "col", None, None),
        P("row", "col", None, None),
        P("row", "col"),
        P("row", "col"),
        P("row", "col"),
        P("row"),
        P(),
        P("col"),
    )
    return jax.shard_map(
        on_device,
        mesh=mesh,
        in_specs=placed,
        out_specs=P("row", "col", None, None),
        check_vma=False,
    )
```

profile of v0, /device:TPU:100, one launch (start us, length us, event | category | flops | bytes accessed | tf_op | source)
XLA Modules:
  0.0 412.5 jit_solution(13725251406724489667)
XLA Ops:
  6.5 0.0 all-gather.5.cloned.1.call-start
  6.5 0.7 dynamic_slice.7
  7.3 0.1 iota_compare_fusion.2
  7.3 0.7 broadcast_compare_fusion.1
  8.0 0.1 copy.11
  8.1 0.7 iota_compare_fusion
  8.9 0.1 broadcast_and_fusion
  8.9 2.0 and_select_fusion
  11.0 0.0 all-gather.5.cloned.1.call-update
  11.0 0.0 all-gather.3.cloned.1.call-start
  11.1 1.3 dynamic_slice.6
  12.3 1.1 copy.10
  13.4 0.6 iota_compare_fusion.3
  14.0 0.7 compare_bitcast_fusion
  14.7 0.7 iota_compare_fusion.1
  15.4 0.8 and_select_fusion.1
  16.3 0.0 all-gather.3.cloned.1.call-update
  16.3 0.7 broadcast_compare_fusion
  17.0 0.1 copy.9
  17.1 91.4 %all-gather.5.cloned.1.call-done = f32[4,32,128,128]{3,2,1,0:T(8,128)} async-done(((f32[4,2,128,128]{3,2,1,0:T(8,128)}), f32[4,32,128,128]{3,2,1,0:T(8,128)}) %all-gather.5.cloned.1.call-update) | async-done | bytes 8388624 | tf_op jit(solution)/shard_map/all_gather | solution.py:26
  108.5 279.3 %all-gather.3.cloned.1.call-done = f32[32,4,128,128]{2,3,0,1:T(8,128)} async-done(((f32[1,4,128,128]{2,3,0,1:T(8,128)}), f32[32,4,128,128]{2,3,0,1:T(8,128)}) %all-gather.3.cloned.1.call-update) | async-done | bytes 8388624 | tf_op jit(solution)/shard_map/all_gather | solution.py:23
  387.8 16.6 %fusion.8 = f32[4,4,128,128]{2,3,0,1:T(8,128)S(1)} fusion(f32[4,32,128,128]{3,2,1,0:T(8,128)} %all-gather.5.cloned.1.call-done, f32[32,4,128,128]{2,3,0,1:T(8,128)} %all-gather.3.cloned.1.call-done, pred[4,4]{0,1:T(4,128)(4,1)S(1)} %copy.9), kind=kOutput, calls=%fused_computation.4 | convolution fusion | flops 12885164032 | bytes 17825808 | tf_op jit(solution)/shard_map/ikab,kjbc->ijac/dot_general | solution.py:24
  404.3 1.3 copy.12
Async XLA Ops:
  6.5 101.9 %all-gather.5.cloned.1.call-start = ((), (), s32[]{:S(2)}) async-start(), calls=%async_computation.1 | async-start | bytes 8912896 | tf_op jit(solution)/shard_map/all_gather | solution.py:26
  11.0 376.8 %all-gather.3.cloned.1.call-start = ((), (), s32[]{:S(2)}) async-start(), calls=%async_computation | async-start | bytes 8650752 | tf_op jit(solution)/shard_map/all_gather | solution.py:23
Sparse Core Ops, SparseCore 0:
  11.1 97.3 all-gather.4
  112.8 274.9 all-gather.2
where the time goes:
time: 413 us; the launch traced here: 412 us
  waiting for transfers between devices  371 us (90%)
  matrix products  16.6 us (4%)
  between operations  13.4 us (3%)
  other arithmetic  7.16 us (2%)
  local copies, waits for them, and re-layouts  4.59 us (1%)
    all_gather x1, waiting for transfers between devices, on_device(): right_panel = lax.all_gather(right, 'row', axis=0, tiled=True)  279 us
    all_gather x1, waiting for transfers between devices, on_device(): lax.all_gather(left, 'col', axis=1, tiled=True)  91.4 us
    dot_general x1, matrix products, on_device(): jnp.einsum('ikab,kjbc->ijac', lax.all_gather(left, 'col', axis=1, tiled=T...  16.6 us
  transfers between devices with their start and end apart: 2, of which 2 were waited for; matrix products, arithmetic and copies ran while one was open for 1% of the time, Pallas kernels for 0%

commit v1 on v0

v1 whole, which is shorter than its diff:
```python
import functools

import jax
import jax.numpy as jnp
from jax import lax
from jax.experimental import pallas as pl
from jax.experimental.pallas import tpu as pltpu
from jax.sharding import PartitionSpec as P

BS = 128
CAP = 6
SLOT_ROWS = CAP * BS
PAY_ROWS = SLOT_ROWS + 8
HALF_ROWS = 8 * BS
AXES = ("row", "col")
NX, NY, NZH, NZL, NC = 4, 4, 2, 8, 2


def device_pairs(move):
    pairs = []
    for zh in range(NZH):
        for x in range(NX):
            for y in range(NY):
                for zl in range(NZL):
                    for core in range(NC):
                        to = move(zh, x, y, zl, core)
                        pairs.append((linear(zh, x, y, zl, core), linear(*to)))
    return pairs


def linear(zh, x, y, zl, core):
    return (((zh * NX + x) * NY + y) * NZL + zl) * NC + core


def along_x(n):
    return device_pairs(lambda zh, x, y, zl, core: (zh, (x + n) % NX, y, zl, core))


def along_y(n):
    return device_pairs(lambda zh, x, y, zl, core: (zh, x, (y + n) % NY, zl, core))


def other_half():
    return device_pairs(lambda zh, x, y, zl, core: (1 - zh, x, y, zl, core))


def other_core():
    return device_pairs(lambda zh, x, y, zl, core: (zh, x, y, zl, 1 - core))


def send(value, pairs):
    return lax.ppermute(value, AXES, pairs)


def near(block, along):
    return send(block, along(1)), send(block, along(-1)), send(block, along(2))


def gather_far(group, along):
    half = group.shape[0] // 2
    below = send(group, along(1))
    above = send(group, along(-1))
    return below, above, send(below[:half], along(1)), send(above[half:], along(-1))


def pack_left(blocks, occupied, row_sizes, k_sizes, out):
    first_k = lax.axis_index("col") * 2
    line = lax.broadcasted_iota(jnp.int32, (BS, BS), 0)
    lane = lax.broadcasted_iota(jnp.int32, (BS, BS), 1)
    slot = jnp.int32(0)
    for i in range(4):
        for k in range(2):
            here = (occupied[i, k] > 0) & (slot < CAP)
            place = slot

            @pl.when(here)
            def _():
                keep = (line < row_sizes[i]) & (lane < k_sizes[first_k + k])
                start = pl.multiple_of(place * BS, BS)
                out[pl.ds(start, BS), :] = jnp.where(keep, blocks[i, k], 0.0)

            where = jnp.where(here, place, -1).astype(jnp.float32)
            out[SLOT_ROWS + 2 * i + k, :] = jnp.full((BS,), where, jnp.float32)
            slot = slot + here.astype(jnp.int32)


def mask_right(blocks, occupied, k_sizes, col_sizes, out):
    used = k_sizes[lax.axis_index("row")]
    line = lax.broadcasted_iota(jnp.int32, (BS, BS), 0)
    lane = lax.broadcasted_iota(jnp.int32, (BS, BS), 1)
    for j in range(4):
        columns = jnp.where(occupied[0, j] > 0, col_sizes[j], 0)
        out[j * BS:(j + 1) * BS, :] = jnp.where((line < used) & (lane < columns), blocks[0, j], 0.0)


def split(value):
    high = value.astype(jnp.bfloat16)
    return high, (value - high.astype(jnp.float32)).astype(jnp.bfloat16)


NEAR = (0, -1, 1, 2)


def prepare_right(pieces, own_family, high_out, low_out):
    row, core = lax.axis_index("row"), lax.axis_index("col") % 2
    x, y = (row // 4) % 4, row % 4
    for step in range(4):
        for t in range(4):
            ref, at = (pieces[step], t) if step < 3 else (pieces[3 + t // 2], t % 2)
            across, along = (NEAR[t], NEAR[step]) if own_family else (NEAR[step], NEAR[t])
            from_x, from_y = (x + across + 4) % 4, (y + along + 4) % 4
            foreign = (from_y // 2 != core).astype(jnp.int32)
            start = pl.multiple_of(foreign * HALF_ROWS + from_x * 2 * BS + from_y % 2 * BS, BS)
            for j in range(4):
                high, low = split(ref[(4 * at + j) * BS:(4 * at + j + 1) * BS, :])
                high_out[pl.ds(start, BS), j * BS:(j + 1) * BS] = high
                low_out[pl.ds(start, BS), j * BS:(j + 1) * BS] = low


def multiply(panel, rights, ready, places, copied, left_high, left_low):
    zh = lax.axis_index("row") // 16
    dot = functools.partial(jnp.dot, preferred_element_type=jnp.float32)
    total = None
    for family in range(2):
        half = zh if family == 0 else 1 - zh
        for x in range(4):
            zl = half * 4 + x
            wide = 2 * BS * (4 * family + x)
            for i in range(4):
                for k in range(2):
                    slot = places[zl, 2 * i + k, 0].astype(jnp.int32)
                    start = pl.multiple_of(zl * PAY_ROWS + jnp.maximum(slot, 0) * BS, 8)
                    block_high, block_low = split(jnp.where(slot >= 0, panel[pl.ds(start, BS), :], 0.0))
                    left_high[i * BS:(i + 1) * BS, wide + k * BS:wide + (k + 1) * BS] = block_high
                    left_low[i * BS:(i + 1) * BS, wide + k * BS:wide + (k + 1) * BS] = block_low
    for family in range(2):
        ready(family)
        high, low = rights[2 * family], rights[2 * family + 1]
        for x in range(4):
            wide = 2 * BS * (4 * family + x)
            right_high, right_low = high[2 * BS * x:2 * BS * (x + 1), :], low[2 * BS * x:2 * BS * (x + 1), :]
            here_high = left_high[:, wide:wide + 2 * BS]
            part = dot(here_high, right_high) + dot(here_high, right_low)
            part = part + dot(left_low[:, wide:wide + 2 * BS], right_high)
            total = part if total is None else total + part
    return total


def copy_places(panel, places, copied):
    copies = [
        pltpu.make_async_copy(panel.at[pl.ds(zl * PAY_ROWS + SLOT_ROWS, 8)], places.at[zl], copied.at[zl])
        for zl in range(NZL)
    ]
    for copy in copies:
        copy.start()
    for copy in copies:
        copy.wait()


def own_half(*refs):
    sources, total, passed_on = refs[:11], refs[11], refs[12:16]
    held, rights, arrived, leaving, scratch = refs[16:27], refs[27:31], refs[31], refs[32], refs[33:]
    copies = [pltpu.make_async_copy(source, to, arrived.at[n]) for n, (source, to) in enumerate(zip(sources, held))]
    for copy in copies:
        copy.start()
    copies[0].wait()
    copy_places(held[0], scratch[0], scratch[1])
    onward = [
        pltpu.make_async_copy(source.at[pl.ds(HALF_ROWS, HALF_ROWS)], to, leaving.at[n])
        for n, (source, to) in enumerate(zip(rights, passed_on))
    ]

    def ready(family):
        pieces = slice(5 * family + 1, 5 * family + 6)
        for copy in copies[pieces]:
            copy.wait()
        prepare_right(held[pieces], family == 0, *rights[2 * family:2 * family + 2])
        for copy in onward[2 * family:2 * family + 2]:
            copy.start()

    total[...] = multiply(held[0], rights, ready, *scratch)
    for copy in onward:
        copy.wait()


def other_half_of(*refs):
    c_filter, panel, before, sources, out = refs[0], refs[1], refs[2], refs[3:7], refs[7]
    rights, arrived, scratch = refs[8:12], refs[12], refs[13:]
    copies = [pltpu.make_async_copy(source, to, arrived.at[n]) for n, (source, to) in enumerate(zip(sources, rights))]
    for copy in copies:
        copy.start()
    copy_places(panel, scratch[0], scratch[1])

    def ready(family):
        for copy in copies[2 * family:2 * family + 2]:
            copy.wait()

    total = before[...] + multiply(panel, rights, ready, *scratch)
    for i in range(4):
        for j in range(4):
            value = total[i * BS:(i + 1) * BS, j * BS:(j + 1) * BS]
            out[i, j] = jnp.where(c_filter[i, j] > 0, value, 0.0)


VMEM = pl.BlockSpec(memory_space=pltpu.VMEM)
SMEM = pl.BlockSpec(memory_space=pltpu.SMEM)
ANY = pl.BlockSpec(memory_space=pl.ANY)


def on_device(a_blocks, b_blocks, a_occupied, b_occupied, c_filter, row_sizes, k_sizes, col_sizes):
    right = pl.pallas_call(
        mask_right,
        out_shape=jax.ShapeDtypeStruct((4 * BS, BS), jnp.float32),
        in_specs=[VMEM, SMEM, SMEM, SMEM],
        out_specs=VMEM,
    )(b_blocks, b_occupied, k_sizes, col_sizes)
    partner = send(right, other_half())
    left = pl.pallas_call(
        pack_left,
        out_shape=jax.ShapeDtypeStruct((PAY_ROWS, BS), jnp.float32),
        in_specs=[VMEM, SMEM, SMEM, SMEM],
        out_specs=VMEM,
    )(a_blocks, a_occupied, row_sizes, k_sizes)
    same_core = [[zl * NC + core for zl in range(NZL)] for core in range(NC)]
    own = lax.all_gather(left, "col", axis_index_groups=same_core, tiled=True)
    first = [right, *near(right, along_x)]
    second = [partner, *near(partner, along_y)]
    parts = lax.optimization_barrier((*first, *second))
    first, second = jnp.concatenate(parts[:4]), jnp.concatenate(parts[4:])
    rights = (first, *gather_far(first, along_y), second, *gather_far(second, along_x))
    own, *rights = lax.optimization_barrier((own, *rights))
    other = send(own, other_core())
    scratch = [
        pltpu.SMEM((NZL, 8, BS), jnp.float32),
        pltpu.SemaphoreType.DMA((NZL,)),
        pltpu.VMEM((4 * BS, 16 * BS), jnp.bfloat16),
        pltpu.VMEM((4 * BS, 16 * BS), jnp.bfloat16),
    ]
    cost = pl.CostEstimate(flops=6 * 512 * 512 * 2048, bytes_accessed=8 << 20, transcendentals=0)
    part, *prepared = pl.pallas_call(
        own_half,
        out_shape=[jax.ShapeDtypeStruct((4 * BS, 4 * BS), jnp.float32)]
        + [jax.ShapeDtypeStruct((HALF_ROWS, 4 * BS), jnp.bfloat16)] * 4,
        in_specs=[ANY] * 11,
        out_specs=[VMEM] + [ANY] * 4,
        scratch_shapes=[pltpu.VMEM(source.shape, jnp.float32) for source in (own, *rights)]
        + [pltpu.VMEM((2 * HALF_ROWS, 4 * BS), jnp.bfloat16)] * 4
        + [pltpu.SemaphoreType.DMA((11,)), pltpu.SemaphoreType.DMA((4,))]
        + scratch,
        compiler_params=pltpu.CompilerParams(vmem_limit_bytes=46 << 20),
        cost_estimate=cost,
    )(own, *rights)
    return pl.pallas_call(
        other_half_of,
        out_shape=jax.ShapeDtypeStruct((4, 4, BS, BS), jnp.float32),
        in_specs=[SMEM] + [VMEM] * 2 + [ANY] * 4,
        out_specs=VMEM,
        scratch_shapes=[pltpu.VMEM((HALF_ROWS, 4 * BS), jnp.bfloat16)] * 4 + [pltpu.SemaphoreType.DMA((4,))] + scratch,
        compiler_params=pltpu.CompilerParams(vmem_limit_bytes=24 << 20),
        cost_estimate=cost,
    )(c_filter, other, part, *prepared)


def solution(mesh):
    placed = (
        P("row", "col", None, None),
        P("row", "col", None, None),
        P("row", "col"),
        P("row", "col"),
        P("row", "col"),
        P("row"),
        P(),
        P("col"),
    )
    return jax.shard_map(
        on_device,
        mesh=mesh,
        in_specs=placed,
        out_specs=P("row", "col", None, None),
        check_vma=False,
    )
```

time: 413 us -> 154 us (0.37)
  the two profiles are of different devices: /device:TPU:100 before, /device:TPU:199 now
where the time goes in v1:
time: 154 us; the launch traced here: 153 us
  starting transfers between devices  61.3 us (40%)
  waiting for transfers between devices  54.2 us (35%)
  Pallas kernels  20.5 us (13%)
  between operations  13.8 us (9%)
  local copies, waits for them, and re-layouts  3.57 us (2%)
    ppermute x16, starting transfers between devices, send(): return lax.ppermute(value, AXES, pairs)  61.3 us
    ppermute x16, waiting for transfers between devices, send(): return lax.ppermute(value, AXES, pairs)  54.2 us
    pallas_call x1, Pallas kernels, on_device(): pl.pallas_call(own_half, out_shape=[jax.ShapeDtypeStruct((4 * BS, 4 * BS)...  9.32 us
    pallas_call x1, Pallas kernels, on_device(): pl.pallas_call(other_half_of, out_shape=jax.ShapeDtypeStruct((4, 4, BS, B...  7.52 us
    unnamed x21, local copies, waits for them, and re-layouts  3.39 us
  transfers between devices with their start and end apart: 17, of which 8 were waited for; matrix products, arithmetic and copies ran while one was open for 1% of the time, Pallas kernels for 7%

profile of v1, /device:TPU:199, one launch (start us, length us, event | category | flops | bytes accessed | tf_op | source)
XLA Modules:
  0.0 153.3 jit_solution(7552121325771015448)
XLA Ops:
  6.5 0.0 all-gather.2.cloned.1.call-start
  6.5 1.3 copy.9.occupied
  7.9 2.0 %shard_map.82 = f32[776,128]{1,0:T(8,128)} custom-call(f32[4,2,128,128]{3,2,1,0:T(8,128)} %blocks.2, s32[4,2]{1,0:T(4,128)} %copy.9.occupied, s32[4]{0:T(128)} %row_sizes.1, s32[32]{0:T(128)} %k_sizes.3), custom_call_target="tpu_custom_call" | custom-call | tf_op jit(solution)/shard_map/pallas_call | solution.py:218
  9.8 0.0 all-gather.2.cloned.1.call-update
  9.9 1.7 %shard_map.83 = f32[512,128]{1,0:T(8,128)} custom-call(f32[1,4,128,128]{3,2,1,0:T(8,128)} %blocks.3, s32[1,4]{1,0:T(1,128)} %occupied.2, s32[32]{0:T(128)} %k_sizes.3, s32[4]{0:T(128)} %col_sizes.1), custom_call_target="tpu_custom_call" | custom-call | tf_op jit(solution)/shard_map/pallas_call | solution.py:211
  11.6 8.8 %collective-permute-start.3 = (f32[512,128]{1,0:T(8,128)}, f32[512,128]{1,0:T(8,128)S(1)}, u32[]{:S(2)}, u32[]{:S(2)}) collective-permute-start(f32[512,128]{1,0:T(8,128)} %shard_map.83), channel_id=1, source_target_pairs={{0,256},{1,257},{2,258},{3,259},{4,260},{5,261},{6,262},{7,263},{8... | collective-permute-start | bytes 786440 | tf_op jit(solution)/shard_map/ppermute | solution.py:52
  20.4 3.1 %collective-permute-start.2 = (f32[512,128]{1,0:T(8,128)}, f32[512,128]{1,0:T(8,128)S(1)}, u32[]{:S(2)}, u32[]{:S(2)}) collective-permute-start(f32[512,128]{1,0:T(8,128)} %shard_map.83), channel_id=1, source_target_pairs={{0,128},{1,129},{2,130},{3,131},{4,132},{5,133},{6,134},{7,135},{8... | collective-permute-start | bytes 786440 | tf_op jit(solution)/shard_map/ppermute | solution.py:52
  23.5 1.9 %collective-permute-start.1 = (f32[512,128]{1,0:T(8,128)}, f32[512,128]{1,0:T(8,128)S(1)}, u32[]{:S(2)}, u32[]{:S(2)}) collective-permute-start(f32[512,128]{1,0:T(8,128)} %shard_map.83), channel_id=1, source_target_pairs={{0,192},{1,193},{2,194},{3,195},{4,196},{5,197},{6,198},{7,199},{8... | collective-permute-start | bytes 786440 | tf_op jit(solution)/shard_map/ppermute | solution.py:52
  25.4 4.6 %collective-permute-start = (f32[512,128]{1,0:T(8,128)}, f32[512,128]{1,0:T(8,128)S(1)}, u32[]{:S(2)}, u32[]{:S(2)}) collective-permute-start(f32[512,128]{1,0:T(8,128)} %shard_map.83), channel_id=1, source_target_pairs={{0,64},{1,65},{2,66},{3,67},{4,68},{5,69},{6,70},{7,71},{8,72},{9,... | collective-permute-start | bytes 786440 | tf_op jit(solution)/shard_map/ppermute | solution.py:52
  30.0 23.0 %collective-permute-done.3 = f32[512,128]{1,0:T(8,128)S(1)} collective-permute-done((f32[512,128]{1,0:T(8,128)}, f32[512,128]{1,0:T(8,128)S(1)}, u32[]{:S(2)}, u32[]{:S(2)}) %collective-permute-start.3) | collective-permute-done | bytes 262176 | tf_op jit(solution)/shard_map/ppermute | solution.py:52
  52.9 4.8 %collective-permute-start.6 = (f32[512,128]{1,0:T(8,128)S(1)}, f32[512,128]{1,0:T(8,128)S(1)}, u32[]{:S(2)}, u32[]{:S(2)}) collective-permute-start(f32[512,128]{1,0:T(8,128)S(1)} %collective-permute-done.3), channel_id=1, source_target_pairs={{0,32},{1,33},{2,34},{3,35},{4,36},{5,37},{6,38},{7,39},{8,40},{9,... | collective-permute-start | bytes 786440 | tf_op jit(solution)/shard_map/ppermute | solution.py:52
  57.8 2.7 %collective-permute-start.5 = (f32[512,128]{1,0:T(8,128)S(1)}, f32[512,128]{1,0:T(8,128)S(1)}, u32[]{:S(2)}, u32[]{:S(2)}) collective-permute-start(f32[512,128]{1,0:T(8,128)S(1)} %collective-permute-done.3), channel_id=1, source_target_pairs={{0,48},{1,49},{2,50},{3,51},{4,52},{5,53},{6,54},{7,55},{8,56},{9,... | collective-permute-start | bytes 786440 | tf_op jit(solution)/shard_map/ppermute | solution.py:52
  60.4 0.0 collective-permute-done.2
  60.4 2.6 %collective-permute-start.4 = (f32[512,128]{1,0:T(8,128)S(1)}, f32[512,128]{1,0:T(8,128)S(1)}, u32[]{:S(2)}, u32[]{:S(2)}) collective-permute-start(f32[512,128]{1,0:T(8,128)S(1)} %collective-permute-done.3), channel_id=1, source_target_pairs={{0,16},{1,17},{2,18},{3,19},{4,20},{5,21},{6,22},{7,23},{8,24},{9,... | collective-permute-start | bytes 786440 | tf_op jit(solution)/shard_map/ppermute | solution.py:52
  63.1 0.0 collective-permute-done.1
  63.1 0.0 collective-permute-done
  63.1 0.3 collective-permute-done.6
  63.4 6.2 %collective-permute-done.5 = f32[512,128]{1,0:T(8,128)S(1)} collective-permute-done((f32[512,128]{1,0:T(8,128)S(1)}, f32[512,128]{1,0:T(8,128)S(1)}, u32[]{:S(2)}, u32[]{:S(2)}) %collective-permute-start.5) | collective-permute-done | bytes 262176 | tf_op jit(solution)/shard_map/ppermute | solution.py:52
  69.6 0.4 collective-permute-done.4
  70.1 0.0 copy-start.5
  70.1 2.5 %collective-permute-start.12 = (f32[2048,128]{1,0:T(8,128)S(1)}, f32[2048,128]{1,0:T(8,128)S(1)}, u32[]{:S(2)}, u32[]{:S(2)}) collective-permute-start(f32[2048,128]{1,0:T(8,128)S(1)} %constant_dynamic-update-slice_fusion.4.refs_6_), channel_id=1, source_target_pairs={{0,192},{1,193},{2,194},{3,195},{4,196},{5,197},{6,198},{7,199},{8... | collective-permute-start | bytes 3145736 | tf_op jit(solution)/shard_map/ppermute | solution.py:52
  72.6 4.0 %collective-permute-start.11 = (f32[2048,128]{1,0:T(8,128)S(1)}, f32[2048,128]{1,0:T(8,128)S(1)}, u32[]{:S(2)}, u32[]{:S(2)}) collective-permute-start(f32[2048,128]{1,0:T(8,128)S(1)} %constant_dynamic-update-slice_fusion.4.refs_6_), channel_id=1, source_target_pairs={{0,64},{1,65},{2,66},{3,67},{4,68},{5,69},{6,70},{7,71},{8,72},{9,... | collective-permute-start | bytes 3145736 | tf_op jit(solution)/shard_map/ppermute | solution.py:52
  76.6 1.0 constant_dynamic-update-slice_fusion.3
  77.7 0.0 copy-start.6
  77.7 4.9 %collective-permute-start.8 = (f32[2048,128]{1,0:T(8,128)S(1)}, f32[2048,128]{1,0:T(8,128)S(1)}, u32[]{:S(2)}, u32[]{:S(2)}) collective-permute-start(f32[2048,128]{1,0:T(8,128)S(1)} %constant_dynamic-update-slice_fusion.refs_1_), channel_id=1, source_target_pairs={{0,48},{1,49},{2,50},{3,51},{4,52},{5,53},{6,54},{7,55},{8,56},{9,... | collective-permute-start | bytes 3145736 | tf_op jit(solution)/shard_map/ppermute | solution.py:52
  82.6 1.9 %collective-permute-start.7 = (f32[2048,128]{1,0:T(8,128)S(1)}, f32[2048,128]{1,0:T(8,128)S(1)}, u32[]{:S(2)}, u32[]{:S(2)}) collective-permute-start(f32[2048,128]{1,0:T(8,128)S(1)} %constant_dynamic-update-slice_fusion.refs_1_), channel_id=1, source_target_pairs={{0,16},{1,17},{2,18},{3,19},{4,20},{5,21},{6,22},{7,23},{8,24},{9,... | collective-permute-start | bytes 3145736 | tf_op jit(solution)/shard_map/ppermute | solution.py:52
  84.5 11.1 %collective-permute-done.12.refs_8_ = f32[2048,128]{1,0:T(8,128)S(1)} collective-permute-done((f32[2048,128]{1,0:T(8,128)S(1)}, f32[2048,128]{1,0:T(8,128)S(1)}, u32[]{:S(2)}, u32[]{:S(2)}) %collective-permute-start.12) | collective-permute-done | bytes 1048608 | tf_op jit(solution)/shard_map/ppermute | solution.py:52
  95.6 1.9 %collective-permute-start.14 = (f32[1024,128]{1,0:T(8,128)S(1)}, f32[1024,128]{1,0:T(8,128)S(1)}, u32[]{:S(2)}, u32[]{:S(2)}) collective-permute-start(f32[1024,128]{1,0:T(8,128)S(1)} %slice.19), channel_id=1, source_target_pairs={{0,192},{1,193},{2,194},{3,195},{4,196},{5,197},{6,198},{7,199},{8... | collective-permute-start | bytes 1572872 | tf_op jit(solution)/shard_map/ppermute | solution.py:52
  97.5 0.0 copy-done.5
  97.6 0.0 collective-permute-done.11.refs_7_
  97.6 0.0 copy-start.2
  97.6 1.0 copy-done.2
  98.6 4.6 %collective-permute-start.13 = (f32[1024,128]{1,0:T(8,128)S(1)}, f32[1024,128]{1,0:T(8,128)S(1)}, u32[]{:S(2)}, u32[]{:S(2)}) collective-permute-start(f32[1024,128]{1,0:T(8,128)S(1)} %slice.18), channel_id=1, source_target_pairs={{0,64},{1,65},{2,66},{3,67},{4,68},{5,69},{6,70},{7,71},{8,72},{9,... | collective-permute-start | bytes 1572872 | tf_op jit(solution)/shard_map/ppermute | solution.py:52
  103.1 0.8 collective-permute-done.8.refs_3_
  104.0 6.0 %collective-permute-start.10 = (f32[1024,128]{1,0:T(8,128)S(1)}, f32[1024,128]{1,0:T(8,128)S(1)}, u32[]{:S(2)}, u32[]{:S(2)}) collective-permute-start(f32[1024,128]{1,0:T(8,128)S(1)} %slice.17), channel_id=1, source_target_pairs={{0,48},{1,49},{2,50},{3,51},{4,52},{5,53},{6,54},{7,55},{8,56},{9,... | collective-permute-start | bytes 1572872 | tf_op jit(solution)/shard_map/ppermute | solution.py:52
  110.0 0.0 collective-permute-done.7.refs_2_
  110.0 0.0 copy-start.4
  110.1 0.0 copy-start
  110.1 2.1 %collective-permute-start.9 = (f32[1024,128]{1,0:T(8,128)S(1)}, f32[1024,128]{1,0:T(8,128)S(1)}, u32[]{:S(2)}, u32[]{:S(2)}) collective-permute-start(f32[1024,128]{1,0:T(8,128)S(1)} %slice.16), channel_id=1, source_target_pairs={{0,16},{1,17},{2,18},{3,19},{4,20},{5,21},{6,22},{7,23},{8,24},{9,... | collective-permute-start | bytes 1572872 | tf_op jit(solution)/shard_map/ppermute | solution.py:52
  112.1 0.0 collective-permute-done.14.refs_10_
  112.1 0.0 collective-permute-done.13.refs_9_
  112.2 7.1 %collective-permute-done.10.refs_5_ = f32[1024,128]{1,0:T(8,128)S(1)} collective-permute-done((f32[1024,128]{1,0:T(8,128)S(1)}, f32[1024,128]{1,0:T(8,128)S(1)}, u32[]{:S(2)}, u32[]{:S(2)}) %collective-permute-start.10) | collective-permute-done | bytes 524320 | tf_op jit(solution)/shard_map/ppermute | solution.py:52
  119.3 0.0 copy-done.6
  119.3 5.3 %collective-permute-done.9.refs_4_ = f32[1024,128]{1,0:T(8,128)S(1)} collective-permute-done((f32[1024,128]{1,0:T(8,128)S(1)}, f32[1024,128]{1,0:T(8,128)S(1)}, u32[]{:S(2)}, u32[]{:S(2)}) %collective-permute-start.9) | collective-permute-done | bytes 524320 | tf_op jit(solution)/shard_map/ppermute | solution.py:52
  124.6 5.0 %collective-permute-start.15 = (f32[6208,128]{1,0:T(8,128)}, f32[6208,128]{1,0:T(8,128)S(1)}, u32[]{:S(2)}, u32[]{:S(2)}) collective-permute-start(f32[6208,128]{1,0:T(8,128)} %all-gather.2.cloned.1.call-done.refs_0_), channel_id=1, source_target_pairs={{0,1},{1,0},{2,3},{3,2},{4,5},{5,4},{6,7},{7,6},{8,9},{9,8},{10,11... | collective-permute-start | bytes 9535496 | tf_op jit(solution)/shard_map/ppermute | solution.py:52
  129.6 9.3 %shard_map.84 = (f32[512,512]{1,0:T(8,128)S(1)}, bf16[1024,512]{1,0:T(8,128)(2,1)S(1)}, bf16[1024,512]{1,0:T(8,128)(2,1)S(1)}, bf16[1024,512]{1,0:T(8,128)(2,1)S(1)}, bf16[1024,512]{1,0:T(8,128)(2,1)S(1)}) custom-call(f32[6208,128]{1,0:T(8,128)} %all-gather.2.cloned.1.call-done.refs_0_, f32[2048,128]{1,0:T(8,128)} %copy-done.6, f32[2048,128]{1,0:T(8,128)} %copy-done.4, ...), custom_call_target="tpu_custom_call" | custom-call | flops 3221225472 | bytes 8388608 | tf_op jit(solution)/shard_map/pallas_call | solution.py:240
  138.9 0.0 collective-permute-done.15.refs_1_
  138.9 7.5 %shard_map.85 = f32[4,4,128,128]{3,2,1,0:T(8,128)} custom-call(s32[4,4]{1,0:T(4,128)S(1)} %copy-done, f32[6208,128]{1,0:T(8,128)S(1)} %collective-permute-done.15.refs_1_, f32[512,512]{1,0:T(8,128)S(1)} %get-tuple-element.48.refs_2_, bf16[1024,512]{1,0:T(8,128)(2,1)S(1)} %get-tuple-element.49.refs_3_, bf16[1024,512]{1,0:T(8,128)(2,1)S(1)} %get-tuple-element.50.refs_4_, ...), custom_call_target="tpu_custom_call" | custom-call | flops 3221225472 | bytes 8388608 | tf_op jit(solution)/shard_map/pallas_call | solution.py:253
  (18 shorter events, 0.3 us)
Async XLA Ops:
  6.5 118.0 %all-gather.2.cloned.1.call-start = ((), (), s32[]{:S(2)}) async-start(), calls=%async_computation | async-start | bytes 3575808 | tf_op jit(solution)/shard_map/all_gather | solution.py:225
  11.6 41.4 %collective-permute-start.3 = (f32[512,128]{1,0:T(8,128)}, f32[512,128]{1,0:T(8,128)S(1)}, u32[]{:S(2)}, u32[]{:S(2)}) collective-permute-start(f32[512,128]{1,0:T(8,128)} %shard_map.83), channel_id=1, source_target_pairs={{0,256},{1,257},{2,258},{3,259},{4,260},{5,261},{6,262},{7,263},{8... | collective-permute-start | bytes 786440 | tf_op jit(solution)/shard_map/ppermute | solution.py:52
  20.4 40.0 %collective-permute-start.2 = (f32[512,128]{1,0:T(8,128)}, f32[512,128]{1,0:T(8,128)S(1)}, u32[]{:S(2)}, u32[]{:S(2)}) collective-permute-start(f32[512,128]{1,0:T(8,128)} %shard_map.83), channel_id=1, source_target_pairs={{0,128},{1,129},{2,130},{3,131},{4,132},{5,133},{6,134},{7,135},{8... | collective-permute-start | bytes 786440 | tf_op jit(solution)/shard_map/ppermute | solution.py:52
  23.5 39.6 %collective-permute-start.1 = (f32[512,128]{1,0:T(8,128)}, f32[512,128]{1,0:T(8,128)S(1)}, u32[]{:S(2)}, u32[]{:S(2)}) collective-permute-start(f32[512,128]{1,0:T(8,128)} %shard_map.83), channel_id=1, source_target_pairs={{0,192},{1,193},{2,194},{3,195},{4,196},{5,197},{6,198},{7,199},{8... | collective-permute-start | bytes 786440 | tf_op jit(solution)/shard_map/ppermute | solution.py:52
  25.4 37.7 %collective-permute-start = (f32[512,128]{1,0:T(8,128)}, f32[512,128]{1,0:T(8,128)S(1)}, u32[]{:S(2)}, u32[]{:S(2)}) collective-permute-start(f32[512,128]{1,0:T(8,128)} %shard_map.83), channel_id=1, source_target_pairs={{0,64},{1,65},{2,66},{3,67},{4,68},{5,69},{6,70},{7,71},{8,72},{9,... | collective-permute-start | bytes 786440 | tf_op jit(solution)/shard_map/ppermute | solution.py:52
  52.9 10.5 %collective-permute-start.6 = (f32[512,128]{1,0:T(8,128)S(1)}, f32[512,128]{1,0:T(8,128)S(1)}, u32[]{:S(2)}, u32[]{:S(2)}) collective-permute-start(f32[512,128]{1,0:T(8,128)S(1)} %collective-permute-done.3), channel_id=1, source_target_pairs={{0,32},{1,33},{2,34},{3,35},{4,36},{5,37},{6,38},{7,39},{8,40},{9,... | collective-permute-start | bytes 786440 | tf_op jit(solution)/shard_map/ppermute | solution.py:52
  57.8 11.8 %collective-permute-start.5 = (f32[512,128]{1,0:T(8,128)S(1)}, f32[512,128]{1,0:T(8,128)S(1)}, u32[]{:S(2)}, u32[]{:S(2)}) collective-permute-start(f32[512,128]{1,0:T(8,128)S(1)} %collective-permute-done.3), channel_id=1, source_target_pairs={{0,48},{1,49},{2,50},{3,51},{4,52},{5,53},{6,54},{7,55},{8,56},{9,... | collective-permute-start | bytes 786440 | tf_op jit(solution)/shard_map/ppermute | solution.py:52
  60.4 9.5 %collective-permute-start.4 = (f32[512,128]{1,0:T(8,128)S(1)}, f32[512,128]{1,0:T(8,128)S(1)}, u32[]{:S(2)}, u32[]{:S(2)}) collective-permute-start(f32[512,128]{1,0:T(8,128)S(1)} %collective-permute-done.3), channel_id=1, source_target_pairs={{0,16},{1,17},{2,18},{3,19},{4,20},{5,21},{6,22},{7,23},{8,24},{9,... | collective-permute-start | bytes 786440 | tf_op jit(solution)/shard_map/ppermute | solution.py:52
  70.1 27.5 %copy-start.5 = (f32[2048,128]{1,0:T(8,128)}, f32[2048,128]{1,0:T(8,128)S(1)}, u32[]{:S(2)}) copy-start(f32[2048,128]{1,0:T(8,128)S(1)} %constant_dynamic-update-slice_fusion.4.refs_6_) | copy-start | bytes 3145732
  70.1 25.5 %collective-permute-start.12 = (f32[2048,128]{1,0:T(8,128)S(1)}, f32[2048,128]{1,0:T(8,128)S(1)}, u32[]{:S(2)}, u32[]{:S(2)}) collective-permute-start(f32[2048,128]{1,0:T(8,128)S(1)} %constant_dynamic-update-slice_fusion.4.refs_6_), channel_id=1, source_target_pairs={{0,192},{1,193},{2,194},{3,195},{4,196},{5,197},{6,198},{7,199},{8... | collective-permute-start | bytes 3145736 | tf_op jit(solution)/shard_map/ppermute | solution.py:52
  72.6 25.0 %collective-permute-start.11 = (f32[2048,128]{1,0:T(8,128)S(1)}, f32[2048,128]{1,0:T(8,128)S(1)}, u32[]{:S(2)}, u32[]{:S(2)}) collective-permute-start(f32[2048,128]{1,0:T(8,128)S(1)} %constant_dynamic-update-slice_fusion.4.refs_6_), channel_id=1, source_target_pairs={{0,64},{1,65},{2,66},{3,67},{4,68},{5,69},{6,70},{7,71},{8,72},{9,... | collective-permute-start | bytes 3145736 | tf_op jit(solution)/shard_map/ppermute | solution.py:52
  77.7 41.6 %copy-start.6 = (f32[2048,128]{1,0:T(8,128)}, f32[2048,128]{1,0:T(8,128)S(1)}, u32[]{:S(2)}) copy-start(f32[2048,128]{1,0:T(8,128)S(1)} %constant_dynamic-update-slice_fusion.refs_1_) | copy-start | bytes 3145732
  77.7 26.3 %collective-permute-start.8 = (f32[2048,128]{1,0:T(8,128)S(1)}, f32[2048,128]{1,0:T(8,128)S(1)}, u32[]{:S(2)}, u32[]{:S(2)}) collective-permute-start(f32[2048,128]{1,0:T(8,128)S(1)} %constant_dynamic-update-slice_fusion.refs_1_), channel_id=1, source_target_pairs={{0,48},{1,49},{2,50},{3,51},{4,52},{5,53},{6,54},{7,55},{8,56},{9,... | collective-permute-start | bytes 3145736 | tf_op jit(solution)/shard_map/ppermute | solution.py:52
  82.6 27.4 %collective-permute-start.7 = (f32[2048,128]{1,0:T(8,128)S(1)}, f32[2048,128]{1,0:T(8,128)S(1)}, u32[]{:S(2)}, u32[]{:S(2)}) collective-permute-start(f32[2048,128]{1,0:T(8,128)S(1)} %constant_dynamic-update-slice_fusion.refs_1_), channel_id=1, source_target_pairs={{0,16},{1,17},{2,18},{3,19},{4,20},{5,21},{6,22},{7,23},{8,24},{9,... | collective-permute-start | bytes 3145736 | tf_op jit(solution)/shard_map/ppermute | solution.py:52
  95.6 34.0 %copy-start.1 = (f32[2048,128]{1,0:T(8,128)}, f32[2048,128]{1,0:T(8,128)S(1)}, u32[]{:S(2)}) copy-start(f32[2048,128]{1,0:T(8,128)S(1)} %collective-permute-done.12.refs_8_) | copy-start | bytes 3145732
  95.6 16.5 %collective-permute-start.14 = (f32[1024,128]{1,0:T(8,128)S(1)}, f32[1024,128]{1,0:T(8,128)S(1)}, u32[]{:S(2)}, u32[]{:S(2)}) collective-permute-start(f32[1024,128]{1,0:T(8,128)S(1)} %slice.19), channel_id=1, source_target_pairs={{0,192},{1,193},{2,194},{3,195},{4,196},{5,197},{6,198},{7,199},{8... | collective-permute-start | bytes 1572872 | tf_op jit(solution)/shard_map/ppermute | solution.py:52
  97.6 1.0 copy-start.2
  98.6 13.6 %collective-permute-start.13 = (f32[1024,128]{1,0:T(8,128)S(1)}, f32[1024,128]{1,0:T(8,128)S(1)}, u32[]{:S(2)}, u32[]{:S(2)}) collective-permute-start(f32[1024,128]{1,0:T(8,128)S(1)} %slice.18), channel_id=1, source_target_pairs={{0,64},{1,65},{2,66},{3,67},{4,68},{5,69},{6,70},{7,71},{8,72},{9,... | collective-permute-start | bytes 1572872 | tf_op jit(solution)/shard_map/ppermute | solution.py:52
  104.0 6.0 %copy-start.3 = (f32[2048,128]{1,0:T(8,128)}, f32[2048,128]{1,0:T(8,128)S(1)}, u32[]{:S(2)}) copy-start(f32[2048,128]{1,0:T(8,128)S(1)} %collective-permute-done.8.refs_3_) | copy-start | bytes 3145732
  104.0 15.3 %collective-permute-start.10 = (f32[1024,128]{1,0:T(8,128)S(1)}, f32[1024,128]{1,0:T(8,128)S(1)}, u32[]{:S(2)}, u32[]{:S(2)}) collective-permute-start(f32[1024,128]{1,0:T(8,128)S(1)} %slice.17), channel_id=1, source_target_pairs={{0,48},{1,49},{2,50},{3,51},{4,52},{5,53},{6,54},{7,55},{8,56},{9,... | collective-permute-start | bytes 1572872 | tf_op jit(solution)/shard_map/ppermute | solution.py:52
  110.0 9.3 %copy-start.4 = (f32[2048,128]{1,0:T(8,128)}, f32[2048,128]{1,0:T(8,128)S(1)}, u32[]{:S(2)}) copy-start(f32[2048,128]{1,0:T(8,128)S(1)} %collective-permute-done.7.refs_2_) | copy-start | bytes 3145732
  110.1 28.8 %copy-start = (s32[4,4]{1,0:T(4,128)S(1)}, s32[4,4]{1,0:T(4,128)}, u32[]{:S(2)}) copy-start(s32[4,4]{1,0:T(4,128)} %refs_0_.1) | copy-start | bytes 196
  110.1 14.5 %collective-permute-start.9 = (f32[1024,128]{1,0:T(8,128)S(1)}, f32[1024,128]{1,0:T(8,128)S(1)}, u32[]{:S(2)}, u32[]{:S(2)}) collective-permute-start(f32[1024,128]{1,0:T(8,128)S(1)} %slice.16), channel_id=1, source_target_pairs={{0,16},{1,17},{2,18},{3,19},{4,20},{5,21},{6,22},{7,23},{8,24},{9,... | collective-permute-start | bytes 1572872 | tf_op jit(solution)/shard_map/ppermute | solution.py:52
  124.6 14.3 %collective-permute-start.15 = (f32[6208,128]{1,0:T(8,128)}, f32[6208,128]{1,0:T(8,128)S(1)}, u32[]{:S(2)}, u32[]{:S(2)}) collective-permute-start(f32[6208,128]{1,0:T(8,128)} %all-gather.2.cloned.1.call-done.refs_0_), channel_id=1, source_target_pairs={{0,1},{1,0},{2,3},{3,2},{4,5},{5,4},{6,7},{7,6},{8,9},{9,8},{10,11... | collective-permute-start | bytes 9535496 | tf_op jit(solution)/shard_map/ppermute | solution.py:52
Sparse Core Ops, SparseCore 0:
  10.0 92.4 all-gather.1

commit v2 on v1

v2 whole, which is shorter than its diff:
```python
import functools

import jax
import jax.numpy as jnp
from jax import lax
from jax.experimental import pallas as pl
from jax.experimental.pallas import tpu as pltpu
from jax.sharding import PartitionSpec as P

BS = 128
CAP = 6
SLOT_ROWS = CAP * BS
PAY_ROWS = SLOT_ROWS + 8
HALF_ROWS = 8 * BS
AXES = ("row", "col")
NX, NY, NZH, NZL, NC = 4, 4, 2, 8, 2


def device_pairs(move):
    pairs = []
    for zh in range(NZH):
        for x in range(NX):
            for y in range(NY):
                for zl in range(NZL):
                    for core in range(NC):
                        to = move(zh, x, y, zl, core)
                        pairs.append((linear(zh, x, y, zl, core), linear(*to)))
    return pairs


def linear(zh, x, y, zl, core):
    return (((zh * NX + x) * NY + y) * NZL + zl) * NC + core


def along_x(n):
    return device_pairs(lambda zh, x, y, zl, core: (zh, (x + n) % NX, y, zl, core))


def along_y(n):
    return device_pairs(lambda zh, x, y, zl, core: (zh, x, (y + n) % NY, zl, core))


def other_half():
    return device_pairs(lambda zh, x, y, zl, core: (1 - zh, x, y, zl, core))


def other_core():
    return device_pairs(lambda zh, x, y, zl, core: (zh, x, y, zl, 1 - core))


def send(value, pairs):
    return lax.ppermute(value, AXES, pairs)


def near(block, along):
    return send(block, along(1)), send(block, along(-1)), send(block, along(2))


def gather_far(group, along):
    half = group.shape[0] // 2
    below = send(group, along(1))
    above = send(group, along(-1))
    return below, above, send(below[:half], along(1)), send(above[half:], along(-1))


def pack_left(blocks, occupied, row_sizes, k_sizes, out):
    first_k = lax.axis_index("col") * 2
    line = lax.broadcasted_iota(jnp.int32, (BS, BS), 0)
    lane = lax.broadcasted_iota(jnp.int32, (BS, BS), 1)
    slot = jnp.int32(0)
    for i in range(4):
        for k in range(2):
            here = (occupied[i, k] > 0) & (slot < CAP)
            place = slot

            @pl.when(here)
            def _():
                keep = (line < row_sizes[i]) & (lane < k_sizes[first_k + k])
                start = pl.multiple_of(place * BS, BS)
                out[pl.ds(start, BS), :] = jnp.where(keep, blocks[i, k], 0.0)

            where = jnp.where(here, place, -1).astype(jnp.float32)
            out[SLOT_ROWS + 2 * i + k, :] = jnp.full((BS,), where, jnp.float32)
            slot = slot + here.astype(jnp.int32)


def mask_right(blocks, occupied, k_sizes, col_sizes, out):
    used = k_sizes[lax.axis_index("row")]
    line = lax.broadcasted_iota(jnp.int32, (BS, BS), 0)
    lane = lax.broadcasted_iota(jnp.int32, (BS, BS), 1)
    for j in range(4):
        columns = jnp.where(occupied[0, j] > 0, col_sizes[j], 0)
        out[j * BS:(j + 1) * BS, :] = jnp.where((line < used) & (lane < columns), blocks[0, j], 0.0)


def split(value):
    high = value.astype(jnp.bfloat16)
    return high, (value - high.astype(jnp.float32)).astype(jnp.bfloat16)


NEAR = (0, -1, 1, 2)


def prepare_right(own_family, *refs):
    pieces, outs = refs[:5], refs[5:]
    row, core = lax.axis_index("row"), lax.axis_index("col") % 2
    x, y = (row // 4) % 4, row % 4
    for step in range(4):
        for t in range(4):
            ref, at = (pieces[step], t) if step < 3 else (pieces[3 + t // 2], t % 2)
            across, along = (NEAR[t], NEAR[step]) if own_family else (NEAR[step], NEAR[t])
            from_x, from_y = (x + across + 4) % 4, (y + along + 4) % 4
            foreign = from_y // 2 != core
            start = pl.multiple_of(from_x * 2 * BS + from_y % 2 * BS, BS)
            for other in range(2):

                @pl.when(foreign if other else jnp.logical_not(foreign))
                def _():
                    for j in range(4):
                        high, low = split(ref[(4 * at + j) * BS:(4 * at + j + 1) * BS, :])
                        outs[2 * other][pl.ds(start, BS), j * BS:(j + 1) * BS] = high
                        outs[2 * other + 1][pl.ds(start, BS), j * BS:(j + 1) * BS] = low


def multiply(last, *refs):
    if last:
        c_filter, panel, before = refs[:3]
        refs = refs[3:]
    else:
        panel, refs = refs[0], refs[1:]
    sources, out, rights, arrived, refs = refs[:4], refs[4], refs[5:9], refs[9], refs[10:]
    if not last:
        held, landed, refs = refs[0], refs[1], refs[2:]
    places, copied, left_high, left_low = refs
    zh = lax.axis_index("row") // 16
    copies = [
        pltpu.make_async_copy(source, to, arrived.at[n])
        for n, (source, to) in enumerate(zip(sources, rights))
    ]
    if not last:
        loading = pltpu.make_async_copy(panel, held, landed)
        loading.start()
    for copy in copies:
        copy.start()
    if not last:
        loading.wait()
        panel = held
    placing = [
        pltpu.make_async_copy(panel.at[pl.ds(zl * PAY_ROWS + SLOT_ROWS, 8)], places.at[zl], copied.at[zl])
        for zl in range(NZL)
    ]
    for copy in placing:
        copy.start()
    for copy in placing:
        copy.wait()

    def unpack(n):
        zl = (zh if n < 4 else 1 - zh) * 4 + n % 4
        for i in range(4):
            for k in range(2):
                slot = places[zl, 2 * i + k, 0].astype(jnp.int32)
                start = pl.multiple_of(zl * PAY_ROWS + jnp.maximum(slot, 0) * BS, 8)
                high, low = split(jnp.where(slot >= 0, panel[pl.ds(start, BS), :], 0.0))
                left_high[i * BS:(i + 1) * BS, (2 * n + k) * BS:(2 * n + k + 1) * BS] = high
                left_low[i * BS:(i + 1) * BS, (2 * n + k) * BS:(2 * n + k + 1) * BS] = low

    dot = functools.partial(jnp.dot, preferred_element_type=jnp.float32)
    total = before[...] if last else None
    for n in range(4):
        unpack(n)
    for family in range(2):
        if family == 0:
            for n in range(4, 8):
                unpack(n)
        for copy in copies[2 * family:2 * family + 2]:
            copy.wait()
        wide = slice(HALF_ROWS * family, HALF_ROWS * (family + 1))
        right_high, right_low = rights[2 * family][...], rights[2 * family + 1][...]
        part = dot(left_high[:, wide], right_high)
        part = part + dot(left_high[:, wide], right_low)
        part = part + dot(left_low[:, wide], right_high)
        total = part if total is None else total + part
    if not last:
        out[...] = total
        return
    for i in range(4):
        for j in range(4):
            value = total[i * BS:(i + 1) * BS, j * BS:(j + 1) * BS]
            out[i, j] = jnp.where(c_filter[i, j] > 0, value, 0.0)


VMEM = pl.BlockSpec(memory_space=pltpu.VMEM)
SMEM = pl.BlockSpec(memory_space=pltpu.SMEM)
ANY = pl.BlockSpec(memory_space=pl.ANY)


def on_device(a_blocks, b_blocks, a_occupied, b_occupied, c_filter, row_sizes, k_sizes, col_sizes):
    right = pl.pallas_call(
        mask_right,
        out_shape=jax.ShapeDtypeStruct((4 * BS, BS), jnp.float32),
        in_specs=[VMEM, SMEM, SMEM, SMEM],
        out_specs=VMEM,
    )(b_blocks, b_occupied, k_sizes, col_sizes)
    partner = send(right, other_half())
    first = [right, *near(right, along_x)]
    left = pl.pallas_call(
        pack_left,
        out_shape=jax.ShapeDtypeStruct((PAY_ROWS, BS), jnp.float32),
        in_specs=[VMEM, SMEM, SMEM, SMEM],
        out_specs=VMEM,
    )(a_blocks, a_occupied, row_sizes, k_sizes)
    same_core = [[zl * NC + core for zl in range(NZL)] for core in range(NC)]
    own = lax.all_gather(left, "col", axis_index_groups=same_core, tiled=True)
    partner, *first = lax.optimization_barrier((partner, *first))
    second = [partner, *near(partner, along_y)]
    first = jnp.concatenate(first)
    second = jnp.concatenate(lax.optimization_barrier(tuple(second)))
    rights = (first, *gather_far(first, along_y), second, *gather_far(second, along_x))
    prepared = []
    for family in range(2):
        prepared += pl.pallas_call(
            functools.partial(prepare_right, family == 0),
            out_shape=[jax.ShapeDtypeStruct((HALF_ROWS, 4 * BS), jnp.bfloat16)] * 4,
            in_specs=[VMEM] * 5,
            out_specs=[VMEM] * 4,
            compiler_params=pltpu.CompilerParams(vmem_limit_bytes=24 << 20),
        )(*rights[5 * family:5 * family + 5])
    own, *prepared = lax.optimization_barrier((own, *prepared))
    other = send(own, other_core())
    gathered = [pltpu.VMEM((HALF_ROWS, 4 * BS), jnp.bfloat16)] * 4 + [pltpu.SemaphoreType.DMA((4,))]
    scratch = [
        pltpu.SMEM((NZL, 8, BS), jnp.float32),
        pltpu.SemaphoreType.DMA((NZL,)),
        pltpu.VMEM((4 * BS, 16 * BS), jnp.bfloat16),
        pltpu.VMEM((4 * BS, 16 * BS), jnp.bfloat16),
    ]
    cost = pl.CostEstimate(flops=6 * 512 * 512 * 2048, bytes_accessed=8 << 20, transcendentals=0)
    part = pl.pallas_call(
        functools.partial(multiply, False),
        out_shape=jax.ShapeDtypeStruct((4 * BS, 4 * BS), jnp.float32),
        in_specs=[ANY] * 5,
        out_specs=VMEM,
        scratch_shapes=gathered
        + [pltpu.VMEM((NZL * PAY_ROWS, BS), jnp.float32), pltpu.SemaphoreType.DMA]
        + scratch,
        compiler_params=pltpu.CompilerParams(vmem_limit_bytes=52 << 20),
        cost_estimate=cost,
    )(own, *prepared[:2], *prepared[4:6])
    return pl.pallas_call(
        functools.partial(multiply, True),
        out_shape=jax.ShapeDtypeStruct((4, 4, BS, BS), jnp.float32),
        in_specs=[SMEM] + [VMEM] * 2 + [ANY] * 4,
        out_specs=VMEM,
        scratch_shapes=gathered + scratch,
        compiler_params=pltpu.CompilerParams(vmem_limit_bytes=24 << 20),
        cost_estimate=cost,
    )(c_filter, other, part, *prepared[2:4], *prepared[6:])


def solution(mesh):
    placed = (
        P("row", "col", None, None),
        P("row", "col", None, None),
        P("row", "col"),
        P("row", "col"),
        P("row", "col"),
        P("row"),
        P(),
        P("col"),
    )
    return jax.shard_map(
        on_device,
        mesh=mesh,
        in_specs=placed,
        out_specs=P("row", "col", None, None),
        check_vma=False,
    )
```

time: 154 us -> 149 us (0.968)
  the two profiles are of different devices: /device:TPU:199 before, /device:TPU:39 now
where the time goes in v2:
time: 149 us; the launch traced here: 148 us
  starting transfers between devices  68.2 us (46%)
  waiting for transfers between devices  37.5 us (25%)
  Pallas kernels  21.2 us (14%)
  between operations  13.8 us (9%)
  local copies, waits for them, and re-layouts  7.46 us (5%)
    ppermute x16, starting transfers between devices, send(): return lax.ppermute(value, AXES, pairs)  68.2 us
    ppermute x16, waiting for transfers between devices, send(): return lax.ppermute(value, AXES, pairs)  37.4 us
    pallas_call x1, Pallas kernels, on_device(): pl.pallas_call(functools.partial(multiply, False), out_shape=jax.ShapeDty...  8.5 us
    pallas_call x1, Pallas kernels, on_device(): pl.pallas_call(functools.partial(multiply, True), out_shape=jax.ShapeDtyp...  7.52 us
    unnamed x21, local copies, waits for them, and re-layouts  7.28 us
  transfers between devices with their start and end apart: 17, of which 4 were waited for; matrix products, arithmetic and copies ran while one was open for 1% of the time, Pallas kernels for 8%

profile of v2, /device:TPU:39, one launch (start us, length us, event | category | flops | bytes accessed | tf_op | source)
XLA Modules:
  0.0 148.1 jit_solution(549167732700890990)
XLA Ops:
  6.5 0.0 all-gather.2.cloned.1.call-start
  6.5 1.3 copy.9.occupied
  7.9 1.9 %shard_map.82 = f32[776,128]{1,0:T(8,128)} custom-call(f32[4,2,128,128]{3,2,1,0:T(8,128)} %blocks.2, s32[4,2]{1,0:T(4,128)} %copy.9.occupied, s32[4]{0:T(128)} %row_sizes.1, s32[32]{0:T(128)} %k_sizes.3), custom_call_target="tpu_custom_call" | custom-call | tf_op jit(solution)/shard_map/pallas_call | solution.py:206
  9.8 0.0 all-gather.2.cloned.1.call-update
  9.8 1.7 %shard_map.83 = f32[512,128]{1,0:T(8,128)} custom-call(f32[1,4,128,128]{3,2,1,0:T(8,128)} %blocks.3, s32[1,4]{1,0:T(1,128)} %occupied.2, s32[32]{0:T(128)} %k_sizes.3, s32[4]{0:T(128)} %col_sizes.1), custom_call_target="tpu_custom_call" | custom-call | tf_op jit(solution)/shard_map/pallas_call | solution.py:198
  11.5 14.5 %collective-permute-start = (f32[512,128]{1,0:T(8,128)}, f32[512,128]{1,0:T(8,128)S(1)}, u32[]{:S(2)}, u32[]{:S(2)}) collective-permute-start(f32[512,128]{1,0:T(8,128)} %shard_map.83), channel_id=1, source_target_pairs={{0,256},{1,257},{2,258},{3,259},{4,260},{5,261},{6,262},{7,263},{8... | collective-permute-start | bytes 786440 | tf_op jit(solution)/shard_map/ppermute | solution.py:52
  26.0 2.1 %collective-permute-start.1 = (f32[512,128]{1,0:T(8,128)}, f32[512,128]{1,0:T(8,128)S(1)}, u32[]{:S(2)}, u32[]{:S(2)}) collective-permute-start(f32[512,128]{1,0:T(8,128)} %shard_map.83), channel_id=1, source_target_pairs={{0,64},{1,65},{2,66},{3,67},{4,68},{5,69},{6,70},{7,71},{8,72},{9,... | collective-permute-start | bytes 786440 | tf_op jit(solution)/shard_map/ppermute | solution.py:52
  28.1 3.2 %collective-permute-start.2 = (f32[512,128]{1,0:T(8,128)}, f32[512,128]{1,0:T(8,128)S(1)}, u32[]{:S(2)}, u32[]{:S(2)}) collective-permute-start(f32[512,128]{1,0:T(8,128)} %shard_map.83), channel_id=1, source_target_pairs={{0,192},{1,193},{2,194},{3,195},{4,196},{5,197},{6,198},{7,199},{8... | collective-permute-start | bytes 786440 | tf_op jit(solution)/shard_map/ppermute | solution.py:52
  31.3 3.0 %collective-permute-start.3 = (f32[512,128]{1,0:T(8,128)}, f32[512,128]{1,0:T(8,128)S(1)}, u32[]{:S(2)}, u32[]{:S(2)}) collective-permute-start(f32[512,128]{1,0:T(8,128)} %shard_map.83), channel_id=1, source_target_pairs={{0,128},{1,129},{2,130},{3,131},{4,132},{5,133},{6,134},{7,135},{8... | collective-permute-start | bytes 786440 | tf_op jit(solution)/shard_map/ppermute | solution.py:52
  34.4 18.2 %collective-permute-done = f32[512,128]{1,0:T(8,128)S(1)} collective-permute-done((f32[512,128]{1,0:T(8,128)}, f32[512,128]{1,0:T(8,128)S(1)}, u32[]{:S(2)}, u32[]{:S(2)}) %collective-permute-start) | collective-permute-done | bytes 262176 | tf_op jit(solution)/shard_map/ppermute | solution.py:52
  52.6 0.0 collective-permute-done.1
  52.6 0.0 collective-permute-done.2
  52.6 0.0 collective-permute-done.3
  52.6 4.6 %collective-permute-start.10 = (f32[512,128]{1,0:T(8,128)S(1)}, f32[512,128]{1,0:T(8,128)S(1)}, u32[]{:S(2)}, u32[]{:S(2)}) collective-permute-start(f32[512,128]{1,0:T(8,128)S(1)} %collective-permute-done), channel_id=1, source_target_pairs={{0,32},{1,33},{2,34},{3,35},{4,36},{5,37},{6,38},{7,39},{8,40},{9,... | collective-permute-start | bytes 786440 | tf_op jit(solution)/shard_map/ppermute | solution.py:52
  57.2 3.0 %collective-permute-start.8 = (f32[512,128]{1,0:T(8,128)S(1)}, f32[512,128]{1,0:T(8,128)S(1)}, u32[]{:S(2)}, u32[]{:S(2)}) collective-permute-start(f32[512,128]{1,0:T(8,128)S(1)} %collective-permute-done), channel_id=1, source_target_pairs={{0,16},{1,17},{2,18},{3,19},{4,20},{5,21},{6,22},{7,23},{8,24},{9,... | collective-permute-start | bytes 786440 | tf_op jit(solution)/shard_map/ppermute | solution.py:52
  60.2 3.5 %collective-permute-start.9 = (f32[512,128]{1,0:T(8,128)S(1)}, f32[512,128]{1,0:T(8,128)S(1)}, u32[]{:S(2)}, u32[]{:S(2)}) collective-permute-start(f32[512,128]{1,0:T(8,128)S(1)} %collective-permute-done), channel_id=1, source_target_pairs={{0,48},{1,49},{2,50},{3,51},{4,52},{5,53},{6,54},{7,55},{8,56},{9,... | collective-permute-start | bytes 786440 | tf_op jit(solution)/shard_map/ppermute | solution.py:52
  63.7 1.0 constant_dynamic-update-slice_fusion.3
  64.8 1.9 %collective-permute-start.4 = (f32[2048,128]{1,0:T(8,128)S(1)}, f32[2048,128]{1,0:T(8,128)S(1)}, u32[]{:S(2)}, u32[]{:S(2)}) collective-permute-start(f32[2048,128]{1,0:T(8,128)S(1)} %constant_dynamic-update-slice_fusion.refs_0_), channel_id=1, source_target_pairs={{0,16},{1,17},{2,18},{3,19},{4,20},{5,21},{6,22},{7,23},{8,24},{9,... | collective-permute-start | bytes 3145736 | tf_op jit(solution)/shard_map/ppermute | solution.py:52
  66.7 4.6 %collective-permute-start.5 = (f32[2048,128]{1,0:T(8,128)S(1)}, f32[2048,128]{1,0:T(8,128)S(1)}, u32[]{:S(2)}, u32[]{:S(2)}) collective-permute-start(f32[2048,128]{1,0:T(8,128)S(1)} %constant_dynamic-update-slice_fusion.refs_0_), channel_id=1, source_target_pairs={{0,48},{1,49},{2,50},{3,51},{4,52},{5,53},{6,54},{7,55},{8,56},{9,... | collective-permute-start | bytes 3145736 | tf_op jit(solution)/shard_map/ppermute | solution.py:52
  71.3 0.0 collective-permute-done.10
  71.3 0.0 collective-permute-done.8
  71.3 0.0 collective-permute-done.9
  71.4 3.5 %collective-permute-start.11 = (f32[2048,128]{1,0:T(8,128)S(1)}, f32[2048,128]{1,0:T(8,128)S(1)}, u32[]{:S(2)}, u32[]{:S(2)}) collective-permute-start(f32[2048,128]{1,0:T(8,128)S(1)} %constant_dynamic-update-slice_fusion.4.refs_0_), channel_id=1, source_target_pairs={{0,64},{1,65},{2,66},{3,67},{4,68},{5,69},{6,70},{7,71},{8,72},{9,... | collective-permute-start | bytes 3145736 | tf_op jit(solution)/shard_map/ppermute | solution.py:52
  74.9 1.9 %collective-permute-start.12 = (f32[2048,128]{1,0:T(8,128)S(1)}, f32[2048,128]{1,0:T(8,128)S(1)}, u32[]{:S(2)}, u32[]{:S(2)}) collective-permute-start(f32[2048,128]{1,0:T(8,128)S(1)} %constant_dynamic-update-slice_fusion.4.refs_0_), channel_id=1, source_target_pairs={{0,192},{1,193},{2,194},{3,195},{4,196},{5,197},{6,198},{7,199},{8... | collective-permute-start | bytes 3145736 | tf_op jit(solution)/shard_map/ppermute | solution.py:52
  76.8 12.8 %collective-permute-done.4.refs_1_ = f32[2048,128]{1,0:T(8,128)S(1)} collective-permute-done((f32[2048,128]{1,0:T(8,128)S(1)}, f32[2048,128]{1,0:T(8,128)S(1)}, u32[]{:S(2)}, u32[]{:S(2)}) %collective-permute-start.4) | collective-permute-done | bytes 1048608 | tf_op jit(solution)/shard_map/ppermute | solution.py:52
  89.7 4.2 %collective-permute-start.6 = (f32[1024,128]{1,0:T(8,128)S(1)}, f32[1024,128]{1,0:T(8,128)S(1)}, u32[]{:S(2)}, u32[]{:S(2)}) collective-permute-start(f32[1024,128]{1,0:T(8,128)S(1)} %slice.16), channel_id=1, source_target_pairs={{0,16},{1,17},{2,18},{3,19},{4,20},{5,21},{6,22},{7,23},{8,24},{9,... | collective-permute-start | bytes 1572872 | tf_op jit(solution)/shard_map/ppermute | solution.py:52
  93.9 0.0 collective-permute-done.5.refs_2_
  94.0 2.3 %collective-permute-start.7 = (f32[1024,128]{1,0:T(8,128)S(1)}, f32[1024,128]{1,0:T(8,128)S(1)}, u32[]{:S(2)}, u32[]{:S(2)}) collective-permute-start(f32[1024,128]{1,0:T(8,128)S(1)} %slice.17), channel_id=1, source_target_pairs={{0,48},{1,49},{2,50},{3,51},{4,52},{5,53},{6,54},{7,55},{8,56},{9,... | collective-permute-start | bytes 1572872 | tf_op jit(solution)/shard_map/ppermute | solution.py:52
  96.2 0.0 collective-permute-done.11.refs_1_
  96.3 4.2 %collective-permute-start.13 = (f32[1024,128]{1,0:T(8,128)S(1)}, f32[1024,128]{1,0:T(8,128)S(1)}, u32[]{:S(2)}, u32[]{:S(2)}) collective-permute-start(f32[1024,128]{1,0:T(8,128)S(1)} %slice.18), channel_id=1, source_target_pairs={{0,64},{1,65},{2,66},{3,67},{4,68},{5,69},{6,70},{7,71},{8,72},{9,... | collective-permute-start | bytes 1572872 | tf_op jit(solution)/shard_map/ppermute | solution.py:52
  100.5 0.0 collective-permute-done.12.refs_2_
  100.5 1.9 %collective-permute-start.14 = (f32[1024,128]{1,0:T(8,128)S(1)}, f32[1024,128]{1,0:T(8,128)S(1)}, u32[]{:S(2)}, u32[]{:S(2)}) collective-permute-start(f32[1024,128]{1,0:T(8,128)S(1)} %slice.19), channel_id=1, source_target_pairs={{0,192},{1,193},{2,194},{3,195},{4,196},{5,197},{6,198},{7,199},{8... | collective-permute-start | bytes 1572872 | tf_op jit(solution)/shard_map/ppermute | solution.py:52
  102.4 0.0 collective-permute-done.6.refs_3_
  102.5 3.0 %collective-permute-done.7.refs_4_ = f32[1024,128]{1,0:T(8,128)S(1)} collective-permute-done((f32[1024,128]{1,0:T(8,128)S(1)}, f32[1024,128]{1,0:T(8,128)S(1)}, u32[]{:S(2)}, u32[]{:S(2)}) %collective-permute-start.7) | collective-permute-done | bytes 524320 | tf_op jit(solution)/shard_map/ppermute | solution.py:52
  105.5 0.8 shard_map.84
  106.3 0.0 copy-start
  106.3 1.0 copy-done
  107.3 1.0 copy-done.1
  108.3 0.0 collective-permute-done.13.refs_3_
  108.3 3.4 %collective-permute-done.14.refs_4_ = f32[1024,128]{1,0:T(8,128)S(1)} collective-permute-done((f32[1024,128]{1,0:T(8,128)S(1)}, f32[1024,128]{1,0:T(8,128)S(1)}, u32[]{:S(2)}, u32[]{:S(2)}) %collective-permute-start.14) | collective-permute-done | bytes 524320 | tf_op jit(solution)/shard_map/ppermute | solution.py:52
  111.7 0.8 shard_map.85
  112.5 0.9 copy-done.2
  113.4 1.0 copy-done.4
  114.4 1.0 copy-done.5
  115.4 9.8 %collective-permute-start.15 = (f32[6208,128]{1,0:T(8,128)}, f32[6208,128]{1,0:T(8,128)S(1)}, u32[]{:S(2)}, u32[]{:S(2)}) collective-permute-start(f32[6208,128]{1,0:T(8,128)} %all-gather.2.cloned.1.call-done.refs_0_), channel_id=1, source_target_pairs={{0,1},{1,0},{2,3},{3,2},{4,5},{5,4},{6,7},{7,6},{8,9},{9,8},{10,11... | collective-permute-start | bytes 9535496 | tf_op jit(solution)/shard_map/ppermute | solution.py:52
  125.2 8.5 %shard_map.86.refs_2_ = f32[512,512]{1,0:T(8,128)S(1)} custom-call(f32[6208,128]{1,0:T(8,128)} %all-gather.2.cloned.1.call-done.refs_0_, bf16[1024,512]{1,0:T(8,128)(2,1)} %copy-done, bf16[1024,512]{1,0:T(8,128)(2,1)} %copy-done.1, bf16[1024,512]{1,0:T(8,128)(2,1)} %copy-done.4, bf16[1024,512]{1,0:T(8,128)(2,1)} %copy-done.5), custom_call_target="tpu_custom_call" | custom-call | flops 3221225472 | bytes 8388608 | tf_op jit(solution)/shard_map/pallas_call | solution.py:238
  133.7 0.0 collective-permute-done.15.refs_1_
  133.7 7.5 %shard_map.87 = f32[4,4,128,128]{3,2,1,0:T(8,128)} custom-call(s32[4,4]{1,0:T(4,128)S(1)} %copy-done.6, f32[6208,128]{1,0:T(8,128)S(1)} %collective-permute-done.15.refs_1_, f32[512,512]{1,0:T(8,128)S(1)} %shard_map.86.refs_2_, bf16[1024,512]{1,0:T(8,128)(2,1)S(1)} %get-tuple-element.53.refs_3_, bf16[1024,512]{1,0:T(8,128)(2,1)S(1)} %get-tuple-element.54.refs_4_, ...), custom_call_target="tpu_custom_call" | custom-call | flops 3221225472 | bytes 8388608 | tf_op jit(solution)/shard_map/pallas_call | solution.py:249
  (20 shorter events, 0.3 us)
Async XLA Ops:
  6.5 108.8 %all-gather.2.cloned.1.call-start = ((), (), s32[]{:S(2)}) async-start(), calls=%async_computation | async-start | bytes 3575808 | tf_op jit(solution)/shard_map/all_gather | solution.py:213
  11.5 41.0 %collective-permute-start = (f32[512,128]{1,0:T(8,128)}, f32[512,128]{1,0:T(8,128)S(1)}, u32[]{:S(2)}, u32[]{:S(2)}) collective-permute-start(f32[512,128]{1,0:T(8,128)} %shard_map.83), channel_id=1, source_target_pairs={{0,256},{1,257},{2,258},{3,259},{4,260},{5,261},{6,262},{7,263},{8... | collective-permute-start | bytes 786440 | tf_op jit(solution)/shard_map/ppermute | solution.py:52
  26.0 26.5 %collective-permute-start.1 = (f32[512,128]{1,0:T(8,128)}, f32[512,128]{1,0:T(8,128)S(1)}, u32[]{:S(2)}, u32[]{:S(2)}) collective-permute-start(f32[512,128]{1,0:T(8,128)} %shard_map.83), channel_id=1, source_target_pairs={{0,64},{1,65},{2,66},{3,67},{4,68},{5,69},{6,70},{7,71},{8,72},{9,... | collective-permute-start | bytes 786440 | tf_op jit(solution)/shard_map/ppermute | solution.py:52
  28.1 24.4 %collective-permute-start.2 = (f32[512,128]{1,0:T(8,128)}, f32[512,128]{1,0:T(8,128)S(1)}, u32[]{:S(2)}, u32[]{:S(2)}) collective-permute-start(f32[512,128]{1,0:T(8,128)} %shard_map.83), channel_id=1, source_target_pairs={{0,192},{1,193},{2,194},{3,195},{4,196},{5,197},{6,198},{7,199},{8... | collective-permute-start | bytes 786440 | tf_op jit(solution)/shard_map/ppermute | solution.py:52
  31.3 21.2 %collective-permute-start.3 = (f32[512,128]{1,0:T(8,128)}, f32[512,128]{1,0:T(8,128)S(1)}, u32[]{:S(2)}, u32[]{:S(2)}) collective-permute-start(f32[512,128]{1,0:T(8,128)} %shard_map.83), channel_id=1, source_target_pairs={{0,128},{1,129},{2,130},{3,131},{4,132},{5,133},{6,134},{7,135},{8... | collective-permute-start | bytes 786440 | tf_op jit(solution)/shard_map/ppermute | solution.py:52
  52.6 18.7 %collective-permute-start.10 = (f32[512,128]{1,0:T(8,128)S(1)}, f32[512,128]{1,0:T(8,128)S(1)}, u32[]{:S(2)}, u32[]{:S(2)}) collective-permute-start(f32[512,128]{1,0:T(8,128)S(1)} %collective-permute-done), channel_id=1, source_target_pairs={{0,32},{1,33},{2,34},{3,35},{4,36},{5,37},{6,38},{7,39},{8,40},{9,... | collective-permute-start | bytes 786440 | tf_op jit(solution)/shard_map/ppermute | solution.py:52
  57.2 14.1 %collective-permute-start.8 = (f32[512,128]{1,0:T(8,128)S(1)}, f32[512,128]{1,0:T(8,128)S(1)}, u32[]{:S(2)}, u32[]{:S(2)}) collective-permute-start(f32[512,128]{1,0:T(8,128)S(1)} %collective-permute-done), channel_id=1, source_target_pairs={{0,16},{1,17},{2,18},{3,19},{4,20},{5,21},{6,22},{7,23},{8,24},{9,... | collective-permute-start | bytes 786440 | tf_op jit(solution)/shard_map/ppermute | solution.py:52
  60.2 11.1 %collective-permute-start.9 = (f32[512,128]{1,0:T(8,128)S(1)}, f32[512,128]{1,0:T(8,128)S(1)}, u32[]{:S(2)}, u32[]{:S(2)}) collective-permute-start(f32[512,128]{1,0:T(8,128)S(1)} %collective-permute-done), channel_id=1, source_target_pairs={{0,48},{1,49},{2,50},{3,51},{4,52},{5,53},{6,54},{7,55},{8,56},{9,... | collective-permute-start | bytes 786440 | tf_op jit(solution)/shard_map/ppermute | solution.py:52
  64.8 24.9 %collective-permute-start.4 = (f32[2048,128]{1,0:T(8,128)S(1)}, f32[2048,128]{1,0:T(8,128)S(1)}, u32[]{:S(2)}, u32[]{:S(2)}) collective-permute-start(f32[2048,128]{1,0:T(8,128)S(1)} %constant_dynamic-update-slice_fusion.refs_0_), channel_id=1, source_target_pairs={{0,16},{1,17},{2,18},{3,19},{4,20},{5,21},{6,22},{7,23},{8,24},{9,... | collective-permute-start | bytes 3145736 | tf_op jit(solution)/shard_map/ppermute | solution.py:52
  66.7 27.2 %collective-permute-start.5 = (f32[2048,128]{1,0:T(8,128)S(1)}, f32[2048,128]{1,0:T(8,128)S(1)}, u32[]{:S(2)}, u32[]{:S(2)}) collective-permute-start(f32[2048,128]{1,0:T(8,128)S(1)} %constant_dynamic-update-slice_fusion.refs_0_), channel_id=1, source_target_pairs={{0,48},{1,49},{2,50},{3,51},{4,52},{5,53},{6,54},{7,55},{8,56},{9,... | collective-permute-start | bytes 3145736 | tf_op jit(solution)/shard_map/ppermute | solution.py:52
  71.4 24.8 %collective-permute-start.11 = (f32[2048,128]{1,0:T(8,128)S(1)}, f32[2048,128]{1,0:T(8,128)S(1)}, u32[]{:S(2)}, u32[]{:S(2)}) collective-permute-start(f32[2048,128]{1,0:T(8,128)S(1)} %constant_dynamic-update-slice_fusion.4.refs_0_), channel_id=1, source_target_pairs={{0,64},{1,65},{2,66},{3,67},{4,68},{5,69},{6,70},{7,71},{8,72},{9,... | collective-permute-start | bytes 3145736 | tf_op jit(solution)/shard_map/ppermute | solution.py:52
  74.9 25.6 %collective-permute-start.12 = (f32[2048,128]{1,0:T(8,128)S(1)}, f32[2048,128]{1,0:T(8,128)S(1)}, u32[]{:S(2)}, u32[]{:S(2)}) collective-permute-start(f32[2048,128]{1,0:T(8,128)S(1)} %constant_dynamic-update-slice_fusion.4.refs_0_), channel_id=1, source_target_pairs={{0,192},{1,193},{2,194},{3,195},{4,196},{5,197},{6,198},{7,199},{8... | collective-permute-start | bytes 3145736 | tf_op jit(solution)/shard_map/ppermute | solution.py:52
  89.7 12.8 %collective-permute-start.6 = (f32[1024,128]{1,0:T(8,128)S(1)}, f32[1024,128]{1,0:T(8,128)S(1)}, u32[]{:S(2)}, u32[]{:S(2)}) collective-permute-start(f32[1024,128]{1,0:T(8,128)S(1)} %slice.16), channel_id=1, source_target_pairs={{0,16},{1,17},{2,18},{3,19},{4,20},{5,21},{6,22},{7,23},{8,24},{9,... | collective-permute-start | bytes 1572872 | tf_op jit(solution)/shard_map/ppermute | solution.py:52
  94.0 11.5 %collective-permute-start.7 = (f32[1024,128]{1,0:T(8,128)S(1)}, f32[1024,128]{1,0:T(8,128)S(1)}, u32[]{:S(2)}, u32[]{:S(2)}) collective-permute-start(f32[1024,128]{1,0:T(8,128)S(1)} %slice.17), channel_id=1, source_target_pairs={{0,48},{1,49},{2,50},{3,51},{4,52},{5,53},{6,54},{7,55},{8,56},{9,... | collective-permute-start | bytes 1572872 | tf_op jit(solution)/shard_map/ppermute | solution.py:52
  96.3 12.0 %collective-permute-start.13 = (f32[1024,128]{1,0:T(8,128)S(1)}, f32[1024,128]{1,0:T(8,128)S(1)}, u32[]{:S(2)}, u32[]{:S(2)}) collective-permute-start(f32[1024,128]{1,0:T(8,128)S(1)} %slice.18), channel_id=1, source_target_pairs={{0,64},{1,65},{2,66},{3,67},{4,68},{5,69},{6,70},{7,71},{8,72},{9,... | collective-permute-start | bytes 1572872 | tf_op jit(solution)/shard_map/ppermute | solution.py:52
  100.5 11.1 %collective-permute-start.14 = (f32[1024,128]{1,0:T(8,128)S(1)}, f32[1024,128]{1,0:T(8,128)S(1)}, u32[]{:S(2)}, u32[]{:S(2)}) collective-permute-start(f32[1024,128]{1,0:T(8,128)S(1)} %slice.19), channel_id=1, source_target_pairs={{0,192},{1,193},{2,194},{3,195},{4,196},{5,197},{6,198},{7,199},{8... | collective-permute-start | bytes 1572872 | tf_op jit(solution)/shard_map/ppermute | solution.py:52
  106.3 1.0 copy-start
  107.3 1.0 copy-start.1
  112.5 1.0 copy-start.2
  113.4 1.0 copy-start.4
  114.4 1.0 copy-start.5
  115.4 18.3 %copy-start.3 = (bf16[1024,512]{1,0:T(8,128)(2,1)S(1)}, bf16[1024,512]{1,0:T(8,128)(2,1)}, u32[]{:S(2)}) copy-start(bf16[1024,512]{1,0:T(8,128)(2,1)} %copy-done.2) | copy-start | bytes 3145732
  115.4 18.3 %copy-start.6 = (s32[4,4]{1,0:T(4,128)S(1)}, s32[4,4]{1,0:T(4,128)}, u32[]{:S(2)}) copy-start(s32[4,4]{1,0:T(4,128)} %refs_0_.1) | copy-start | bytes 196
  115.4 18.3 %collective-permute-start.15 = (f32[6208,128]{1,0:T(8,128)}, f32[6208,128]{1,0:T(8,128)S(1)}, u32[]{:S(2)}, u32[]{:S(2)}) collective-permute-start(f32[6208,128]{1,0:T(8,128)} %all-gather.2.cloned.1.call-done.refs_0_), channel_id=1, source_target_pairs={{0,1},{1,0},{2,3},{3,2},{4,5},{5,4},{6,7},{7,6},{8,9},{9,8},{10,11... | collective-permute-start | bytes 9535496 | tf_op jit(solution)/shard_map/ppermute | solution.py:52
Sparse Core Ops, SparseCore 0:
  9.9 100.3 all-gather.1

commit v3 on v2

v3 whole, which is shorter than its diff:
```python
import functools

import jax
import jax.numpy as jnp
from jax import lax
from jax.experimental import pallas as pl
from jax.experimental.pallas import tpu as pltpu
from jax.sharding import PartitionSpec as P

BS = 128
CAP = 6
SLOT_ROWS = CAP * BS
PAY_ROWS = SLOT_ROWS + 8
HALF_ROWS = 8 * BS
AXES = ("row", "col")
NX, NY, NZH, NZL, NC = 4, 4, 2, 8, 2


def device_pairs(move):
    pairs = []
    for zh in range(NZH):
        for x in range(NX):
            for y in range(NY):
                for zl in range(NZL):
                    for core in range(NC):
                        to = move(zh, x, y, zl, core)
                        pairs.append((linear(zh, x, y, zl, core), linear(*to)))
    return pairs


def linear(zh, x, y, zl, core):
    return (((zh * NX + x) * NY + y) * NZL + zl) * NC + core


def along_x(n):
    return device_pairs(lambda zh, x, y, zl, core: (zh, (x + n) % NX, y, zl, core))


def along_y(n):
    return device_pairs(lambda zh, x, y, zl, core: (zh, x, (y + n) % NY, zl, core))


def other_half():
    return device_pairs(lambda zh, x, y, zl, core: (1 - zh, x, y, zl, core))


def other_core():
    return device_pairs(lambda zh, x, y, zl, core: (zh, x, y, zl, 1 - core))


def send(value, pairs):
    return lax.ppermute(value, AXES, pairs)


def near(block, along):
    return send(block, along(1)), send(block, along(-1)), send(block, along(2))


def gather_far(group, along):
    half = group.shape[0] // 2
    below = send(group, along(1))
    above = send(group, along(-1))
    return below, above, send(below[:half], along(1)), send(above[half:], along(-1))


def pack_left(blocks, occupied, row_sizes, k_sizes, out):
    first_k = lax.axis_index("col") * 2
    line = lax.broadcasted_iota(jnp.int32, (BS, BS), 0)
    lane = lax.broadcasted_iota(jnp.int32, (BS, BS), 1)
    slot = jnp.int32(0)
    for i in range(4):
        for k in range(2):
            here = (occupied[i, k] > 0) & (slot < CAP)
            place = slot

            @pl.when(here)
            def _():
                keep = (line < row_sizes[i]) & (lane < k_sizes[first_k + k])
                start = pl.multiple_of(place * BS, BS)
                out[pl.ds(start, BS), :] = jnp.where(keep, blocks[i, k], 0.0)

            where = jnp.where(here, place, -1).astype(jnp.float32)
            out[SLOT_ROWS + 2 * i + k, :] = jnp.full((BS,), where, jnp.float32)
            slot = slot + here.astype(jnp.int32)


def mask_right(blocks, occupied, k_sizes, col_sizes, out):
    used = k_sizes[lax.axis_index("row")]
    line = lax.broadcasted_iota(jnp.int32, (BS, BS), 0)
    lane = lax.broadcasted_iota(jnp.int32, (BS, BS), 1)
    for j in range(4):
        columns = jnp.where(occupied[0, j] > 0, col_sizes[j], 0)
        out[j * BS:(j + 1) * BS, :] = jnp.where((line < used) & (lane < columns), blocks[0, j], 0.0)


def split(value):
    high = value.astype(jnp.bfloat16)
    return high, (value - high.astype(jnp.float32)).astype(jnp.bfloat16)


NEAR = (0, -1, 1, 2)


def prepare_right(along_first, *refs):
    pieces, outs = refs[:5], refs[5:]
    wide = outs[0].shape[1] // BS
    row, core = lax.axis_index("row"), lax.axis_index("col") % 2
    x, y = (row // 4) % 4, row % 4
    for step in range(4):
        for t in range(4):
            ref, at = (pieces[step], t) if step < 3 else (pieces[3 + t // 2], t % 2)
            across, along = (NEAR[t], NEAR[step]) if along_first == "x" else (NEAR[step], NEAR[t])
            from_x, from_y = (x + across + 4) % 4, (y + along + 4) % 4
            foreign = from_y // 2 != core
            start = pl.multiple_of(from_x * 2 * BS + from_y % 2 * BS, BS)
            for other in range(2):

                @pl.when(foreign if other else jnp.logical_not(foreign))
                def _():
                    for j in range(wide):
                        high, low = split(ref[(wide * at + j) * BS:(wide * at + j + 1) * BS, :])
                        outs[2 * other][pl.ds(start, BS), j * BS:(j + 1) * BS] = high
                        outs[2 * other + 1][pl.ds(start, BS), j * BS:(j + 1) * BS] = low


def multiply(families, first, last, *refs):
    many = 2 * len(families)
    refs = list(refs)
    c_filter = refs.pop(0) if last else None
    before = None if first else refs.pop(0)
    source, sources, out = refs[0], refs[1:1 + many], refs[1 + many]
    held, rights, arrived, places, copied, left_high, left_low = refs[2 + many], refs[3 + many:3 + 2 * many], *refs[3 + 2 * many:]
    zh = lax.axis_index("row") // 16
    loading, placing = [], []
    for at in range(4 * len(families)):
        family = families[at // 4]
        zl = (1 - zh if family else zh) * 4 + at % 4
        start = pl.multiple_of(zl * PAY_ROWS, 8)
        here = slice(at * PAY_ROWS, (at + 1) * PAY_ROWS)
        loading.append(pltpu.make_async_copy(source.at[pl.ds(start, PAY_ROWS)], held.at[here], arrived.at[at]))
        ends = slice(at * PAY_ROWS + SLOT_ROWS, (at + 1) * PAY_ROWS)
        placing.append(pltpu.make_async_copy(held.at[ends], places.at[at], copied.at[at]))
    copies = [pltpu.make_async_copy(begin, to, arrived.at[8 + n]) for n, (begin, to) in enumerate(zip(sources, rights))]
    for copy in loading + copies:
        copy.start()
    for copy, place in zip(loading, placing):
        copy.wait()
        place.start()
    for place in placing:
        place.wait()
    for at in range(4 * len(families)):
        for i in range(4):
            for k in range(2):
                slot = places[at, 2 * i + k, 0].astype(jnp.int32)
                start = pl.multiple_of(at * PAY_ROWS + jnp.maximum(slot, 0) * BS, 8)
                high, low = split(jnp.where(slot >= 0, held[pl.ds(start, BS), :], 0.0))
                left_high[i * BS:(i + 1) * BS, (2 * at + k) * BS:(2 * at + k + 1) * BS] = high
                left_low[i * BS:(i + 1) * BS, (2 * at + k) * BS:(2 * at + k + 1) * BS] = low
    dot = functools.partial(jnp.dot, preferred_element_type=jnp.float32)
    total = None if first else before[...]
    for n in range(len(families)):
        wide = slice(HALF_ROWS * n, HALF_ROWS * (n + 1))
        for copy in copies[2 * n:2 * n + 2]:
            copy.wait()
        right_high, right_low = rights[2 * n][...], rights[2 * n + 1][...]
        part = dot(left_high[:, wide], right_high) + dot(left_high[:, wide], right_low)
        part = part + dot(left_low[:, wide], right_high)
        total = part if total is None else total + part
    if not last:
        out[...] = total
        return
    for i in range(4):
        for j in range(4):
            value = total[i * BS:(i + 1) * BS, j * BS:(j + 1) * BS]
            out[i, j] = jnp.where(c_filter[i, j] > 0, value, 0.0)


def add_products(families, panel, rights, before=None, c_filter=None, limit=52, flops=1 << 30):
    last = c_filter is not None
    operands = ([c_filter] if last else []) + ([] if before is None else [before]) + [panel, *rights]
    specs = ([SMEM] if last else []) + ([] if before is None else [VMEM]) + [ANY] * (1 + len(rights))
    count = len(families)
    shape = (4, 4, BS, BS) if last else (4 * BS, 4 * BS)
    return pl.pallas_call(
        functools.partial(multiply, families, before is None, last),
        out_shape=jax.ShapeDtypeStruct(shape, jnp.float32),
        in_specs=specs,
        out_specs=VMEM,
        scratch_shapes=[pltpu.VMEM((4 * count * PAY_ROWS, BS), jnp.float32)]
        + [pltpu.VMEM(part.shape, part.dtype) for part in rights]
        + [
            pltpu.SemaphoreType.DMA((12,)),
            pltpu.SMEM((NZL, 8, BS), jnp.float32),
            pltpu.SemaphoreType.DMA((NZL,)),
            pltpu.VMEM((4 * BS, 8 * count * BS), jnp.bfloat16),
            pltpu.VMEM((4 * BS, 8 * count * BS), jnp.bfloat16),
        ],
        compiler_params=pltpu.CompilerParams(vmem_limit_bytes=limit << 20),
        cost_estimate=pl.CostEstimate(flops=flops, bytes_accessed=4 << 20, transcendentals=0),
    )(*operands)


VMEM = pl.BlockSpec(memory_space=pltpu.VMEM)
SMEM = pl.BlockSpec(memory_space=pltpu.SMEM)
ANY = pl.BlockSpec(memory_space=pl.ANY)


def prepare(pieces, along_first):
    return pl.pallas_call(
        functools.partial(prepare_right, along_first),
        out_shape=[jax.ShapeDtypeStruct((HALF_ROWS, 4 * BS), jnp.bfloat16)] * 4,
        in_specs=[VMEM] * 5,
        out_specs=[VMEM] * 4,
        compiler_params=pltpu.CompilerParams(vmem_limit_bytes=24 << 20),
    )(*pieces)


def on_device(a_blocks, b_blocks, a_occupied, b_occupied, c_filter, row_sizes, k_sizes, col_sizes):
    right = pl.pallas_call(
        mask_right,
        out_shape=jax.ShapeDtypeStruct((4 * BS, BS), jnp.float32),
        in_specs=[VMEM, SMEM, SMEM, SMEM],
        out_specs=VMEM,
    )(b_blocks, b_occupied, k_sizes, col_sizes)
    partner = send(right, other_half())
    first = [right, *near(right, along_x)]
    left = pl.pallas_call(
        pack_left,
        out_shape=jax.ShapeDtypeStruct((PAY_ROWS, BS), jnp.float32),
        in_specs=[VMEM, SMEM, SMEM, SMEM],
        out_specs=VMEM,
    )(a_blocks, a_occupied, row_sizes, k_sizes)
    same_core = [[zl * NC + core for zl in range(NZL)] for core in range(NC)]
    own = lax.all_gather(left, "col", axis_index_groups=same_core, tiled=True)
    partner, *first = lax.optimization_barrier((partner, *first))
    second = [partner, *near(partner, along_y)]
    first = jnp.concatenate(first)
    second = jnp.concatenate(lax.optimization_barrier(tuple(second)))
    first = [first, *gather_far(first, along_y)]
    second = [second, *gather_far(second, along_x)]
    near_by = prepare(first, "x")
    own, near_by, second[1], second[2] = lax.optimization_barrier((own, near_by, second[1], second[2]))
    other = send(own, other_core())
    far_off = prepare(second, "y")
    part = add_products((0,), own, near_by[:2], limit=52)
    part = add_products((1,), own, far_off[:2], before=part, limit=24, flops=80 << 30)
    return add_products((0, 1), other, (*near_by[2:], *far_off[2:]), before=part, c_filter=c_filter, limit=36)


def solution(mesh):
    placed = (
        P("row", "col", None, None),
        P("row", "col", None, None),
        P("row", "col"),
        P("row", "col"),
        P("row", "col"),
        P("row"),
        P(),
        P("col"),
    )
    return jax.shard_map(
        on_device,
        mesh=mesh,
        in_specs=placed,
        out_specs=P("row", "col", None, None),
        check_vma=False,
    )
```

time: 149 us -> 165 us (1.11)
  the two profiles are of different devices: /device:TPU:39 before, /device:TPU:192 now
where the time goes in v3:
time: 165 us; the launch traced here: 164 us
  waiting for transfers between devices  60.2 us (36%)
  starting transfers between devices  57.4 us (35%)
  Pallas kernels  24.4 us (15%)
  between operations  13.8 us (8%)
  local copies, waits for them, and re-layouts  8.2 us (5%)
    ppermute x16, waiting for transfers between devices, send(): return lax.ppermute(value, AXES, pairs)  60.2 us
    ppermute x16, starting transfers between devices, send(): return lax.ppermute(value, AXES, pairs)  57.4 us
    pallas_call x3, Pallas kernels, add_products(): pl.pallas_call(functools.partial(multiply, families, before is None, last...  17.8 us
    unnamed x23, local copies, waits for them, and re-layouts  6.35 us
  transfers between devices with their start and end apart: 17, of which 6 were waited for; matrix products, arithmetic and copies ran while one was open for 2% of the time, Pallas kernels for 8%

profile of v3, /device:TPU:192, one launch (start us, length us, event | category | flops | bytes accessed | tf_op | source)
XLA Modules:
  0.0 164.1 jit_solution(3914753525560018817)
XLA Ops:
  6.5 1.3 copy.9.occupied
  7.9 1.9 %shard_map.82 = f32[776,128]{1,0:T(8,128)} custom-call(f32[4,2,128,128]{3,2,1,0:T(8,128)} %blocks.2, s32[4,2]{1,0:T(4,128)} %copy.9.occupied, s32[4]{0:T(128)} %row_sizes.1, s32[32]{0:T(128)} %k_sizes.3), custom_call_target="tpu_custom_call" | custom-call | tf_op jit(solution)/shard_map/pallas_call | solution.py:227
  9.8 0.0 all-gather.2.cloned.1.call-update
  9.8 1.7 %shard_map.83 = f32[512,128]{1,0:T(8,128)} custom-call(f32[1,4,128,128]{3,2,1,0:T(8,128)} %blocks.3, s32[1,4]{1,0:T(1,128)} %occupied.2, s32[32]{0:T(128)} %k_sizes.3, s32[4]{0:T(128)} %col_sizes.1), custom_call_target="tpu_custom_call" | custom-call | tf_op jit(solution)/shard_map/pallas_call | solution.py:219
  11.6 4.9 %collective-permute-start.3 = (f32[512,128]{1,0:T(8,128)}, f32[512,128]{1,0:T(8,128)S(1)}, u32[]{:S(2)}, u32[]{:S(2)}) collective-permute-start(f32[512,128]{1,0:T(8,128)} %shard_map.83), channel_id=1, source_target_pairs={{0,128},{1,129},{2,130},{3,131},{4,132},{5,133},{6,134},{7,135},{8... | collective-permute-start | bytes 786440 | tf_op jit(solution)/shard_map/ppermute | solution.py:52
  16.5 3.0 %collective-permute-start.2 = (f32[512,128]{1,0:T(8,128)}, f32[512,128]{1,0:T(8,128)S(1)}, u32[]{:S(2)}, u32[]{:S(2)}) collective-permute-start(f32[512,128]{1,0:T(8,128)} %shard_map.83), channel_id=1, source_target_pairs={{0,192},{1,193},{2,194},{3,195},{4,196},{5,197},{6,198},{7,199},{8... | collective-permute-start | bytes 786440 | tf_op jit(solution)/shard_map/ppermute | solution.py:52
  19.5 2.8 %collective-permute-start.1 = (f32[512,128]{1,0:T(8,128)}, f32[512,128]{1,0:T(8,128)S(1)}, u32[]{:S(2)}, u32[]{:S(2)}) collective-permute-start(f32[512,128]{1,0:T(8,128)} %shard_map.83), channel_id=1, source_target_pairs={{0,64},{1,65},{2,66},{3,67},{4,68},{5,69},{6,70},{7,71},{8,72},{9,... | collective-permute-start | bytes 786440 | tf_op jit(solution)/shard_map/ppermute | solution.py:52
  22.3 9.1 %collective-permute-start = (f32[512,128]{1,0:T(8,128)}, f32[512,128]{1,0:T(8,128)S(1)}, u32[]{:S(2)}, u32[]{:S(2)}) collective-permute-start(f32[512,128]{1,0:T(8,128)} %shard_map.83), channel_id=1, source_target_pairs={{0,256},{1,257},{2,258},{3,259},{4,260},{5,261},{6,262},{7,263},{8... | collective-permute-start | bytes 786440 | tf_op jit(solution)/shard_map/ppermute | solution.py:52
  31.5 0.0 collective-permute-done.3
  31.5 0.0 collective-permute-done.2
  31.5 0.0 collective-permute-done.1
  31.5 37.8 %collective-permute-done = f32[512,128]{1,0:T(8,128)S(1)} collective-permute-done((f32[512,128]{1,0:T(8,128)}, f32[512,128]{1,0:T(8,128)S(1)}, u32[]{:S(2)}, u32[]{:S(2)}) %collective-permute-start) | collective-permute-done | bytes 262176 | tf_op jit(solution)/shard_map/ppermute | solution.py:52
  69.3 5.2 %collective-permute-start.10 = (f32[512,128]{1,0:T(8,128)S(1)}, f32[512,128]{1,0:T(8,128)S(1)}, u32[]{:S(2)}, u32[]{:S(2)}) collective-permute-start(f32[512,128]{1,0:T(8,128)S(1)} %collective-permute-done), channel_id=1, source_target_pairs={{0,32},{1,33},{2,34},{3,35},{4,36},{5,37},{6,38},{7,39},{8,40},{9,... | collective-permute-start | bytes 786440 | tf_op jit(solution)/shard_map/ppermute | solution.py:52
  74.5 2.9 %collective-permute-start.9 = (f32[512,128]{1,0:T(8,128)S(1)}, f32[512,128]{1,0:T(8,128)S(1)}, u32[]{:S(2)}, u32[]{:S(2)}) collective-permute-start(f32[512,128]{1,0:T(8,128)S(1)} %collective-permute-done), channel_id=1, source_target_pairs={{0,48},{1,49},{2,50},{3,51},{4,52},{5,53},{6,54},{7,55},{8,56},{9,... | collective-permute-start | bytes 786440 | tf_op jit(solution)/shard_map/ppermute | solution.py:52
  77.4 2.9 %collective-permute-start.8 = (f32[512,128]{1,0:T(8,128)S(1)}, f32[512,128]{1,0:T(8,128)S(1)}, u32[]{:S(2)}, u32[]{:S(2)}) collective-permute-start(f32[512,128]{1,0:T(8,128)S(1)} %collective-permute-done), channel_id=1, source_target_pairs={{0,16},{1,17},{2,18},{3,19},{4,20},{5,21},{6,22},{7,23},{8,24},{9,... | collective-permute-start | bytes 786440 | tf_op jit(solution)/shard_map/ppermute | solution.py:52
  80.4 1.0 constant_dynamic-update-slice_fusion.3
  81.4 4.1 %collective-permute-start.5 = (f32[2048,128]{1,0:T(8,128)S(1)}, f32[2048,128]{1,0:T(8,128)S(1)}, u32[]{:S(2)}, u32[]{:S(2)}) collective-permute-start(f32[2048,128]{1,0:T(8,128)S(1)} %constant_dynamic-update-slice_fusion.refs_0_), channel_id=1, source_target_pairs={{0,48},{1,49},{2,50},{3,51},{4,52},{5,53},{6,54},{7,55},{8,56},{9,... | collective-permute-start | bytes 3145736 | tf_op jit(solution)/shard_map/ppermute | solution.py:52
  85.6 1.9 %collective-permute-start.4 = (f32[2048,128]{1,0:T(8,128)S(1)}, f32[2048,128]{1,0:T(8,128)S(1)}, u32[]{:S(2)}, u32[]{:S(2)}) collective-permute-start(f32[2048,128]{1,0:T(8,128)S(1)} %constant_dynamic-update-slice_fusion.refs_0_), channel_id=1, source_target_pairs={{0,16},{1,17},{2,18},{3,19},{4,20},{5,21},{6,22},{7,23},{8,24},{9,... | collective-permute-start | bytes 3145736 | tf_op jit(solution)/shard_map/ppermute | solution.py:52
  87.5 0.0 collective-permute-done.10
  87.5 0.5 collective-permute-done.9
  88.0 0.3 collective-permute-done.8
  88.4 4.2 %collective-permute-start.12 = (f32[2048,128]{1,0:T(8,128)S(1)}, f32[2048,128]{1,0:T(8,128)S(1)}, u32[]{:S(2)}, u32[]{:S(2)}) collective-permute-start(f32[2048,128]{1,0:T(8,128)S(1)} %constant_dynamic-update-slice_fusion.4.refs_0_), channel_id=1, source_target_pairs={{0,192},{1,193},{2,194},{3,195},{4,196},{5,197},{6,198},{7,199},{8... | collective-permute-start | bytes 3145736 | tf_op jit(solution)/shard_map/ppermute | solution.py:52
  92.6 1.9 %collective-permute-start.11 = (f32[2048,128]{1,0:T(8,128)S(1)}, f32[2048,128]{1,0:T(8,128)S(1)}, u32[]{:S(2)}, u32[]{:S(2)}) collective-permute-start(f32[2048,128]{1,0:T(8,128)S(1)} %constant_dynamic-update-slice_fusion.4.refs_0_), channel_id=1, source_target_pairs={{0,64},{1,65},{2,66},{3,67},{4,68},{5,69},{6,70},{7,71},{8,72},{9,... | collective-permute-start | bytes 3145736 | tf_op jit(solution)/shard_map/ppermute | solution.py:52
  94.5 15.1 %collective-permute-done.5.refs_2_ = f32[2048,128]{1,0:T(8,128)S(1)} collective-permute-done((f32[2048,128]{1,0:T(8,128)S(1)}, f32[2048,128]{1,0:T(8,128)S(1)}, u32[]{:S(2)}, u32[]{:S(2)}) %collective-permute-start.5) | collective-permute-done | bytes 1048608 | tf_op jit(solution)/shard_map/ppermute | solution.py:52
  109.7 4.5 %collective-permute-start.7 = (f32[1024,128]{1,0:T(8,128)S(1)}, f32[1024,128]{1,0:T(8,128)S(1)}, u32[]{:S(2)}, u32[]{:S(2)}) collective-permute-start(f32[1024,128]{1,0:T(8,128)S(1)} %slice.17), channel_id=1, source_target_pairs={{0,48},{1,49},{2,50},{3,51},{4,52},{5,53},{6,54},{7,55},{8,56},{9,... | collective-permute-start | bytes 1572872 | tf_op jit(solution)/shard_map/ppermute | solution.py:52
  114.2 0.0 collective-permute-done.4.refs_1_
  114.3 1.9 %collective-permute-start.6 = (f32[1024,128]{1,0:T(8,128)S(1)}, f32[1024,128]{1,0:T(8,128)S(1)}, u32[]{:S(2)}, u32[]{:S(2)}) collective-permute-start(f32[1024,128]{1,0:T(8,128)S(1)} %slice.16), channel_id=1, source_target_pairs={{0,16},{1,17},{2,18},{3,19},{4,20},{5,21},{6,22},{7,23},{8,24},{9,... | collective-permute-start | bytes 1572872 | tf_op jit(solution)/shard_map/ppermute | solution.py:52
  116.2 0.9 slice.19
  117.1 4.1 %collective-permute-start.14 = (f32[1024,128]{1,0:T(8,128)}, f32[1024,128]{1,0:T(8,128)}, u32[]{:S(2)}, u32[]{:S(2)}) collective-permute-start(f32[1024,128]{1,0:T(8,128)} %slice.19), channel_id=1, source_target_pairs={{0,192},{1,193},{2,194},{3,195},{4,196},{5,197},{6,198},{7,199},{8... | collective-permute-start | bytes 1572872 | tf_op jit(solution)/shard_map/ppermute | solution.py:52
  121.2 0.9 slice.18
  122.0 1.9 %collective-permute-start.13 = (f32[1024,128]{1,0:T(8,128)}, f32[1024,128]{1,0:T(8,128)}, u32[]{:S(2)}, u32[]{:S(2)}) collective-permute-start(f32[1024,128]{1,0:T(8,128)} %slice.18), channel_id=1, source_target_pairs={{0,64},{1,65},{2,66},{3,67},{4,68},{5,69},{6,70},{7,71},{8,72},{9,... | collective-permute-start | bytes 1572872 | tf_op jit(solution)/shard_map/ppermute | solution.py:52
  124.0 1.1 collective-permute-done.7.refs_4_
  125.1 5.4 %collective-permute-done.6.refs_3_ = f32[1024,128]{1,0:T(8,128)S(1)} collective-permute-done((f32[1024,128]{1,0:T(8,128)S(1)}, f32[1024,128]{1,0:T(8,128)S(1)}, u32[]{:S(2)}, u32[]{:S(2)}) %collective-permute-start.6) | collective-permute-done | bytes 524320 | tf_op jit(solution)/shard_map/ppermute | solution.py:52
  130.4 0.8 shard_map.84
  131.3 0.0 copy-start.1
  131.3 1.0 copy-done.1
  132.2 1.0 copy-done.2
  133.2 1.0 copy-done.3
  134.2 1.0 copy-done.5
  135.2 1.9 %collective-permute-start.15 = (f32[6208,128]{1,0:T(8,128)}, f32[6208,128]{1,0:T(8,128)S(1)}, u32[]{:S(2)}, u32[]{:S(2)}) collective-permute-start(f32[6208,128]{1,0:T(8,128)} %all-gather.2.cloned.1.call-done.refs_0_.refs_1_), channel_id=1, source_target_pairs={{0,1},{1,0},{2,3},{3,2},{4,5},{5,4},{6,7},{7,6},{8,9},{9,8},{10,11... | collective-permute-start | bytes 9535496 | tf_op jit(solution)/shard_map/ppermute | solution.py:52
  137.1 4.4 %shard_map.85.refs_0_ = f32[512,512]{1,0:T(8,128)S(1)} custom-call(f32[6208,128]{1,0:T(8,128)} %all-gather.2.cloned.1.call-done.refs_0_.refs_1_, bf16[1024,512]{1,0:T(8,128)(2,1)} %copy-done.1, bf16[1024,512]{1,0:T(8,128)(2,1)} %copy-done.2), custom_call_target="tpu_custom_call" | custom-call | flops 1073741824 | bytes 4194304 | tf_op jit(solution)/shard_map/pallas_call | solution.py:184
  141.6 0.0 collective-permute-done.14.refs_4_
  141.6 0.0 collective-permute-done.13.refs_3_
  141.6 2.2 %shard_map.86 = (bf16[1024,512]{1,0:T(8,128)(2,1)S(1)}, bf16[1024,512]{1,0:T(8,128)(2,1)S(1)}, bf16[1024,512]{1,0:T(8,128)(2,1)S(1)}, bf16[1024,512]{1,0:T(8,128)(2,1)S(1)}) custom-call(f32[2048,128]{1,0:T(8,128)S(1)} %constant_dynamic-update-slice_fusion.4.refs_0_, f32[2048,128]{1,0:T(8,128)S(1)} %collective-permute-done.11.refs_1_, ...), custom_call_target="tpu_custom_call" | custom-call | tf_op jit(solution)/shard_map/pallas_call | solution.py:209
  143.7 0.0 copy-done
  143.8 0.0 copy-start.7
  143.8 4.2 %shard_map.87.refs_1_ = f32[512,512]{1,0:T(8,128)S(1)} custom-call(f32[512,512]{1,0:T(8,128)S(1)} %shard_map.85.refs_0_, f32[6208,128]{1,0:T(8,128)S(1)} %copy-done, bf16[1024,512]{1,0:T(8,128)(2,1)S(1)} %get-tuple-element.47.refs_2_, bf16[1024,512]{1,0:T(8,128)(2,1)S(1)} %get-tuple-element.48.refs_3_), custom_call_target="tpu_custom_call" | custom-call | flops 85899345920 | bytes 4194304 | tf_op jit(solution)/shard_map/pallas_call | solution.py:184
  148.1 9.1 %shard_map.88 = f32[4,4,128,128]{3,2,1,0:T(8,128)} custom-call(s32[4,4]{1,0:T(4,128)S(1)} %copy-done.7, f32[512,512]{1,0:T(8,128)S(1)} %shard_map.87.refs_1_, f32[6208,128]{1,0:T(8,128)S(1)} %collective-permute-done.15.refs_2_, bf16[1024,512]{1,0:T(8,128)(2,1)S(1)} %copy-done.4, bf16[1024,512]{1,0:T(8,128)(2,1)S(1)} %copy-done.6, ...), custom_call_target="tpu_custom_call" | custom-call | flops 1073741824 | bytes 4194304 | tf_op jit(solution)/shard_map/pallas_call | solution.py:184
  (23 shorter events, 0.2 us)
Async XLA Ops:
  6.5 128.6 %all-gather.2.cloned.1.call-start = ((), (), s32[]{:S(2)}) async-start(), calls=%async_computation | async-start | bytes 3575808 | tf_op jit(solution)/shard_map/all_gather | solution.py:234
  11.6 19.9 %collective-permute-start.3 = (f32[512,128]{1,0:T(8,128)}, f32[512,128]{1,0:T(8,128)S(1)}, u32[]{:S(2)}, u32[]{:S(2)}) collective-permute-start(f32[512,128]{1,0:T(8,128)} %shard_map.83), channel_id=1, source_target_pairs={{0,128},{1,129},{2,130},{3,131},{4,132},{5,133},{6,134},{7,135},{8... | collective-permute-start | bytes 786440 | tf_op jit(solution)/shard_map/ppermute | solution.py:52
  16.5 15.0 %collective-permute-start.2 = (f32[512,128]{1,0:T(8,128)}, f32[512,128]{1,0:T(8,128)S(1)}, u32[]{:S(2)}, u32[]{:S(2)}) collective-permute-start(f32[512,128]{1,0:T(8,128)} %shard_map.83), channel_id=1, source_target_pairs={{0,192},{1,193},{2,194},{3,195},{4,196},{5,197},{6,198},{7,199},{8... | collective-permute-start | bytes 786440 | tf_op jit(solution)/shard_map/ppermute | solution.py:52
  19.5 12.0 %collective-permute-start.1 = (f32[512,128]{1,0:T(8,128)}, f32[512,128]{1,0:T(8,128)S(1)}, u32[]{:S(2)}, u32[]{:S(2)}) collective-permute-start(f32[512,128]{1,0:T(8,128)} %shard_map.83), channel_id=1, source_target_pairs={{0,64},{1,65},{2,66},{3,67},{4,68},{5,69},{6,70},{7,71},{8,72},{9,... | collective-permute-start | bytes 786440 | tf_op jit(solution)/shard_map/ppermute | solution.py:52
  22.3 47.0 %collective-permute-start = (f32[512,128]{1,0:T(8,128)}, f32[512,128]{1,0:T(8,128)S(1)}, u32[]{:S(2)}, u32[]{:S(2)}) collective-permute-start(f32[512,128]{1,0:T(8,128)} %shard_map.83), channel_id=1, source_target_pairs={{0,256},{1,257},{2,258},{3,259},{4,260},{5,261},{6,262},{7,263},{8... | collective-permute-start | bytes 786440 | tf_op jit(solution)/shard_map/ppermute | solution.py:52
  69.3 18.2 %collective-permute-start.10 = (f32[512,128]{1,0:T(8,128)S(1)}, f32[512,128]{1,0:T(8,128)S(1)}, u32[]{:S(2)}, u32[]{:S(2)}) collective-permute-start(f32[512,128]{1,0:T(8,128)S(1)} %collective-permute-done), channel_id=1, source_target_pairs={{0,32},{1,33},{2,34},{3,35},{4,36},{5,37},{6,38},{7,39},{8,40},{9,... | collective-permute-start | bytes 786440 | tf_op jit(solution)/shard_map/ppermute | solution.py:52
  74.5 13.5 %collective-permute-start.9 = (f32[512,128]{1,0:T(8,128)S(1)}, f32[512,128]{1,0:T(8,128)S(1)}, u32[]{:S(2)}, u32[]{:S(2)}) collective-permute-start(f32[512,128]{1,0:T(8,128)S(1)} %collective-permute-done), channel_id=1, source_target_pairs={{0,48},{1,49},{2,50},{3,51},{4,52},{5,53},{6,54},{7,55},{8,56},{9,... | collective-permute-start | bytes 786440 | tf_op jit(solution)/shard_map/ppermute | solution.py:52
  77.4 10.9 %collective-permute-start.8 = (f32[512,128]{1,0:T(8,128)S(1)}, f32[512,128]{1,0:T(8,128)S(1)}, u32[]{:S(2)}, u32[]{:S(2)}) collective-permute-start(f32[512,128]{1,0:T(8,128)S(1)} %collective-permute-done), channel_id=1, source_target_pairs={{0,16},{1,17},{2,18},{3,19},{4,20},{5,21},{6,22},{7,23},{8,24},{9,... | collective-permute-start | bytes 786440 | tf_op jit(solution)/shard_map/ppermute | solution.py:52
  81.4 28.2 %collective-permute-start.5 = (f32[2048,128]{1,0:T(8,128)S(1)}, f32[2048,128]{1,0:T(8,128)S(1)}, u32[]{:S(2)}, u32[]{:S(2)}) collective-permute-start(f32[2048,128]{1,0:T(8,128)S(1)} %constant_dynamic-update-slice_fusion.refs_0_), channel_id=1, source_target_pairs={{0,48},{1,49},{2,50},{3,51},{4,52},{5,53},{6,54},{7,55},{8,56},{9,... | collective-permute-start | bytes 3145736 | tf_op jit(solution)/shard_map/ppermute | solution.py:52
  85.6 28.7 %collective-permute-start.4 = (f32[2048,128]{1,0:T(8,128)S(1)}, f32[2048,128]{1,0:T(8,128)S(1)}, u32[]{:S(2)}, u32[]{:S(2)}) collective-permute-start(f32[2048,128]{1,0:T(8,128)S(1)} %constant_dynamic-update-slice_fusion.refs_0_), channel_id=1, source_target_pairs={{0,16},{1,17},{2,18},{3,19},{4,20},{5,21},{6,22},{7,23},{8,24},{9,... | collective-permute-start | bytes 3145736 | tf_op jit(solution)/shard_map/ppermute | solution.py:52
  88.4 27.8 %collective-permute-start.12 = (f32[2048,128]{1,0:T(8,128)S(1)}, f32[2048,128]{1,0:T(8,128)S(1)}, u32[]{:S(2)}, u32[]{:S(2)}) collective-permute-start(f32[2048,128]{1,0:T(8,128)S(1)} %constant_dynamic-update-slice_fusion.4.refs_0_), channel_id=1, source_target_pairs={{0,192},{1,193},{2,194},{3,195},{4,196},{5,197},{6,198},{7,199},{8... | collective-permute-start | bytes 3145736 | tf_op jit(solution)/shard_map/ppermute | solution.py:52
  92.6 28.6 %collective-permute-start.11 = (f32[2048,128]{1,0:T(8,128)S(1)}, f32[2048,128]{1,0:T(8,128)S(1)}, u32[]{:S(2)}, u32[]{:S(2)}) collective-permute-start(f32[2048,128]{1,0:T(8,128)S(1)} %constant_dynamic-update-slice_fusion.4.refs_0_), channel_id=1, source_target_pairs={{0,64},{1,65},{2,66},{3,67},{4,68},{5,69},{6,70},{7,71},{8,72},{9,... | collective-permute-start | bytes 3145736 | tf_op jit(solution)/shard_map/ppermute | solution.py:52
  109.7 15.4 %collective-permute-start.7 = (f32[1024,128]{1,0:T(8,128)S(1)}, f32[1024,128]{1,0:T(8,128)S(1)}, u32[]{:S(2)}, u32[]{:S(2)}) collective-permute-start(f32[1024,128]{1,0:T(8,128)S(1)} %slice.17), channel_id=1, source_target_pairs={{0,48},{1,49},{2,50},{3,51},{4,52},{5,53},{6,54},{7,55},{8,56},{9,... | collective-permute-start | bytes 1572872 | tf_op jit(solution)/shard_map/ppermute | solution.py:52
  114.3 16.2 %collective-permute-start.6 = (f32[1024,128]{1,0:T(8,128)S(1)}, f32[1024,128]{1,0:T(8,128)S(1)}, u32[]{:S(2)}, u32[]{:S(2)}) collective-permute-start(f32[1024,128]{1,0:T(8,128)S(1)} %slice.16), channel_id=1, source_target_pairs={{0,16},{1,17},{2,18},{3,19},{4,20},{5,21},{6,22},{7,23},{8,24},{9,... | collective-permute-start | bytes 1572872 | tf_op jit(solution)/shard_map/ppermute | solution.py:52
  117.1 24.5 %collective-permute-start.14 = (f32[1024,128]{1,0:T(8,128)}, f32[1024,128]{1,0:T(8,128)}, u32[]{:S(2)}, u32[]{:S(2)}) collective-permute-start(f32[1024,128]{1,0:T(8,128)} %slice.19), channel_id=1, source_target_pairs={{0,192},{1,193},{2,194},{3,195},{4,196},{5,197},{6,198},{7,199},{8... | collective-permute-start | bytes 1572872 | tf_op jit(solution)/shard_map/ppermute | solution.py:52
  122.0 19.5 %collective-permute-start.13 = (f32[1024,128]{1,0:T(8,128)}, f32[1024,128]{1,0:T(8,128)}, u32[]{:S(2)}, u32[]{:S(2)}) collective-permute-start(f32[1024,128]{1,0:T(8,128)} %slice.18), channel_id=1, source_target_pairs={{0,64},{1,65},{2,66},{3,67},{4,68},{5,69},{6,70},{7,71},{8,72},{9,... | collective-permute-start | bytes 1572872 | tf_op jit(solution)/shard_map/ppermute | solution.py:52
  131.3 1.0 copy-start.1
  132.2 1.0 copy-start.2
  133.2 1.0 copy-start.3
  134.2 1.0 copy-start.5
  135.2 12.9 %collective-permute-start.15 = (f32[6208,128]{1,0:T(8,128)}, f32[6208,128]{1,0:T(8,128)S(1)}, u32[]{:S(2)}, u32[]{:S(2)}) collective-permute-start(f32[6208,128]{1,0:T(8,128)} %all-gather.2.cloned.1.call-done.refs_0_.refs_1_), channel_id=1, source_target_pairs={{0,1},{1,0},{2,3},{3,2},{4,5},{5,4},{6,7},{7,6},{8,9},{9,8},{10,11... | collective-permute-start | bytes 9535496 | tf_op jit(solution)/shard_map/ppermute | solution.py:52
  141.5 2.2 %copy-start = (f32[6208,128]{1,0:T(8,128)S(1)}, f32[6208,128]{1,0:T(8,128)}, u32[]{:S(2)}) copy-start(f32[6208,128]{1,0:T(8,128)} %all-gather.2.cloned.1.call-done.refs_0_.refs_1_) | copy-start | bytes 9535492
  143.8 4.3 %copy-start.4 = (bf16[1024,512]{1,0:T(8,128)(2,1)S(1)}, bf16[1024,512]{1,0:T(8,128)(2,1)}, u32[]{:S(2)}) copy-start(bf16[1024,512]{1,0:T(8,128)(2,1)} %copy-done.3) | copy-start | bytes 3145732
  143.8 4.3 %copy-start.6 = (bf16[1024,512]{1,0:T(8,128)(2,1)S(1)}, bf16[1024,512]{1,0:T(8,128)(2,1)}, u32[]{:S(2)}) copy-start(bf16[1024,512]{1,0:T(8,128)(2,1)} %copy-done.5) | copy-start | bytes 3145732
  143.8 4.3 %copy-start.7 = (s32[4,4]{1,0:T(4,128)S(1)}, s32[4,4]{1,0:T(4,128)}, u32[]{:S(2)}) copy-start(s32[4,4]{1,0:T(4,128)} %refs_0_.1) | copy-start | bytes 196
Sparse Core Ops, SparseCore 0:
  10.0 102.7 all-gather.1

commit v4 on v3

--- a/solution.py
+++ b/solution.py
@@ -123,46 +123,36 @@
                         outs[2 * other + 1][pl.ds(start, BS), j * BS:(j + 1) * BS] = low
 
 
-def multiply(families, first, last, *refs):
-    many = 2 * len(families)
-    refs = list(refs)
-    c_filter = refs.pop(0) if last else None
-    before = None if first else refs.pop(0)
-    source, sources, out = refs[0], refs[1:1 + many], refs[1 + many]
-    held, rights, arrived, places, copied, left_high, left_low = refs[2 + many], refs[3 + many:3 + 2 * many], *refs[3 + 2 * many:]
+def multiply(last, *refs):
+    if last:
+        c_filter, before, panel, *rights = refs[:7]
+        out, places, copied, left_high, left_low = refs[7:]
+    else:
+        panel, *rights = refs[:5]
+        out, places, copied, left_high, left_low = refs[5:]
     zh = lax.axis_index("row") // 16
-    loading, placing = [], []
-    for at in range(4 * len(families)):
-        family = families[at // 4]
-        zl = (1 - zh if family else zh) * 4 + at % 4
-        start = pl.multiple_of(zl * PAY_ROWS, 8)
-        here = slice(at * PAY_ROWS, (at + 1) * PAY_ROWS)
-        loading.append(pltpu.make_async_copy(source.at[pl.ds(start, PAY_ROWS)], held.at[here], arrived.at[at]))
-        ends = slice(at * PAY_ROWS + SLOT_ROWS, (at + 1) * PAY_ROWS)
-        placing.append(pltpu.make_async_copy(held.at[ends], places.at[at], copied.at[at]))
-    copies = [pltpu.make_async_copy(begin, to, arrived.at[8 + n]) for n, (begin, to) in enumerate(zip(sources, rights))]
-    for copy in loading + copies:
+    placing = [
+        pltpu.make_async_copy(panel.at[pl.ds(zl * PAY_ROWS + SLOT_ROWS, 8)], places.at[zl], copied.at[zl])
+        for zl in range(NZL)
+    ]
+    for copy in placing:
         copy.start()
-    for copy, place in zip(loading, placing):
+    for copy in placing:
         copy.wait()
-        place.start()
-    for place in placing:
-        place.wait()
-    for at in range(4 * len(families)):
+    for n in range(8):
+        zl = (zh if n < 4 else 1 - zh) * 4 + n % 4
         for i in range(4):
             for k in range(2):
-                slot = places[at, 2 * i + k, 0].astype(jnp.int32)
-                start = pl.multiple_of(at * PAY_ROWS + jnp.maximum(slot, 0) * BS, 8)
-                high, low = split(jnp.where(slot >= 0, held[pl.ds(start, BS), :], 0.0))
-                left_high[i * BS:(i + 1) * BS, (2 * at + k) * BS:(2 * at + k + 1) * BS] = high
-                left_low[i * BS:(i + 1) * BS, (2 * at + k) * BS:(2 * at + k + 1) * BS] = low
+                slot = places[zl, 2 * i + k, 0].astype(jnp.int32)
+                start = pl.multiple_of(zl * PAY_ROWS + jnp.maximum(slot, 0) * BS, 8)
+                high, low = split(jnp.where(slot >= 0, panel[pl.ds(start, BS), :], 0.0))
+                left_high[i * BS:(i + 1) * BS, (2 * n + k) * BS:(2 * n + k + 1) * BS] = high
+                left_low[i * BS:(i + 1) * BS, (2 * n + k) * BS:(2 * n + k + 1) * BS] = low
     dot = functools.partial(jnp.dot, preferred_element_type=jnp.float32)
-    total = None if first else before[...]
-    for n in range(len(families)):
-        wide = slice(HALF_ROWS * n, HALF_ROWS * (n + 1))
-        for copy in copies[2 * n:2 * n + 2]:
-            copy.wait()
-        right_high, right_low = rights[2 * n][...], rights[2 * n + 1][...]
+    total = before[...] if last else None
+    for family in range(2):
+        wide = slice(HALF_ROWS * family, HALF_ROWS * (family + 1))
+        right_high, right_low = rights[2 * family][...], rights[2 * family + 1][...]
         part = dot(left_high[:, wide], right_high) + dot(left_high[:, wide], right_low)
         part = part + dot(left_low[:, wide], right_high)
         total = part if total is None else total + part
@@ -175,29 +165,22 @@
             out[i, j] = jnp.where(c_filter[i, j] > 0, value, 0.0)
 
 
-def add_products(families, panel, rights, before=None, c_filter=None, limit=52, flops=1 << 30):
+def add_products(panel, rights, before=None, c_filter=None, flops=1 << 30):
     last = c_filter is not None
-    operands = ([c_filter] if last else []) + ([] if before is None else [before]) + [panel, *rights]
-    specs = ([SMEM] if last else []) + ([] if before is None else [VMEM]) + [ANY] * (1 + len(rights))
-    count = len(families)
-    shape = (4, 4, BS, BS) if last else (4 * BS, 4 * BS)
     return pl.pallas_call(
-        functools.partial(multiply, families, before is None, last),
-        out_shape=jax.ShapeDtypeStruct(shape, jnp.float32),
-        in_specs=specs,
+        functools.partial(multiply, last),
+        out_shape=jax.ShapeDtypeStruct((4, 4, BS, BS) if last else (4 * BS, 4 * BS), jnp.float32),
+        in_specs=([SMEM, VMEM] if last else []) + [VMEM] * 5,
         out_specs=VMEM,
-        scratch_shapes=[pltpu.VMEM((4 * count * PAY_ROWS, BS), jnp.float32)]
-        + [pltpu.VMEM(part.shape, part.dtype) for part in rights]
-        + [
-            pltpu.SemaphoreType.DMA((12,)),
+        scratch_shapes=[
             pltpu.SMEM((NZL, 8, BS), jnp.float32),
             pltpu.SemaphoreType.DMA((NZL,)),
-            pltpu.VMEM((4 * BS, 8 * count * BS), jnp.bfloat16),
-            pltpu.VMEM((4 * BS, 8 * count * BS), jnp.bfloat16),
+            pltpu.VMEM((4 * BS, 16 * BS), jnp.bfloat16),
+            pltpu.VMEM((4 * BS, 16 * BS), jnp.bfloat16),
         ],
-        compiler_params=pltpu.CompilerParams(vmem_limit_bytes=limit << 20),
+        compiler_params=pltpu.CompilerParams(vmem_limit_bytes=24 << 20),
         cost_estimate=pl.CostEstimate(flops=flops, bytes_accessed=4 << 20, transcendentals=0),
-    )(*operands)
+    )(*((c_filter, before) if last else ()), panel, *rights)
 
 
 VMEM = pl.BlockSpec(memory_space=pltpu.VMEM)
@@ -222,8 +205,8 @@
         in_specs=[VMEM, SMEM, SMEM, SMEM],
         out_specs=VMEM,
     )(b_blocks, b_occupied, k_sizes, col_sizes)
+    first = [right, *near(right, along_x)]
     partner = send(right, other_half())
-    first = [right, *near(right, along_x)]
     left = pl.pallas_call(
         pack_left,
         out_shape=jax.ShapeDtypeStruct((PAY_ROWS, BS), jnp.float32),
@@ -232,19 +215,17 @@
     )(a_blocks, a_occupied, row_sizes, k_sizes)
     same_core = [[zl * NC + core for zl in range(NZL)] for core in range(NC)]
     own = lax.all_gather(left, "col", axis_index_groups=same_core, tiled=True)
-    partner, *first = lax.optimization_barrier((partner, *first))
+    *first, partner = lax.optimization_barrier((*first, partner))
     second = [partner, *near(partner, along_y)]
     first = jnp.concatenate(first)
     second = jnp.concatenate(lax.optimization_barrier(tuple(second)))
     first = [first, *gather_far(first, along_y)]
     second = [second, *gather_far(second, along_x)]
-    near_by = prepare(first, "x")
-    own, near_by, second[1], second[2] = lax.optimization_barrier((own, near_by, second[1], second[2]))
+    own, second[1], second[2] = lax.optimization_barrier((own, second[1], second[2]))
     other = send(own, other_core())
-    far_off = prepare(second, "y")
-    part = add_products((0,), own, near_by[:2], limit=52)
-    part = add_products((1,), own, far_off[:2], before=part, limit=24, flops=80 << 30)
-    return add_products((0, 1), other, (*near_by[2:], *far_off[2:]), before=part, c_filter=c_filter, limit=36)
+    near_by, far_off = prepare(first, "x"), prepare(second, "y")
+    part = add_products(own, (*near_by[:2], *far_off[:2]), flops=30 << 30)
+    return add_products(other, (*near_by[2:], *far_off[2:]), before=part, c_filter=c_filter)
 
 
 def solution(mesh):

time: 165 us -> 145 us (0.88)
  waiting for transfers between devices: 60.2 us -> 45 us
  Pallas kernels: 24.4 us -> 18.7 us
    ppermute x16, waiting for transfers between devices: 60.2 us -> 44.9 us  [send(): return lax.ppermute(value, AXES, pairs)]
    pallas_call x3 -> x2, Pallas kernels: 17.8 us -> 10.9 us  [add_products(): pl.pallas_call(functools.partial(multiply, last), out_shape=jax.ShapeDtyp...]
    unnamed x23, local copies, waits for them, and re-layouts: 6.35 us -> 4.66 us
  transfers between devices with their start and end apart: 17 -> 17, of which waited for: 6 -> 5; matrix products, arithmetic and copies ran while one was open for 2% -> 3% of each run, Pallas kernels for 8% -> 7%
where the time goes in v4:
time: 145 us; the launch traced here: 144 us
  starting transfers between devices  58.7 us (40%)
  waiting for transfers between devices  45 us (31%)
  Pallas kernels  18.7 us (13%)
  between operations  13.7 us (9%)
  local copies, waits for them, and re-layouts  8.19 us (6%)
    ppermute x16, starting transfers between devices, send(): return lax.ppermute(value, AXES, pairs)  58.7 us
    ppermute x16, waiting for transfers between devices, send(): return lax.ppermute(value, AXES, pairs)  44.9 us
    pallas_call x2, Pallas kernels, add_products(): pl.pallas_call(functools.partial(multiply, last), out_shape=jax.ShapeDtyp...  10.9 us
    unnamed x23, local copies, waits for them, and re-layouts  4.66 us
    pallas_call x2, Pallas kernels, prepare(): pl.pallas_call(functools.partial(prepare_right, along_first), out_shape=[...  4.16 us
  transfers between devices with their start and end apart: 17, of which 5 were waited for; matrix products, arithmetic and copies ran while one was open for 3% of the time, Pallas kernels for 7%

profile of v4, /device:TPU:192, one launch (start us, length us, event | category | flops | bytes accessed | tf_op | source)
XLA Modules:
  0.0 144.3 jit_solution(15342939694201650183)
XLA Ops:
  6.5 1.3 copy.9.occupied
  7.9 1.9 %shard_map.82 = f32[776,128]{1,0:T(8,128)} custom-call(f32[4,2,128,128]{3,2,1,0:T(8,128)} %blocks.2, s32[4,2]{1,0:T(4,128)} %copy.9.occupied, s32[4]{0:T(128)} %row_sizes.1, s32[32]{0:T(128)} %k_sizes.3), custom_call_target="tpu_custom_call" | custom-call | tf_op jit(solution)/shard_map/pallas_call | solution.py:210
  9.8 0.0 all-gather.2.cloned.1.call-update
  9.8 1.7 %shard_map.83 = f32[512,128]{1,0:T(8,128)} custom-call(f32[1,4,128,128]{3,2,1,0:T(8,128)} %blocks.3, s32[1,4]{1,0:T(1,128)} %occupied.2, s32[32]{0:T(128)} %k_sizes.3, s32[4]{0:T(128)} %col_sizes.1), custom_call_target="tpu_custom_call" | custom-call | tf_op jit(solution)/shard_map/pallas_call | solution.py:202
  11.5 9.1 %collective-permute-start.3 = (f32[512,128]{1,0:T(8,128)}, f32[512,128]{1,0:T(8,128)S(1)}, u32[]{:S(2)}, u32[]{:S(2)}) collective-permute-start(f32[512,128]{1,0:T(8,128)} %shard_map.83), channel_id=1, source_target_pairs={{0,256},{1,257},{2,258},{3,259},{4,260},{5,261},{6,262},{7,263},{8... | collective-permute-start | bytes 786440 | tf_op jit(solution)/shard_map/ppermute | solution.py:52
  20.6 4.9 %collective-permute-start.2 = (f32[512,128]{1,0:T(8,128)}, f32[512,128]{1,0:T(8,128)S(1)}, u32[]{:S(2)}, u32[]{:S(2)}) collective-permute-start(f32[512,128]{1,0:T(8,128)} %shard_map.83), channel_id=1, source_target_pairs={{0,128},{1,129},{2,130},{3,131},{4,132},{5,133},{6,134},{7,135},{8... | collective-permute-start | bytes 786440 | tf_op jit(solution)/shard_map/ppermute | solution.py:52
  25.6 3.1 %collective-permute-start.1 = (f32[512,128]{1,0:T(8,128)}, f32[512,128]{1,0:T(8,128)S(1)}, u32[]{:S(2)}, u32[]{:S(2)}) collective-permute-start(f32[512,128]{1,0:T(8,128)} %shard_map.83), channel_id=1, source_target_pairs={{0,192},{1,193},{2,194},{3,195},{4,196},{5,197},{6,198},{7,199},{8... | collective-permute-start | bytes 786440 | tf_op jit(solution)/shard_map/ppermute | solution.py:52
  28.6 2.8 %collective-permute-start = (f32[512,128]{1,0:T(8,128)}, f32[512,128]{1,0:T(8,128)S(1)}, u32[]{:S(2)}, u32[]{:S(2)}) collective-permute-start(f32[512,128]{1,0:T(8,128)} %shard_map.83), channel_id=1, source_target_pairs={{0,64},{1,65},{2,66},{3,67},{4,68},{5,69},{6,70},{7,71},{8,72},{9,... | collective-permute-start | bytes 786440 | tf_op jit(solution)/shard_map/ppermute | solution.py:52
  31.4 21.6 %collective-permute-done.3 = f32[512,128]{1,0:T(8,128)S(1)} collective-permute-done((f32[512,128]{1,0:T(8,128)}, f32[512,128]{1,0:T(8,128)S(1)}, u32[]{:S(2)}, u32[]{:S(2)}) %collective-permute-start.3) | collective-permute-done | bytes 262176 | tf_op jit(solution)/shard_map/ppermute | solution.py:52
  53.0 0.0 collective-permute-done.2
  53.0 0.0 collective-permute-done.1
  53.0 0.0 collective-permute-done
  53.0 5.1 %collective-permute-start.6 = (f32[512,128]{1,0:T(8,128)S(1)}, f32[512,128]{1,0:T(8,128)S(1)}, u32[]{:S(2)}, u32[]{:S(2)}) collective-permute-start(f32[512,128]{1,0:T(8,128)S(1)} %collective-permute-done.3), channel_id=1, source_target_pairs={{0,32},{1,33},{2,34},{3,35},{4,36},{5,37},{6,38},{7,39},{8,40},{9,... | collective-permute-start | bytes 786440 | tf_op jit(solution)/shard_map/ppermute | solution.py:52
  58.2 2.9 %collective-permute-start.5 = (f32[512,128]{1,0:T(8,128)S(1)}, f32[512,128]{1,0:T(8,128)S(1)}, u32[]{:S(2)}, u32[]{:S(2)}) collective-permute-start(f32[512,128]{1,0:T(8,128)S(1)} %collective-permute-done.3), channel_id=1, source_target_pairs={{0,48},{1,49},{2,50},{3,51},{4,52},{5,53},{6,54},{7,55},{8,56},{9,... | collective-permute-start | bytes 786440 | tf_op jit(solution)/shard_map/ppermute | solution.py:52
  61.1 3.0 %collective-permute-start.4 = (f32[512,128]{1,0:T(8,128)S(1)}, f32[512,128]{1,0:T(8,128)S(1)}, u32[]{:S(2)}, u32[]{:S(2)}) collective-permute-start(f32[512,128]{1,0:T(8,128)S(1)} %collective-permute-done.3), channel_id=1, source_target_pairs={{0,16},{1,17},{2,18},{3,19},{4,20},{5,21},{6,22},{7,23},{8,24},{9,... | collective-permute-start | bytes 786440 | tf_op jit(solution)/shard_map/ppermute | solution.py:52
  64.1 1.0 constant_dynamic-update-slice_fusion.7
  65.1 0.0 copy-start.2
  65.1 4.1 %collective-permute-start.10 = (f32[2048,128]{1,0:T(8,128)S(1)}, f32[2048,128]{1,0:T(8,128)S(1)}, u32[]{:S(2)}, u32[]{:S(2)}) collective-permute-start(f32[2048,128]{1,0:T(8,128)S(1)} %constant_dynamic-update-slice_fusion.4.refs_0_), channel_id=1, source_target_pairs={{0,48},{1,49},{2,50},{3,51},{4,52},{5,53},{6,54},{7,55},{8,56},{9,... | collective-permute-start | bytes 3145736 | tf_op jit(solution)/shard_map/ppermute | solution.py:52
  69.2 1.9 %collective-permute-start.9 = (f32[2048,128]{1,0:T(8,128)S(1)}, f32[2048,128]{1,0:T(8,128)S(1)}, u32[]{:S(2)}, u32[]{:S(2)}) collective-permute-start(f32[2048,128]{1,0:T(8,128)S(1)} %constant_dynamic-update-slice_fusion.4.refs_0_), channel_id=1, source_target_pairs={{0,16},{1,17},{2,18},{3,19},{4,20},{5,21},{6,22},{7,23},{8,24},{9,... | collective-permute-start | bytes 3145736 | tf_op jit(solution)/shard_map/ppermute | solution.py:52
  71.1 0.0 collective-permute-done.6
  71.1 0.6 collective-permute-done.5
  71.8 0.0 collective-permute-done.4
  71.9 4.8 %collective-permute-start.8 = (f32[2048,128]{1,0:T(8,128)S(1)}, f32[2048,128]{1,0:T(8,128)S(1)}, u32[]{:S(2)}, u32[]{:S(2)}) collective-permute-start(f32[2048,128]{1,0:T(8,128)S(1)} %constant_dynamic-update-slice_fusion.refs_0_), channel_id=1, source_target_pairs={{0,192},{1,193},{2,194},{3,195},{4,196},{5,197},{6,198},{7,199},{8... | collective-permute-start | bytes 3145736 | tf_op jit(solution)/shard_map/ppermute | solution.py:52
  76.7 1.9 %collective-permute-start.7 = (f32[2048,128]{1,0:T(8,128)S(1)}, f32[2048,128]{1,0:T(8,128)S(1)}, u32[]{:S(2)}, u32[]{:S(2)}) collective-permute-start(f32[2048,128]{1,0:T(8,128)S(1)} %constant_dynamic-update-slice_fusion.refs_0_), channel_id=1, source_target_pairs={{0,64},{1,65},{2,66},{3,67},{4,68},{5,69},{6,70},{7,71},{8,72},{9,... | collective-permute-start | bytes 3145736 | tf_op jit(solution)/shard_map/ppermute | solution.py:52
  78.6 14.2 %collective-permute-done.10.refs_2_ = f32[2048,128]{1,0:T(8,128)S(1)} collective-permute-done((f32[2048,128]{1,0:T(8,128)S(1)}, f32[2048,128]{1,0:T(8,128)S(1)}, u32[]{:S(2)}, u32[]{:S(2)}) %collective-permute-start.10) | collective-permute-done | bytes 1048608 | tf_op jit(solution)/shard_map/ppermute | solution.py:52
  92.9 0.8 slice.17
  93.7 4.5 %collective-permute-start.12 = (f32[1024,128]{1,0:T(8,128)}, f32[1024,128]{1,0:T(8,128)}, u32[]{:S(2)}, u32[]{:S(2)}) collective-permute-start(f32[1024,128]{1,0:T(8,128)} %slice.17), channel_id=1, source_target_pairs={{0,48},{1,49},{2,50},{3,51},{4,52},{5,53},{6,54},{7,55},{8,56},{9,... | collective-permute-start | bytes 1572872 | tf_op jit(solution)/shard_map/ppermute | solution.py:52
  98.3 0.0 collective-permute-done.9.refs_1_
  98.3 0.9 slice.16
  99.2 1.9 %collective-permute-start.11 = (f32[1024,128]{1,0:T(8,128)}, f32[1024,128]{1,0:T(8,128)}, u32[]{:S(2)}, u32[]{:S(2)}) collective-permute-start(f32[1024,128]{1,0:T(8,128)} %slice.16), channel_id=1, source_target_pairs={{0,16},{1,17},{2,18},{3,19},{4,20},{5,21},{6,22},{7,23},{8,24},{9,... | collective-permute-start | bytes 1572872 | tf_op jit(solution)/shard_map/ppermute | solution.py:52
  101.1 0.0 collective-permute-done.8.refs_2_
  101.1 0.9 slice.19
  102.0 4.7 %collective-permute-start.14 = (f32[1024,128]{1,0:T(8,128)}, f32[1024,128]{1,0:T(8,128)}, u32[]{:S(2)}, u32[]{:S(2)}) collective-permute-start(f32[1024,128]{1,0:T(8,128)} %slice.19), channel_id=1, source_target_pairs={{0,192},{1,193},{2,194},{3,195},{4,196},{5,197},{6,198},{7,199},{8... | collective-permute-start | bytes 1572872 | tf_op jit(solution)/shard_map/ppermute | solution.py:52
  106.8 0.0 collective-permute-done.7.refs_1_
  106.8 0.8 slice.18
  107.6 1.0 copy-done
  108.6 1.9 %collective-permute-start.13 = (f32[1024,128]{1,0:T(8,128)}, f32[1024,128]{1,0:T(8,128)}, u32[]{:S(2)}, u32[]{:S(2)}) collective-permute-start(f32[1024,128]{1,0:T(8,128)} %slice.18), channel_id=1, source_target_pairs={{0,64},{1,65},{2,66},{3,67},{4,68},{5,69},{6,70},{7,71},{8,72},{9,... | collective-permute-start | bytes 1572872 | tf_op jit(solution)/shard_map/ppermute | solution.py:52
  110.5 0.0 all-gather.2.cloned.1.call-done.refs_0_
  110.6 2.1 %collective-permute-start.15 = (f32[6208,128]{1,0:T(8,128)}, f32[6208,128]{1,0:T(8,128)S(1)}, u32[]{:S(2)}, u32[]{:S(2)}) collective-permute-start(f32[6208,128]{1,0:T(8,128)} %all-gather.2.cloned.1.call-done.refs_0_), channel_id=1, source_target_pairs={{0,1},{1,0},{2,3},{3,2},{4,5},{5,4},{6,7},{7,6},{8,9},{9,8},{10,11... | collective-permute-start | bytes 9535496 | tf_op jit(solution)/shard_map/ppermute | solution.py:52
  112.6 0.0 collective-permute-done.12.refs_4_
  112.6 2.6 %collective-permute-done.11.refs_3_ = f32[1024,128]{1,0:T(8,128)} collective-permute-done((f32[1024,128]{1,0:T(8,128)}, f32[1024,128]{1,0:T(8,128)}, u32[]{:S(2)}, u32[]{:S(2)}) %collective-permute-start.11) | collective-permute-done | bytes 524320 | tf_op jit(solution)/shard_map/ppermute | solution.py:52
  115.3 1.2 copy-done.3
  116.5 2.2 %shard_map.84 = (bf16[1024,512]{1,0:T(8,128)(2,1)S(1)}, bf16[1024,512]{1,0:T(8,128)(2,1)S(1)}, bf16[1024,512]{1,0:T(8,128)(2,1)S(1)}, bf16[1024,512]{1,0:T(8,128)(2,1)S(1)}) custom-call(f32[2048,128]{1,0:T(8,128)S(1)} %copy-done.3, f32[2048,128]{1,0:T(8,128)S(1)} %collective-permute-done.9.refs_1_, f32[2048,128]{1,0:T(8,128)S(1)} %collective-permute-done.10.refs_2_, ...), custom_call_target="tpu_custom_call" | custom-call | tf_op jit(solution)/shard_map/pallas_call | solution.py:192
  118.7 5.8 %collective-permute-done.13.refs_3_ = f32[1024,128]{1,0:T(8,128)} collective-permute-done((f32[1024,128]{1,0:T(8,128)}, f32[1024,128]{1,0:T(8,128)}, u32[]{:S(2)}, u32[]{:S(2)}) %collective-permute-start.13) | collective-permute-done | bytes 524320 | tf_op jit(solution)/shard_map/ppermute | solution.py:52
  124.5 2.0 %shard_map.85 = (bf16[1024,512]{1,0:T(8,128)(2,1)S(1)}, bf16[1024,512]{1,0:T(8,128)(2,1)S(1)}, bf16[1024,512]{1,0:T(8,128)(2,1)S(1)}, bf16[1024,512]{1,0:T(8,128)(2,1)S(1)}) custom-call(f32[2048,128]{1,0:T(8,128)S(1)} %copy-done.5, f32[2048,128]{1,0:T(8,128)S(1)} %copy-done.1, f32[2048,128]{1,0:T(8,128)S(1)} %collective-permute-done.8.refs_2_, ...), custom_call_target="tpu_custom_call" | custom-call | tf_op jit(solution)/shard_map/pallas_call | solution.py:192
  126.5 0.0 copy-start.6
  126.5 4.7 %shard_map.86.refs_1_ = f32[512,512]{1,0:T(8,128)S(1)} custom-call(f32[6208,128]{1,0:T(8,128)S(1)} %copy-done.7, bf16[1024,512]{1,0:T(8,128)(2,1)S(1)} %get-tuple-element.35.refs_1_, bf16[1024,512]{1,0:T(8,128)(2,1)S(1)} %get-tuple-element.36.refs_2_, bf16[1024,512]{1,0:T(8,128)(2,1)S(1)} %get-tuple-element.39.refs_3_, ...), custom_call_target="tpu_custom_call" | custom-call | flops 32212254720 | bytes 4194304 | tf_op jit(solution)/shard_map/pallas_call | solution.py:170
  131.3 6.2 %shard_map.87 = f32[4,4,128,128]{3,2,1,0:T(8,128)} custom-call(s32[4,4]{1,0:T(4,128)S(1)} %copy-done.6, f32[512,512]{1,0:T(8,128)S(1)} %shard_map.86.refs_1_, f32[6208,128]{1,0:T(8,128)S(1)} %collective-permute-done.15.refs_2_, bf16[1024,512]{1,0:T(8,128)(2,1)S(1)} %get-tuple-element.41.refs_3_, bf16[1024,512]{1,0:T(8,128)(2,1)S(1)} %get-tuple-element.42.refs_4_, ...), custom_call_target="tpu_custom_call" | custom-call | flops 1073741824 | bytes 4194304 | tf_op jit(solution)/shard_map/pallas_call | solution.py:170
  (22 shorter events, 0.2 us)
Async XLA Ops:
  6.5 104.0 %all-gather.2.cloned.1.call-start = ((), (), s32[]{:S(2)}) async-start(), calls=%async_computation | async-start | bytes 3575808 | tf_op jit(solution)/shard_map/all_gather | solution.py:217
  11.5 41.5 %collective-permute-start.3 = (f32[512,128]{1,0:T(8,128)}, f32[512,128]{1,0:T(8,128)S(1)}, u32[]{:S(2)}, u32[]{:S(2)}) collective-permute-start(f32[512,128]{1,0:T(8,128)} %shard_map.83), channel_id=1, source_target_pairs={{0,256},{1,257},{2,258},{3,259},{4,260},{5,261},{6,262},{7,263},{8... | collective-permute-start | bytes 786440 | tf_op jit(solution)/shard_map/ppermute | solution.py:52
  20.6 32.4 %collective-permute-start.2 = (f32[512,128]{1,0:T(8,128)}, f32[512,128]{1,0:T(8,128)S(1)}, u32[]{:S(2)}, u32[]{:S(2)}) collective-permute-start(f32[512,128]{1,0:T(8,128)} %shard_map.83), channel_id=1, source_target_pairs={{0,128},{1,129},{2,130},{3,131},{4,132},{5,133},{6,134},{7,135},{8... | collective-permute-start | bytes 786440 | tf_op jit(solution)/shard_map/ppermute | solution.py:52
  25.6 27.5 %collective-permute-start.1 = (f32[512,128]{1,0:T(8,128)}, f32[512,128]{1,0:T(8,128)S(1)}, u32[]{:S(2)}, u32[]{:S(2)}) collective-permute-start(f32[512,128]{1,0:T(8,128)} %shard_map.83), channel_id=1, source_target_pairs={{0,192},{1,193},{2,194},{3,195},{4,196},{5,197},{6,198},{7,199},{8... | collective-permute-start | bytes 786440 | tf_op jit(solution)/shard_map/ppermute | solution.py:52
  28.6 24.4 %collective-permute-start = (f32[512,128]{1,0:T(8,128)}, f32[512,128]{1,0:T(8,128)S(1)}, u32[]{:S(2)}, u32[]{:S(2)}) collective-permute-start(f32[512,128]{1,0:T(8,128)} %shard_map.83), channel_id=1, source_target_pairs={{0,64},{1,65},{2,66},{3,67},{4,68},{5,69},{6,70},{7,71},{8,72},{9,... | collective-permute-start | bytes 786440 | tf_op jit(solution)/shard_map/ppermute | solution.py:52
  53.0 18.1 %collective-permute-start.6 = (f32[512,128]{1,0:T(8,128)S(1)}, f32[512,128]{1,0:T(8,128)S(1)}, u32[]{:S(2)}, u32[]{:S(2)}) collective-permute-start(f32[512,128]{1,0:T(8,128)S(1)} %collective-permute-done.3), channel_id=1, source_target_pairs={{0,32},{1,33},{2,34},{3,35},{4,36},{5,37},{6,38},{7,39},{8,40},{9,... | collective-permute-start | bytes 786440 | tf_op jit(solution)/shard_map/ppermute | solution.py:52
  58.2 13.6 %collective-permute-start.5 = (f32[512,128]{1,0:T(8,128)S(1)}, f32[512,128]{1,0:T(8,128)S(1)}, u32[]{:S(2)}, u32[]{:S(2)}) collective-permute-start(f32[512,128]{1,0:T(8,128)S(1)} %collective-permute-done.3), channel_id=1, source_target_pairs={{0,48},{1,49},{2,50},{3,51},{4,52},{5,53},{6,54},{7,55},{8,56},{9,... | collective-permute-start | bytes 786440 | tf_op jit(solution)/shard_map/ppermute | solution.py:52
  61.1 10.7 %collective-permute-start.4 = (f32[512,128]{1,0:T(8,128)S(1)}, f32[512,128]{1,0:T(8,128)S(1)}, u32[]{:S(2)}, u32[]{:S(2)}) collective-permute-start(f32[512,128]{1,0:T(8,128)S(1)} %collective-permute-done.3), channel_id=1, source_target_pairs={{0,16},{1,17},{2,18},{3,19},{4,20},{5,21},{6,22},{7,23},{8,24},{9,... | collective-permute-start | bytes 786440 | tf_op jit(solution)/shard_map/ppermute | solution.py:52
  65.1 42.5 %copy-start.2 = (f32[2048,128]{1,0:T(8,128)}, f32[2048,128]{1,0:T(8,128)S(1)}, u32[]{:S(2)}) copy-start(f32[2048,128]{1,0:T(8,128)S(1)} %constant_dynamic-update-slice_fusion.4.refs_0_) | copy-start | bytes 3145732
  65.1 27.7 %collective-permute-start.10 = (f32[2048,128]{1,0:T(8,128)S(1)}, f32[2048,128]{1,0:T(8,128)S(1)}, u32[]{:S(2)}, u32[]{:S(2)}) collective-permute-start(f32[2048,128]{1,0:T(8,128)S(1)} %constant_dynamic-update-slice_fusion.4.refs_0_), channel_id=1, source_target_pairs={{0,48},{1,49},{2,50},{3,51},{4,52},{5,53},{6,54},{7,55},{8,56},{9,... | collective-permute-start | bytes 3145736 | tf_op jit(solution)/shard_map/ppermute | solution.py:52
  69.2 29.1 %collective-permute-start.9 = (f32[2048,128]{1,0:T(8,128)S(1)}, f32[2048,128]{1,0:T(8,128)S(1)}, u32[]{:S(2)}, u32[]{:S(2)}) collective-permute-start(f32[2048,128]{1,0:T(8,128)S(1)} %constant_dynamic-update-slice_fusion.4.refs_0_), channel_id=1, source_target_pairs={{0,16},{1,17},{2,18},{3,19},{4,20},{5,21},{6,22},{7,23},{8,24},{9,... | collective-permute-start | bytes 3145736 | tf_op jit(solution)/shard_map/ppermute | solution.py:52
  71.9 35.7 %copy-start.4 = (f32[2048,128]{1,0:T(8,128)}, f32[2048,128]{1,0:T(8,128)S(1)}, u32[]{:S(2)}) copy-start(f32[2048,128]{1,0:T(8,128)S(1)} %constant_dynamic-update-slice_fusion.refs_0_) | copy-start | bytes 3145732
  71.9 29.2 %collective-permute-start.8 = (f32[2048,128]{1,0:T(8,128)S(1)}, f32[2048,128]{1,0:T(8,128)S(1)}, u32[]{:S(2)}, u32[]{:S(2)}) collective-permute-start(f32[2048,128]{1,0:T(8,128)S(1)} %constant_dynamic-update-slice_fusion.refs_0_), channel_id=1, source_target_pairs={{0,192},{1,193},{2,194},{3,195},{4,196},{5,197},{6,198},{7,199},{8... | collective-permute-start | bytes 3145736 | tf_op jit(solution)/shard_map/ppermute | solution.py:52
  76.7 30.1 %collective-permute-start.7 = (f32[2048,128]{1,0:T(8,128)S(1)}, f32[2048,128]{1,0:T(8,128)S(1)}, u32[]{:S(2)}, u32[]{:S(2)}) collective-permute-start(f32[2048,128]{1,0:T(8,128)S(1)} %constant_dynamic-update-slice_fusion.refs_0_), channel_id=1, source_target_pairs={{0,64},{1,65},{2,66},{3,67},{4,68},{5,69},{6,70},{7,71},{8,72},{9,... | collective-permute-start | bytes 3145736 | tf_op jit(solution)/shard_map/ppermute | solution.py:52
  93.7 18.9 %collective-permute-start.12 = (f32[1024,128]{1,0:T(8,128)}, f32[1024,128]{1,0:T(8,128)}, u32[]{:S(2)}, u32[]{:S(2)}) collective-permute-start(f32[1024,128]{1,0:T(8,128)} %slice.17), channel_id=1, source_target_pairs={{0,48},{1,49},{2,50},{3,51},{4,52},{5,53},{6,54},{7,55},{8,56},{9,... | collective-permute-start | bytes 1572872 | tf_op jit(solution)/shard_map/ppermute | solution.py:52
  99.2 16.1 %collective-permute-start.11 = (f32[1024,128]{1,0:T(8,128)}, f32[1024,128]{1,0:T(8,128)}, u32[]{:S(2)}, u32[]{:S(2)}) collective-permute-start(f32[1024,128]{1,0:T(8,128)} %slice.16), channel_id=1, source_target_pairs={{0,16},{1,17},{2,18},{3,19},{4,20},{5,21},{6,22},{7,23},{8,24},{9,... | collective-permute-start | bytes 1572872 | tf_op jit(solution)/shard_map/ppermute | solution.py:52
  102.0 16.7 %collective-permute-start.14 = (f32[1024,128]{1,0:T(8,128)}, f32[1024,128]{1,0:T(8,128)}, u32[]{:S(2)}, u32[]{:S(2)}) collective-permute-start(f32[1024,128]{1,0:T(8,128)} %slice.19), channel_id=1, source_target_pairs={{0,192},{1,193},{2,194},{3,195},{4,196},{5,197},{6,198},{7,199},{8... | collective-permute-start | bytes 1572872 | tf_op jit(solution)/shard_map/ppermute | solution.py:52
  107.6 1.0 copy-start
  108.6 15.9 %collective-permute-start.13 = (f32[1024,128]{1,0:T(8,128)}, f32[1024,128]{1,0:T(8,128)}, u32[]{:S(2)}, u32[]{:S(2)}) collective-permute-start(f32[1024,128]{1,0:T(8,128)} %slice.18), channel_id=1, source_target_pairs={{0,64},{1,65},{2,66},{3,67},{4,68},{5,69},{6,70},{7,71},{8,72},{9,... | collective-permute-start | bytes 1572872 | tf_op jit(solution)/shard_map/ppermute | solution.py:52
  110.6 13.9 %copy-start.1 = (f32[2048,128]{1,0:T(8,128)S(1)}, f32[2048,128]{1,0:T(8,128)}, u32[]{:S(2)}) copy-start(f32[2048,128]{1,0:T(8,128)} %copy-done) | copy-start | bytes 3145732
  110.6 20.7 %collective-permute-start.15 = (f32[6208,128]{1,0:T(8,128)}, f32[6208,128]{1,0:T(8,128)S(1)}, u32[]{:S(2)}, u32[]{:S(2)}) collective-permute-start(f32[6208,128]{1,0:T(8,128)} %all-gather.2.cloned.1.call-done.refs_0_), channel_id=1, source_target_pairs={{0,1},{1,0},{2,3},{3,2},{4,5},{5,4},{6,7},{7,6},{8,9},{9,8},{10,11... | collective-permute-start | bytes 9535496 | tf_op jit(solution)/shard_map/ppermute | solution.py:52
  115.3 1.2 copy-start.3
  116.5 8.0 %copy-start.5 = (f32[2048,128]{1,0:T(8,128)S(1)}, f32[2048,128]{1,0:T(8,128)}, u32[]{:S(2)}) copy-start(f32[2048,128]{1,0:T(8,128)} %copy-done.4) | copy-start | bytes 3145732
  116.5 10.0 %copy-start.7 = (f32[6208,128]{1,0:T(8,128)S(1)}, f32[6208,128]{1,0:T(8,128)}, u32[]{:S(2)}) copy-start(f32[6208,128]{1,0:T(8,128)} %all-gather.2.cloned.1.call-done.refs_0_) | copy-start | bytes 9535492
  126.5 4.7 %copy-start.6 = (s32[4,4]{1,0:T(4,128)S(1)}, s32[4,4]{1,0:T(4,128)}, u32[]{:S(2)}) copy-start(s32[4,4]{1,0:T(4,128)} %refs_0_.1) | copy-start | bytes 196
Sparse Core Ops, SparseCore 0:
  9.9 93.6 all-gather.1

commit v5 on v4

--- a/solution.py
+++ b/solution.py
@@ -102,34 +102,29 @@
 
 
 def prepare_right(along_first, *refs):
-    pieces, outs = refs[:5], refs[5:]
-    wide = outs[0].shape[1] // BS
+    *pieces, high_out, low_out = refs
     row, core = lax.axis_index("row"), lax.axis_index("col") % 2
     x, y = (row // 4) % 4, row % 4
     for step in range(4):
         for t in range(4):
-            ref, at = (pieces[step], t) if step < 3 else (pieces[3 + t // 2], t % 2)
+            whole = step < 3 or len(pieces) == 4
+            ref, at = (pieces[step], t) if whole else (pieces[3 + t // 2], t % 2)
             across, along = (NEAR[t], NEAR[step]) if along_first == "x" else (NEAR[step], NEAR[t])
             from_x, from_y = (x + across + 4) % 4, (y + along + 4) % 4
-            foreign = from_y // 2 != core
-            start = pl.multiple_of(from_x * 2 * BS + from_y % 2 * BS, BS)
-            for other in range(2):
-
-                @pl.when(foreign if other else jnp.logical_not(foreign))
-                def _():
-                    for j in range(wide):
-                        high, low = split(ref[(wide * at + j) * BS:(wide * at + j + 1) * BS, :])
-                        outs[2 * other][pl.ds(start, BS), j * BS:(j + 1) * BS] = high
-                        outs[2 * other + 1][pl.ds(start, BS), j * BS:(j + 1) * BS] = low
-
-
-def multiply(last, *refs):
-    if last:
-        c_filter, before, panel, *rights = refs[:7]
-        out, places, copied, left_high, left_low = refs[7:]
-    else:
-        panel, *rights = refs[:5]
-        out, places, copied, left_high, left_low = refs[5:]
+            foreign = (from_y // 2 != core).astype(jnp.int32)
+            start = pl.multiple_of(foreign * HALF_ROWS + from_x * 2 * BS + from_y % 2 * BS, BS)
+            for j in range(4):
+                high, low = split(ref[(4 * at + j) * BS:(4 * at + j + 1) * BS, :])
+                high_out[pl.ds(start, BS), j * BS:(j + 1) * BS] = high
+                low_out[pl.ds(start, BS), j * BS:(j + 1) * BS] = low
+
+
+def multiply(families, first, last, *refs):
+    refs = list(refs)
+    c_filter = refs.pop(0) if last else None
+    before = None if first else refs.pop(0)
+    panel, *rights = refs[:-5]
+    out, places, copied, left_high, left_low = refs[-5:]
     zh = lax.axis_index("row") // 16
     placing = [
         pltpu.make_async_copy(panel.at[pl.ds(zl * PAY_ROWS + SLOT_ROWS, 8)], places.at[zl], copied.at[zl])
@@ -139,8 +134,8 @@
         copy.start()
     for copy in placing:
         copy.wait()
-    for n in range(8):
-        zl = (zh if n < 4 else 1 - zh) * 4 + n % 4
+    for n in range(4 * len(families)):
+        zl = (1 - zh if families[n // 4] else zh) * 4 + n % 4
         for i in range(4):
             for k in range(2):
                 slot = places[zl, 2 * i + k, 0].astype(jnp.int32)
@@ -149,10 +144,11 @@
                 left_high[i * BS:(i + 1) * BS, (2 * n + k) * BS:(2 * n + k + 1) * BS] = high
                 left_low[i * BS:(i + 1) * BS, (2 * n + k) * BS:(2 * n + k + 1) * BS] = low
     dot = functools.partial(jnp.dot, preferred_element_type=jnp.float32)
-    total = before[...] if last else None
-    for family in range(2):
+    total = None if first else before[...]
+    for family in range(len(families)):
         wide = slice(HALF_ROWS * family, HALF_ROWS * (family + 1))
-        right_high, right_low = rights[2 * family][...], rights[2 * family + 1][...]
+        deep = slice(HALF_ROWS, 2 * HALF_ROWS) if last else slice(0, HALF_ROWS)
+        right_high, right_low = rights[2 * family][deep, :], rights[2 * family + 1][deep, :]
         part = dot(left_high[:, wide], right_high) + dot(left_high[:, wide], right_low)
         part = part + dot(left_low[:, wide], right_high)
         total = part if total is None else total + part
@@ -165,35 +161,34 @@
             out[i, j] = jnp.where(c_filter[i, j] > 0, value, 0.0)
 
 
-def add_products(panel, rights, before=None, c_filter=None, flops=1 << 30):
-    last = c_filter is not None
+def add_products(families, panel, rights, before=None, c_filter=None, flops=1 << 30):
+    last, first = c_filter is not None, before is None
     return pl.pallas_call(
-        functools.partial(multiply, last),
+        functools.partial(multiply, families, first, last),
         out_shape=jax.ShapeDtypeStruct((4, 4, BS, BS) if last else (4 * BS, 4 * BS), jnp.float32),
-        in_specs=([SMEM, VMEM] if last else []) + [VMEM] * 5,
+        in_specs=([SMEM] if last else []) + ([] if first else [VMEM]) + [VMEM] * (1 + len(rights)),
         out_specs=VMEM,
         scratch_shapes=[
             pltpu.SMEM((NZL, 8, BS), jnp.float32),
             pltpu.SemaphoreType.DMA((NZL,)),
-            pltpu.VMEM((4 * BS, 16 * BS), jnp.bfloat16),
-            pltpu.VMEM((4 * BS, 16 * BS), jnp.bfloat16),
+            pltpu.VMEM((4 * BS, 8 * len(families) * BS), jnp.bfloat16),
+            pltpu.VMEM((4 * BS, 8 * len(families) * BS), jnp.bfloat16),
         ],
         compiler_params=pltpu.CompilerParams(vmem_limit_bytes=24 << 20),
         cost_estimate=pl.CostEstimate(flops=flops, bytes_accessed=4 << 20, transcendentals=0),
-    )(*((c_filter, before) if last else ()), panel, *rights)
+    )(*((c_filter,) if last else ()), *(() if first else (before,)), panel, *rights)
 
 
 VMEM = pl.BlockSpec(memory_space=pltpu.VMEM)
 SMEM = pl.BlockSpec(memory_space=pltpu.SMEM)
-ANY = pl.BlockSpec(memory_space=pl.ANY)
 
 
 def prepare(pieces, along_first):
     return pl.pallas_call(
         functools.partial(prepare_right, along_first),
-        out_shape=[jax.ShapeDtypeStruct((HALF_ROWS, 4 * BS), jnp.bfloat16)] * 4,
-        in_specs=[VMEM] * 5,
-        out_specs=[VMEM] * 4,
+        out_shape=[jax.ShapeDtypeStruct((2 * HALF_ROWS, 4 * BS), jnp.bfloat16)] * 2,
+        in_specs=[VMEM] * len(pieces),
+        out_specs=[VMEM] * 2,
         compiler_params=pltpu.CompilerParams(vmem_limit_bytes=24 << 20),
     )(*pieces)
 
@@ -219,13 +214,13 @@
     second = [partner, *near(partner, along_y)]
     first = jnp.concatenate(first)
     second = jnp.concatenate(lax.optimization_barrier(tuple(second)))
-    first = [first, *gather_far(first, along_y)]
+    first = [first, *near(first, along_y)]
     second = [second, *gather_far(second, along_x)]
     own, second[1], second[2] = lax.optimization_barrier((own, second[1], second[2]))
     other = send(own, other_core())
     near_by, far_off = prepare(first, "x"), prepare(second, "y")
-    part = add_products(own, (*near_by[:2], *far_off[:2]), flops=30 << 30)
-    return add_products(other, (*near_by[2:], *far_off[2:]), before=part, c_filter=c_filter)
+    part = add_products((0, 1), own, (*near_by, *far_off), flops=30 << 30)
+    return add_products((0, 1), other, (*near_by, *far_off), before=part, c_filter=c_filter)
 
 
 def solution(mesh):

time: 145 us -> 156 us (1.076)
  the two profiles are of different devices: /device:TPU:192 before, /device:TPU:39 now
where the time goes in v5:
time: 156 us
  starting transfers between devices  64 us (41%)
  waiting for transfers between devices  52.4 us (34%)
  Pallas kernels  19.5 us (12%)
  between operations  13.7 us (9%)
  local copies, waits for them, and re-layouts  6.12 us (4%)
    ppermute x15, starting transfers between devices, send(): return lax.ppermute(value, AXES, pairs)  64 us
    ppermute x15, waiting for transfers between devices, send(): return lax.ppermute(value, AXES, pairs)  43.9 us
    pallas_call x2, Pallas kernels, add_products(): pl.pallas_call(functools.partial(multiply, families, first, last), out_sh...  10.9 us
    all_gather x1, waiting for transfers between devices, on_device(): own = lax.all_gather(left, 'col', axis_index_groups=same_core, tiled=True)  8.47 us
    pallas_call x2, Pallas kernels, prepare(): pl.pallas_call(functools.partial(prepare_right, along_first), out_shape=[...  4.93 us
    unnamed x13, local copies, waits for them, and re-layouts  3.68 us
  transfers between devices with their start and end apart: 16, of which 7 were waited for; matrix products, arithmetic and copies ran while one was open for 3% of the time, Pallas kernels for 7%

profile of v5, /device:TPU:39, one launch (start us, length us, event | category | flops | bytes accessed | tf_op | source)
XLA Modules:
  0.0 155.7 jit_solution(9146072698250166643)
XLA Ops:
  6.5 0.0 all-gather.2.cloned.1.call-start
  6.5 1.3 copy.9.occupied
  7.9 2.0 %shard_map.82 = f32[776,128]{1,0:T(8,128)} custom-call(f32[4,2,128,128]{3,2,1,0:T(8,128)} %blocks.2, s32[4,2]{1,0:T(4,128)} %copy.9.occupied, s32[4]{0:T(128)} %row_sizes.1, s32[32]{0:T(128)} %k_sizes.3), custom_call_target="tpu_custom_call" | custom-call | tf_op jit(solution)/shard_map/pallas_call | solution.py:205
  9.8 0.0 all-gather.2.cloned.1.call-update
  9.8 1.7 %shard_map.83 = f32[512,128]{1,0:T(8,128)} custom-call(f32[1,4,128,128]{3,2,1,0:T(8,128)} %blocks.3, s32[1,4]{1,0:T(1,128)} %occupied.2, s32[32]{0:T(128)} %k_sizes.3, s32[4]{0:T(128)} %col_sizes.1), custom_call_target="tpu_custom_call" | custom-call | tf_op jit(solution)/shard_map/pallas_call | solution.py:197
  11.6 14.6 %collective-permute-start.3 = (f32[512,128]{1,0:T(8,128)}, f32[512,128]{1,0:T(8,128)S(1)}, u32[]{:S(2)}, u32[]{:S(2)}) collective-permute-start(f32[512,128]{1,0:T(8,128)} %shard_map.83), channel_id=1, source_target_pairs={{0,256},{1,257},{2,258},{3,259},{4,260},{5,261},{6,262},{7,263},{8... | collective-permute-start | bytes 786440 | tf_op jit(solution)/shard_map/ppermute | solution.py:52
  26.2 3.0 %collective-permute-start.2 = (f32[512,128]{1,0:T(8,128)}, f32[512,128]{1,0:T(8,128)S(1)}, u32[]{:S(2)}, u32[]{:S(2)}) collective-permute-start(f32[512,128]{1,0:T(8,128)} %shard_map.83), channel_id=1, source_target_pairs={{0,128},{1,129},{2,130},{3,131},{4,132},{5,133},{6,134},{7,135},{8... | collective-permute-start | bytes 786440 | tf_op jit(solution)/shard_map/ppermute | solution.py:52
  29.2 1.9 %collective-permute-start.1 = (f32[512,128]{1,0:T(8,128)}, f32[512,128]{1,0:T(8,128)S(1)}, u32[]{:S(2)}, u32[]{:S(2)}) collective-permute-start(f32[512,128]{1,0:T(8,128)} %shard_map.83), channel_id=1, source_target_pairs={{0,192},{1,193},{2,194},{3,195},{4,196},{5,197},{6,198},{7,199},{8... | collective-permute-start | bytes 786440 | tf_op jit(solution)/shard_map/ppermute | solution.py:52
  31.2 4.6 %collective-permute-start = (f32[512,128]{1,0:T(8,128)}, f32[512,128]{1,0:T(8,128)S(1)}, u32[]{:S(2)}, u32[]{:S(2)}) collective-permute-start(f32[512,128]{1,0:T(8,128)} %shard_map.83), channel_id=1, source_target_pairs={{0,64},{1,65},{2,66},{3,67},{4,68},{5,69},{6,70},{7,71},{8,72},{9,... | collective-permute-start | bytes 786440 | tf_op jit(solution)/shard_map/ppermute | solution.py:52
  35.8 17.3 %collective-permute-done.3 = f32[512,128]{1,0:T(8,128)S(1)} collective-permute-done((f32[512,128]{1,0:T(8,128)}, f32[512,128]{1,0:T(8,128)S(1)}, u32[]{:S(2)}, u32[]{:S(2)}) %collective-permute-start.3) | collective-permute-done | bytes 262176 | tf_op jit(solution)/shard_map/ppermute | solution.py:52
  53.1 0.0 collective-permute-done.2
  53.1 0.0 collective-permute-done.1
  53.1 0.0 collective-permute-done
  53.1 5.0 %collective-permute-start.6 = (f32[512,128]{1,0:T(8,128)S(1)}, f32[512,128]{1,0:T(8,128)S(1)}, u32[]{:S(2)}, u32[]{:S(2)}) collective-permute-start(f32[512,128]{1,0:T(8,128)S(1)} %collective-permute-done.3), channel_id=1, source_target_pairs={{0,32},{1,33},{2,34},{3,35},{4,36},{5,37},{6,38},{7,39},{8,40},{9,... | collective-permute-start | bytes 786440 | tf_op jit(solution)/shard_map/ppermute | solution.py:52
  58.1 2.8 %collective-permute-start.5 = (f32[512,128]{1,0:T(8,128)S(1)}, f32[512,128]{1,0:T(8,128)S(1)}, u32[]{:S(2)}, u32[]{:S(2)}) collective-permute-start(f32[512,128]{1,0:T(8,128)S(1)} %collective-permute-done.3), channel_id=1, source_target_pairs={{0,48},{1,49},{2,50},{3,51},{4,52},{5,53},{6,54},{7,55},{8,56},{9,... | collective-permute-start | bytes 786440 | tf_op jit(solution)/shard_map/ppermute | solution.py:52
  60.9 2.5 %collective-permute-start.4 = (f32[512,128]{1,0:T(8,128)S(1)}, f32[512,128]{1,0:T(8,128)S(1)}, u32[]{:S(2)}, u32[]{:S(2)}) collective-permute-start(f32[512,128]{1,0:T(8,128)S(1)} %collective-permute-done.3), channel_id=1, source_target_pairs={{0,16},{1,17},{2,18},{3,19},{4,20},{5,21},{6,22},{7,23},{8,24},{9,... | collective-permute-start | bytes 786440 | tf_op jit(solution)/shard_map/ppermute | solution.py:52
  63.4 0.0 collective-permute-done.6
  63.4 2.2 %collective-permute-done.5 = f32[512,128]{1,0:T(8,128)S(1)} collective-permute-done((f32[512,128]{1,0:T(8,128)S(1)}, f32[512,128]{1,0:T(8,128)S(1)}, u32[]{:S(2)}, u32[]{:S(2)}) %collective-permute-start.5) | collective-permute-done | bytes 262176 | tf_op jit(solution)/shard_map/ppermute | solution.py:52
  65.6 6.4 %collective-permute-done.4 = f32[512,128]{1,0:T(8,128)S(1)} collective-permute-done((f32[512,128]{1,0:T(8,128)S(1)}, f32[512,128]{1,0:T(8,128)S(1)}, u32[]{:S(2)}, u32[]{:S(2)}) %collective-permute-start.4) | collective-permute-done | bytes 262176 | tf_op jit(solution)/shard_map/ppermute | solution.py:52
  72.1 2.4 %collective-permute-start.8 = (f32[2048,128]{1,0:T(8,128)S(1)}, f32[2048,128]{1,0:T(8,128)S(1)}, u32[]{:S(2)}, u32[]{:S(2)}) collective-permute-start(f32[2048,128]{1,0:T(8,128)S(1)} %constant_dynamic-update-slice_fusion.refs_0_), channel_id=1, source_target_pairs={{0,192},{1,193},{2,194},{3,195},{4,196},{5,197},{6,198},{7,199},{8... | collective-permute-start | bytes 3145736 | tf_op jit(solution)/shard_map/ppermute | solution.py:52
  74.5 4.1 %collective-permute-start.7 = (f32[2048,128]{1,0:T(8,128)S(1)}, f32[2048,128]{1,0:T(8,128)S(1)}, u32[]{:S(2)}, u32[]{:S(2)}) collective-permute-start(f32[2048,128]{1,0:T(8,128)S(1)} %constant_dynamic-update-slice_fusion.refs_0_), channel_id=1, source_target_pairs={{0,64},{1,65},{2,66},{3,67},{4,68},{5,69},{6,70},{7,71},{8,72},{9,... | collective-permute-start | bytes 3145736 | tf_op jit(solution)/shard_map/ppermute | solution.py:52
  78.7 0.0 copy-done.2
  78.7 0.7 constant_dynamic-update-slice_fusion.7
  79.4 0.7 constant_dynamic-update-slice_fusion.6
  80.1 0.7 constant_dynamic-update-slice_fusion.5
  80.8 0.7 constant_dynamic-update-slice_fusion.4.refs_0_
  81.5 1.9 %collective-permute-start.11 = (f32[2048,128]{1,0:T(8,128)}, f32[2048,128]{1,0:T(8,128)}, u32[]{:S(2)}, u32[]{:S(2)}) collective-permute-start(f32[2048,128]{1,0:T(8,128)} %constant_dynamic-update-slice_fusion.4.refs_0_), channel_id=1, source_target_pairs={{0,32},{1,33},{2,34},{3,35},{4,36},{5,37},{6,38},{7,39},{8,40},{9,... | collective-permute-start | bytes 3145736 | tf_op jit(solution)/shard_map/ppermute | solution.py:52
  83.5 1.9 %collective-permute-start.10 = (f32[2048,128]{1,0:T(8,128)}, f32[2048,128]{1,0:T(8,128)}, u32[]{:S(2)}, u32[]{:S(2)}) collective-permute-start(f32[2048,128]{1,0:T(8,128)} %constant_dynamic-update-slice_fusion.4.refs_0_), channel_id=1, source_target_pairs={{0,48},{1,49},{2,50},{3,51},{4,52},{5,53},{6,54},{7,55},{8,56},{9,... | collective-permute-start | bytes 3145736 | tf_op jit(solution)/shard_map/ppermute | solution.py:52
  85.4 3.4 %collective-permute-start.9 = (f32[2048,128]{1,0:T(8,128)}, f32[2048,128]{1,0:T(8,128)}, u32[]{:S(2)}, u32[]{:S(2)}) collective-permute-start(f32[2048,128]{1,0:T(8,128)} %constant_dynamic-update-slice_fusion.4.refs_0_), channel_id=1, source_target_pairs={{0,16},{1,17},{2,18},{3,19},{4,20},{5,21},{6,22},{7,23},{8,24},{9,... | collective-permute-start | bytes 3145736 | tf_op jit(solution)/shard_map/ppermute | solution.py:52
  88.8 5.0 %collective-permute-done.8.refs_2_ = f32[2048,128]{1,0:T(8,128)S(1)} collective-permute-done((f32[2048,128]{1,0:T(8,128)S(1)}, f32[2048,128]{1,0:T(8,128)S(1)}, u32[]{:S(2)}, u32[]{:S(2)}) %collective-permute-start.8) | collective-permute-done | bytes 1048608 | tf_op jit(solution)/shard_map/ppermute | solution.py:52
  93.8 0.8 slice.9
  94.6 1.9 %collective-permute-start.13 = (f32[1024,128]{1,0:T(8,128)}, f32[1024,128]{1,0:T(8,128)}, u32[]{:S(2)}, u32[]{:S(2)}) collective-permute-start(f32[1024,128]{1,0:T(8,128)} %slice.9), channel_id=1, source_target_pairs={{0,192},{1,193},{2,194},{3,195},{4,196},{5,197},{6,198},{7,199},{8... | collective-permute-start | bytes 1572872 | tf_op jit(solution)/shard_map/ppermute | solution.py:52
  96.5 0.0 collective-permute-done.7.refs_1_
  96.6 0.9 slice.8
  97.4 4.6 %collective-permute-start.12 = (f32[1024,128]{1,0:T(8,128)}, f32[1024,128]{1,0:T(8,128)}, u32[]{:S(2)}, u32[]{:S(2)}) collective-permute-start(f32[1024,128]{1,0:T(8,128)} %slice.8), channel_id=1, source_target_pairs={{0,64},{1,65},{2,66},{3,67},{4,68},{5,69},{6,70},{7,71},{8,72},{9,... | collective-permute-start | bytes 1572872 | tf_op jit(solution)/shard_map/ppermute | solution.py:52
  102.0 8.5 %all-gather.2.cloned.1.call-done.refs_0_ = f32[6208,128]{1,0:T(8,128)} async-done(((f32[776,128]{1,0:T(8,128)}), f32[6208,128]{1,0:T(8,128)}) %all-gather.2.cloned.1.call-update) | async-done | bytes 3178512 | tf_op jit(solution)/shard_map/all_gather | solution.py:212
  110.5 0.0 collective-permute-done.11.refs_3_
  110.5 9.4 %collective-permute-start.14 = (f32[6208,128]{1,0:T(8,128)}, f32[6208,128]{1,0:T(8,128)S(1)}, u32[]{:S(2)}, u32[]{:S(2)}) collective-permute-start(f32[6208,128]{1,0:T(8,128)} %all-gather.2.cloned.1.call-done.refs_0_), channel_id=1, source_target_pairs={{0,1},{1,0},{2,3},{3,2},{4,5},{5,4},{6,7},{7,6},{8,9},{9,8},{10,11... | collective-permute-start | bytes 9535496 | tf_op jit(solution)/shard_map/ppermute | solution.py:52
  119.9 9.0 %collective-permute-done.10.refs_2_ = f32[2048,128]{1,0:T(8,128)} collective-permute-done((f32[2048,128]{1,0:T(8,128)}, f32[2048,128]{1,0:T(8,128)}, u32[]{:S(2)}, u32[]{:S(2)}) %collective-permute-start.10) | collective-permute-done | bytes 1048608 | tf_op jit(solution)/shard_map/ppermute | solution.py:52
  128.9 3.9 %collective-permute-done.9.refs_1_ = f32[2048,128]{1,0:T(8,128)} collective-permute-done((f32[2048,128]{1,0:T(8,128)}, f32[2048,128]{1,0:T(8,128)}, u32[]{:S(2)}, u32[]{:S(2)}) %collective-permute-start.9) | collective-permute-done | bytes 1048608 | tf_op jit(solution)/shard_map/ppermute | solution.py:52
  132.8 2.9 %shard_map.84 = (bf16[2048,512]{1,0:T(8,128)(2,1)S(1)}, bf16[2048,512]{1,0:T(8,128)(2,1)S(1)}) custom-call(f32[2048,128]{1,0:T(8,128)} %constant_dynamic-update-slice_fusion.4.refs_0_, f32[2048,128]{1,0:T(8,128)} %collective-permute-done.9.refs_1_, f32[2048,128]{1,0:T(8,128)} %collective-permute-done.10.refs_2_, f32[2048,128]{1,0:T(8,128)} %collective-permute-done.11.refs_3_), custom_call_target="tpu_custom_call" | custom-call | tf_op jit(solution)/shard_map/pallas_call | solution.py:187
  135.7 0.0 collective-permute-done.13.refs_4_
  135.7 0.0 collective-permute-done.12.refs_3_
  135.7 2.1 %shard_map.85 = (bf16[2048,512]{1,0:T(8,128)(2,1)S(1)}, bf16[2048,512]{1,0:T(8,128)(2,1)S(1)}) custom-call(f32[2048,128]{1,0:T(8,128)S(1)} %constant_dynamic-update-slice_fusion.refs_0_, f32[2048,128]{1,0:T(8,128)S(1)} %collective-permute-done.7.refs_1_, f32[2048,128]{1,0:T(8,128)S(1)} %collective-permute-done.8.refs_2_, ...), custom_call_target="tpu_custom_call" | custom-call | tf_op jit(solution)/shard_map/pallas_call | solution.py:187
  137.8 0.1 copy-done.1
  137.9 4.7 %shard_map.86.refs_1_ = f32[512,512]{1,0:T(8,128)S(1)} custom-call(f32[6208,128]{1,0:T(8,128)S(1)} %copy-done.1, bf16[2048,512]{1,0:T(8,128)(2,1)S(1)} %get-tuple-element.31.refs_1_.refs_3_, bf16[2048,512]{1,0:T(8,128)(2,1)S(1)} %get-tuple-element.32.refs_2_.refs_4_, bf16[2048,512]{1,0:T(8,128)(2,1)S(1)} %get-tuple-element.35.refs_3_.refs_5_, ...), custom_call_target="tpu_custom_call" | custom-call | flops 32212254720 | bytes 4194304 | tf_op jit(solution)/shard_map/pallas_call | solution.py:166
  142.6 0.0 collective-permute-done.14.refs_2_
  142.6 6.2 %shard_map.87 = f32[4,4,128,128]{3,2,1,0:T(8,128)} custom-call(s32[4,4]{1,0:T(4,128)S(1)} %copy-done, f32[512,512]{1,0:T(8,128)S(1)} %shard_map.86.refs_1_, f32[6208,128]{1,0:T(8,128)S(1)} %collective-permute-done.14.refs_2_, bf16[2048,512]{1,0:T(8,128)(2,1)S(1)} %get-tuple-element.31.refs_1_.refs_3_, ...), custom_call_target="tpu_custom_call" | custom-call | flops 1073741824 | bytes 4194304 | tf_op jit(solution)/shard_map/pallas_call | solution.py:166
  (8 shorter events, 0.1 us)
Async XLA Ops:
  6.5 103.9 %all-gather.2.cloned.1.call-start = ((), (), s32[]{:S(2)}) async-start(), calls=%async_computation | async-start | bytes 3575808 | tf_op jit(solution)/shard_map/all_gather | solution.py:212
  11.6 67.1 %copy-start.2 = (f32[512,128]{1,0:T(8,128)S(1)}, f32[512,128]{1,0:T(8,128)}, u32[]{:S(2)}) copy-start(f32[512,128]{1,0:T(8,128)} %shard_map.83) | copy-start | bytes 786436
  11.6 41.5 %collective-permute-start.3 = (f32[512,128]{1,0:T(8,128)}, f32[512,128]{1,0:T(8,128)S(1)}, u32[]{:S(2)}, u32[]{:S(2)}) collective-permute-start(f32[512,128]{1,0:T(8,128)} %shard_map.83), channel_id=1, source_target_pairs={{0,256},{1,257},{2,258},{3,259},{4,260},{5,261},{6,262},{7,263},{8... | collective-permute-start | bytes 786440 | tf_op jit(solution)/shard_map/ppermute | solution.py:52
  26.2 26.9 %collective-permute-start.2 = (f32[512,128]{1,0:T(8,128)}, f32[512,128]{1,0:T(8,128)S(1)}, u32[]{:S(2)}, u32[]{:S(2)}) collective-permute-start(f32[512,128]{1,0:T(8,128)} %shard_map.83), channel_id=1, source_target_pairs={{0,128},{1,129},{2,130},{3,131},{4,132},{5,133},{6,134},{7,135},{8... | collective-permute-start | bytes 786440 | tf_op jit(solution)/shard_map/ppermute | solution.py:52
  29.2 23.8 %collective-permute-start.1 = (f32[512,128]{1,0:T(8,128)}, f32[512,128]{1,0:T(8,128)S(1)}, u32[]{:S(2)}, u32[]{:S(2)}) collective-permute-start(f32[512,128]{1,0:T(8,128)} %shard_map.83), channel_id=1, source_target_pairs={{0,192},{1,193},{2,194},{3,195},{4,196},{5,197},{6,198},{7,199},{8... | collective-permute-start | bytes 786440 | tf_op jit(solution)/shard_map/ppermute | solution.py:52
  31.2 21.9 %collective-permute-start = (f32[512,128]{1,0:T(8,128)}, f32[512,128]{1,0:T(8,128)S(1)}, u32[]{:S(2)}, u32[]{:S(2)}) collective-permute-start(f32[512,128]{1,0:T(8,128)} %shard_map.83), channel_id=1, source_target_pairs={{0,64},{1,65},{2,66},{3,67},{4,68},{5,69},{6,70},{7,71},{8,72},{9,... | collective-permute-start | bytes 786440 | tf_op jit(solution)/shard_map/ppermute | solution.py:52
  53.1 10.3 %collective-permute-start.6 = (f32[512,128]{1,0:T(8,128)S(1)}, f32[512,128]{1,0:T(8,128)S(1)}, u32[]{:S(2)}, u32[]{:S(2)}) collective-permute-start(f32[512,128]{1,0:T(8,128)S(1)} %collective-permute-done.3), channel_id=1, source_target_pairs={{0,32},{1,33},{2,34},{3,35},{4,36},{5,37},{6,38},{7,39},{8,40},{9,... | collective-permute-start | bytes 786440 | tf_op jit(solution)/shard_map/ppermute | solution.py:52
  58.1 7.5 %collective-permute-start.5 = (f32[512,128]{1,0:T(8,128)S(1)}, f32[512,128]{1,0:T(8,128)S(1)}, u32[]{:S(2)}, u32[]{:S(2)}) collective-permute-start(f32[512,128]{1,0:T(8,128)S(1)} %collective-permute-done.3), channel_id=1, source_target_pairs={{0,48},{1,49},{2,50},{3,51},{4,52},{5,53},{6,54},{7,55},{8,56},{9,... | collective-permute-start | bytes 786440 | tf_op jit(solution)/shard_map/ppermute | solution.py:52
  60.9 11.1 %collective-permute-start.4 = (f32[512,128]{1,0:T(8,128)S(1)}, f32[512,128]{1,0:T(8,128)S(1)}, u32[]{:S(2)}, u32[]{:S(2)}) collective-permute-start(f32[512,128]{1,0:T(8,128)S(1)} %collective-permute-done.3), channel_id=1, source_target_pairs={{0,16},{1,17},{2,18},{3,19},{4,20},{5,21},{6,22},{7,23},{8,24},{9,... | collective-permute-start | bytes 786440 | tf_op jit(solution)/shard_map/ppermute | solution.py:52
  72.1 21.7 %collective-permute-start.8 = (f32[2048,128]{1,0:T(8,128)S(1)}, f32[2048,128]{1,0:T(8,128)S(1)}, u32[]{:S(2)}, u32[]{:S(2)}) collective-permute-start(f32[2048,128]{1,0:T(8,128)S(1)} %constant_dynamic-update-slice_fusion.refs_0_), channel_id=1, source_target_pairs={{0,192},{1,193},{2,194},{3,195},{4,196},{5,197},{6,198},{7,199},{8... | collective-permute-start | bytes 3145736 | tf_op jit(solution)/shard_map/ppermute | solution.py:52
  74.5 22.0 %collective-permute-start.7 = (f32[2048,128]{1,0:T(8,128)S(1)}, f32[2048,128]{1,0:T(8,128)S(1)}, u32[]{:S(2)}, u32[]{:S(2)}) collective-permute-start(f32[2048,128]{1,0:T(8,128)S(1)} %constant_dynamic-update-slice_fusion.refs_0_), channel_id=1, source_target_pairs={{0,64},{1,65},{2,66},{3,67},{4,68},{5,69},{6,70},{7,71},{8,72},{9,... | collective-permute-start | bytes 3145736 | tf_op jit(solution)/shard_map/ppermute | solution.py:52
  81.5 28.9 %collective-permute-start.11 = (f32[2048,128]{1,0:T(8,128)}, f32[2048,128]{1,0:T(8,128)}, u32[]{:S(2)}, u32[]{:S(2)}) collective-permute-start(f32[2048,128]{1,0:T(8,128)} %constant_dynamic-update-slice_fusion.4.refs_0_), channel_id=1, source_target_pairs={{0,32},{1,33},{2,34},{3,35},{4,36},{5,37},{6,38},{7,39},{8,40},{9,... | collective-permute-start | bytes 3145736 | tf_op jit(solution)/shard_map/ppermute | solution.py:52
  83.5 45.5 %collective-permute-start.10 = (f32[2048,128]{1,0:T(8,128)}, f32[2048,128]{1,0:T(8,128)}, u32[]{:S(2)}, u32[]{:S(2)}) collective-permute-start(f32[2048,128]{1,0:T(8,128)} %constant_dynamic-update-slice_fusion.4.refs_0_), channel_id=1, source_target_pairs={{0,48},{1,49},{2,50},{3,51},{4,52},{5,53},{6,54},{7,55},{8,56},{9,... | collective-permute-start | bytes 3145736 | tf_op jit(solution)/shard_map/ppermute | solution.py:52
  85.4 47.4 %collective-permute-start.9 = (f32[2048,128]{1,0:T(8,128)}, f32[2048,128]{1,0:T(8,128)}, u32[]{:S(2)}, u32[]{:S(2)}) collective-permute-start(f32[2048,128]{1,0:T(8,128)} %constant_dynamic-update-slice_fusion.4.refs_0_), channel_id=1, source_target_pairs={{0,16},{1,17},{2,18},{3,19},{4,20},{5,21},{6,22},{7,23},{8,24},{9,... | collective-permute-start | bytes 3145736 | tf_op jit(solution)/shard_map/ppermute | solution.py:52
  94.6 41.1 %collective-permute-start.13 = (f32[1024,128]{1,0:T(8,128)}, f32[1024,128]{1,0:T(8,128)}, u32[]{:S(2)}, u32[]{:S(2)}) collective-permute-start(f32[1024,128]{1,0:T(8,128)} %slice.9), channel_id=1, source_target_pairs={{0,192},{1,193},{2,194},{3,195},{4,196},{5,197},{6,198},{7,199},{8... | collective-permute-start | bytes 1572872 | tf_op jit(solution)/shard_map/ppermute | solution.py:52
  97.4 38.3 %collective-permute-start.12 = (f32[1024,128]{1,0:T(8,128)}, f32[1024,128]{1,0:T(8,128)}, u32[]{:S(2)}, u32[]{:S(2)}) collective-permute-start(f32[1024,128]{1,0:T(8,128)} %slice.8), channel_id=1, source_target_pairs={{0,64},{1,65},{2,66},{3,67},{4,68},{5,69},{6,70},{7,71},{8,72},{9,... | collective-permute-start | bytes 1572872 | tf_op jit(solution)/shard_map/ppermute | solution.py:52
  110.5 32.1 %collective-permute-start.14 = (f32[6208,128]{1,0:T(8,128)}, f32[6208,128]{1,0:T(8,128)S(1)}, u32[]{:S(2)}, u32[]{:S(2)}) collective-permute-start(f32[6208,128]{1,0:T(8,128)} %all-gather.2.cloned.1.call-done.refs_0_), channel_id=1, source_target_pairs={{0,1},{1,0},{2,3},{3,2},{4,5},{5,4},{6,7},{7,6},{8,9},{9,8},{10,11... | collective-permute-start | bytes 9535496 | tf_op jit(solution)/shard_map/ppermute | solution.py:52
  135.7 2.2 %copy-start.1 = (f32[6208,128]{1,0:T(8,128)S(1)}, f32[6208,128]{1,0:T(8,128)}, u32[]{:S(2)}) copy-start(f32[6208,128]{1,0:T(8,128)} %all-gather.2.cloned.1.call-done.refs_0_) | copy-start | bytes 9535492
  137.9 4.7 %copy-start = (s32[4,4]{1,0:T(4,128)S(1)}, s32[4,4]{1,0:T(4,128)}, u32[]{:S(2)}) copy-start(s32[4,4]{1,0:T(4,128)} %refs_0_.1) | copy-start | bytes 196
Sparse Core Ops, SparseCore 0:
  10.0 100.4 all-gather.1

commit v6 on v4

--- a/solution.py
+++ b/solution.py
@@ -70,7 +70,7 @@
     slot = jnp.int32(0)
     for i in range(4):
         for k in range(2):
-            here = (occupied[i, k] > 0) & (slot < CAP)
+            here = (occupied[k, i] > 0) & (slot < CAP)
             place = slot
 
             @pl.when(here)
@@ -126,7 +126,7 @@
 def multiply(last, *refs):
     if last:
         c_filter, before, panel, *rights = refs[:7]
-        out, places, copied, left_high, left_low = refs[7:]
+        out, places, copied, left_high, left_low, ready, left = refs[7:]
     else:
         panel, *rights = refs[:5]
         out, places, copied, left_high, left_low = refs[5:]
@@ -159,10 +159,15 @@
     if not last:
         out[...] = total
         return
+    leaving = []
     for i in range(4):
         for j in range(4):
             value = total[i * BS:(i + 1) * BS, j * BS:(j + 1) * BS]
-            out[i, j] = jnp.where(c_filter[i, j] > 0, value, 0.0)
+            ready[i, j] = jnp.where(c_filter[i, j] > 0, value, 0.0)
+            leaving.append(pltpu.make_async_copy(ready.at[i, j], out.at[i, j], left.at[i, j]))
+            leaving[-1].start()
+    for copy in leaving:
+        copy.wait()
 
 
 def add_products(panel, rights, before=None, c_filter=None, flops=1 << 30):
@@ -171,13 +176,14 @@
         functools.partial(multiply, last),
         out_shape=jax.ShapeDtypeStruct((4, 4, BS, BS) if last else (4 * BS, 4 * BS), jnp.float32),
         in_specs=([SMEM, VMEM] if last else []) + [VMEM] * 5,
-        out_specs=VMEM,
+        out_specs=ANY if last else VMEM,
         scratch_shapes=[
             pltpu.SMEM((NZL, 8, BS), jnp.float32),
             pltpu.SemaphoreType.DMA((NZL,)),
             pltpu.VMEM((4 * BS, 16 * BS), jnp.bfloat16),
             pltpu.VMEM((4 * BS, 16 * BS), jnp.bfloat16),
-        ],
+        ]
+        + ([pltpu.VMEM((4, 4, BS, BS), jnp.float32), pltpu.SemaphoreType.DMA((4, 4))] if last else []),
         compiler_params=pltpu.CompilerParams(vmem_limit_bytes=24 << 20),
         cost_estimate=pl.CostEstimate(flops=flops, bytes_accessed=4 << 20, transcendentals=0),
     )(*((c_filter, before) if last else ()), panel, *rights)
@@ -212,7 +218,7 @@
         out_shape=jax.ShapeDtypeStruct((PAY_ROWS, BS), jnp.float32),
         in_specs=[VMEM, SMEM, SMEM, SMEM],
         out_specs=VMEM,
-    )(a_blocks, a_occupied, row_sizes, k_sizes)
+    )(a_blocks, a_occupied.T, row_sizes, k_sizes)
     same_core = [[zl * NC + core for zl in range(NZL)] for core in range(NC)]
     own = lax.all_gather(left, "col", axis_index_groups=same_core, tiled=True)
     *first, partner = lax.optimization_barrier((*first, partner))

time: 145 us -> 143 us (0.986)
    unnamed x23 -> x22, local copies, waits for them, and re-layouts: 4.66 us -> 3.33 us
where the time goes in v6:
time: 143 us
  starting transfers between devices  58.6 us (41%)
  waiting for transfers between devices  44.8 us (31%)
  Pallas kernels  18.7 us (13%)
  between operations  13.7 us (10%)
  local copies, waits for them, and re-layouts  6.85 us (5%)
    ppermute x16, starting transfers between devices, send(): return lax.ppermute(value, AXES, pairs)  58.6 us
    ppermute x16, waiting for transfers between devices, send(): return lax.ppermute(value, AXES, pairs)  44.7 us
    pallas_call x2, Pallas kernels, add_products(): pl.pallas_call(functools.partial(multiply, last), out_shape=jax.ShapeDtyp...  10.9 us
    pallas_call x2, Pallas kernels, prepare(): pl.pallas_call(functools.partial(prepare_right, along_first), out_shape=[...  4.16 us
    unnamed x22, local copies, waits for them, and re-layouts  3.33 us
  transfers between devices with their start and end apart: 17, of which 5 were waited for; matrix products, arithmetic and copies ran while one was open for 3% of the time, Pallas kernels for 7%

profile of v6, /device:TPU:192, one launch (start us, length us, event | category | flops | bytes accessed | tf_op | source)
XLA Modules:
  0.0 142.7 jit_solution(12913583203091806761)
XLA Ops:
  6.5 1.9 %shard_map.82 = f32[776,128]{1,0:T(8,128)} custom-call(f32[4,2,128,128]{3,2,1,0:T(8,128)} %blocks.2, s32[2,4]{1,0:T(2,128)} %bitcast.1, s32[4]{0:T(128)} %row_sizes.1, s32[32]{0:T(128)} %k_sizes.3), custom_call_target="tpu_custom_call" | custom-call | tf_op jit(solution)/shard_map/pallas_call | solution.py:216
  8.5 0.0 all-gather.2.cloned.1.call-update
  8.5 1.7 %shard_map.83 = f32[512,128]{1,0:T(8,128)} custom-call(f32[1,4,128,128]{3,2,1,0:T(8,128)} %blocks.3, s32[1,4]{1,0:T(1,128)} %occupied.1, s32[32]{0:T(128)} %k_sizes.3, s32[4]{0:T(128)} %col_sizes.1), custom_call_target="tpu_custom_call" | custom-call | tf_op jit(solution)/shard_map/pallas_call | solution.py:208
  10.2 9.1 %collective-permute-start.3 = (f32[512,128]{1,0:T(8,128)}, f32[512,128]{1,0:T(8,128)S(1)}, u32[]{:S(2)}, u32[]{:S(2)}) collective-permute-start(f32[512,128]{1,0:T(8,128)} %shard_map.83), channel_id=1, source_target_pairs={{0,256},{1,257},{2,258},{3,259},{4,260},{5,261},{6,262},{7,263},{8... | collective-permute-start | bytes 786440 | tf_op jit(solution)/shard_map/ppermute | solution.py:52
  19.3 4.9 %collective-permute-start.2 = (f32[512,128]{1,0:T(8,128)}, f32[512,128]{1,0:T(8,128)S(1)}, u32[]{:S(2)}, u32[]{:S(2)}) collective-permute-start(f32[512,128]{1,0:T(8,128)} %shard_map.83), channel_id=1, source_target_pairs={{0,128},{1,129},{2,130},{3,131},{4,132},{5,133},{6,134},{7,135},{8... | collective-permute-start | bytes 786440 | tf_op jit(solution)/shard_map/ppermute | solution.py:52
  24.2 3.0 %collective-permute-start.1 = (f32[512,128]{1,0:T(8,128)}, f32[512,128]{1,0:T(8,128)S(1)}, u32[]{:S(2)}, u32[]{:S(2)}) collective-permute-start(f32[512,128]{1,0:T(8,128)} %shard_map.83), channel_id=1, source_target_pairs={{0,192},{1,193},{2,194},{3,195},{4,196},{5,197},{6,198},{7,199},{8... | collective-permute-start | bytes 786440 | tf_op jit(solution)/shard_map/ppermute | solution.py:52
  27.3 2.8 %collective-permute-start = (f32[512,128]{1,0:T(8,128)}, f32[512,128]{1,0:T(8,128)S(1)}, u32[]{:S(2)}, u32[]{:S(2)}) collective-permute-start(f32[512,128]{1,0:T(8,128)} %shard_map.83), channel_id=1, source_target_pairs={{0,64},{1,65},{2,66},{3,67},{4,68},{5,69},{6,70},{7,71},{8,72},{9,... | collective-permute-start | bytes 786440 | tf_op jit(solution)/shard_map/ppermute | solution.py:52
  30.1 21.5 %collective-permute-done.3 = f32[512,128]{1,0:T(8,128)S(1)} collective-permute-done((f32[512,128]{1,0:T(8,128)}, f32[512,128]{1,0:T(8,128)S(1)}, u32[]{:S(2)}, u32[]{:S(2)}) %collective-permute-start.3) | collective-permute-done | bytes 262176 | tf_op jit(solution)/shard_map/ppermute | solution.py:52
  51.5 0.0 collective-permute-done.2
  51.5 0.0 collective-permute-done.1
  51.6 0.0 collective-permute-done
  51.6 5.1 %collective-permute-start.6 = (f32[512,128]{1,0:T(8,128)S(1)}, f32[512,128]{1,0:T(8,128)S(1)}, u32[]{:S(2)}, u32[]{:S(2)}) collective-permute-start(f32[512,128]{1,0:T(8,128)S(1)} %collective-permute-done.3), channel_id=1, source_target_pairs={{0,32},{1,33},{2,34},{3,35},{4,36},{5,37},{6,38},{7,39},{8,40},{9,... | collective-permute-start | bytes 786440 | tf_op jit(solution)/shard_map/ppermute | solution.py:52
  56.7 2.8 %collective-permute-start.5 = (f32[512,128]{1,0:T(8,128)S(1)}, f32[512,128]{1,0:T(8,128)S(1)}, u32[]{:S(2)}, u32[]{:S(2)}) collective-permute-start(f32[512,128]{1,0:T(8,128)S(1)} %collective-permute-done.3), channel_id=1, source_target_pairs={{0,48},{1,49},{2,50},{3,51},{4,52},{5,53},{6,54},{7,55},{8,56},{9,... | collective-permute-start | bytes 786440 | tf_op jit(solution)/shard_map/ppermute | solution.py:52
  59.5 3.0 %collective-permute-start.4 = (f32[512,128]{1,0:T(8,128)S(1)}, f32[512,128]{1,0:T(8,128)S(1)}, u32[]{:S(2)}, u32[]{:S(2)}) collective-permute-start(f32[512,128]{1,0:T(8,128)S(1)} %collective-permute-done.3), channel_id=1, source_target_pairs={{0,16},{1,17},{2,18},{3,19},{4,20},{5,21},{6,22},{7,23},{8,24},{9,... | collective-permute-start | bytes 786440 | tf_op jit(solution)/shard_map/ppermute | solution.py:52
  62.5 1.0 constant_dynamic-update-slice_fusion.7
  63.6 0.0 copy-start.2
  63.6 4.0 %collective-permute-start.10 = (f32[2048,128]{1,0:T(8,128)S(1)}, f32[2048,128]{1,0:T(8,128)S(1)}, u32[]{:S(2)}, u32[]{:S(2)}) collective-permute-start(f32[2048,128]{1,0:T(8,128)S(1)} %constant_dynamic-update-slice_fusion.4.refs_0_), channel_id=1, source_target_pairs={{0,48},{1,49},{2,50},{3,51},{4,52},{5,53},{6,54},{7,55},{8,56},{9,... | collective-permute-start | bytes 3145736 | tf_op jit(solution)/shard_map/ppermute | solution.py:52
  67.6 1.9 %collective-permute-start.9 = (f32[2048,128]{1,0:T(8,128)S(1)}, f32[2048,128]{1,0:T(8,128)S(1)}, u32[]{:S(2)}, u32[]{:S(2)}) collective-permute-start(f32[2048,128]{1,0:T(8,128)S(1)} %constant_dynamic-update-slice_fusion.4.refs_0_), channel_id=1, source_target_pairs={{0,16},{1,17},{2,18},{3,19},{4,20},{5,21},{6,22},{7,23},{8,24},{9,... | collective-permute-start | bytes 3145736 | tf_op jit(solution)/shard_map/ppermute | solution.py:52
  69.6 0.0 collective-permute-done.6
  69.6 0.7 collective-permute-done.5
  70.3 0.0 collective-permute-done.4
  70.4 4.6 %collective-permute-start.8 = (f32[2048,128]{1,0:T(8,128)S(1)}, f32[2048,128]{1,0:T(8,128)S(1)}, u32[]{:S(2)}, u32[]{:S(2)}) collective-permute-start(f32[2048,128]{1,0:T(8,128)S(1)} %constant_dynamic-update-slice_fusion.refs_0_), channel_id=1, source_target_pairs={{0,192},{1,193},{2,194},{3,195},{4,196},{5,197},{6,198},{7,199},{8... | collective-permute-start | bytes 3145736 | tf_op jit(solution)/shard_map/ppermute | solution.py:52
  75.0 1.9 %collective-permute-start.7 = (f32[2048,128]{1,0:T(8,128)S(1)}, f32[2048,128]{1,0:T(8,128)S(1)}, u32[]{:S(2)}, u32[]{:S(2)}) collective-permute-start(f32[2048,128]{1,0:T(8,128)S(1)} %constant_dynamic-update-slice_fusion.refs_0_), channel_id=1, source_target_pairs={{0,64},{1,65},{2,66},{3,67},{4,68},{5,69},{6,70},{7,71},{8,72},{9,... | collective-permute-start | bytes 3145736 | tf_op jit(solution)/shard_map/ppermute | solution.py:52
  76.9 14.2 %collective-permute-done.10.refs_2_ = f32[2048,128]{1,0:T(8,128)S(1)} collective-permute-done((f32[2048,128]{1,0:T(8,128)S(1)}, f32[2048,128]{1,0:T(8,128)S(1)}, u32[]{:S(2)}, u32[]{:S(2)}) %collective-permute-start.10) | collective-permute-done | bytes 1048608 | tf_op jit(solution)/shard_map/ppermute | solution.py:52
  91.2 0.8 slice.17
  92.0 4.5 %collective-permute-start.12 = (f32[1024,128]{1,0:T(8,128)}, f32[1024,128]{1,0:T(8,128)}, u32[]{:S(2)}, u32[]{:S(2)}) collective-permute-start(f32[1024,128]{1,0:T(8,128)} %slice.17), channel_id=1, source_target_pairs={{0,48},{1,49},{2,50},{3,51},{4,52},{5,53},{6,54},{7,55},{8,56},{9,... | collective-permute-start | bytes 1572872 | tf_op jit(solution)/shard_map/ppermute | solution.py:52
  96.6 0.0 collective-permute-done.9.refs_1_
  96.6 0.9 slice.16
  97.5 1.9 %collective-permute-start.11 = (f32[1024,128]{1,0:T(8,128)}, f32[1024,128]{1,0:T(8,128)}, u32[]{:S(2)}, u32[]{:S(2)}) collective-permute-start(f32[1024,128]{1,0:T(8,128)} %slice.16), channel_id=1, source_target_pairs={{0,16},{1,17},{2,18},{3,19},{4,20},{5,21},{6,22},{7,23},{8,24},{9,... | collective-permute-start | bytes 1572872 | tf_op jit(solution)/shard_map/ppermute | solution.py:52
  99.4 0.0 collective-permute-done.8.refs_2_
  99.4 0.9 slice.19
  100.3 4.9 %collective-permute-start.14 = (f32[1024,128]{1,0:T(8,128)}, f32[1024,128]{1,0:T(8,128)}, u32[]{:S(2)}, u32[]{:S(2)}) collective-permute-start(f32[1024,128]{1,0:T(8,128)} %slice.19), channel_id=1, source_target_pairs={{0,192},{1,193},{2,194},{3,195},{4,196},{5,197},{6,198},{7,199},{8... | collective-permute-start | bytes 1572872 | tf_op jit(solution)/shard_map/ppermute | solution.py:52
  105.2 0.0 collective-permute-done.7.refs_1_
  105.2 0.8 slice.18
  106.1 1.0 copy-done
  107.1 1.9 %collective-permute-start.13 = (f32[1024,128]{1,0:T(8,128)}, f32[1024,128]{1,0:T(8,128)}, u32[]{:S(2)}, u32[]{:S(2)}) collective-permute-start(f32[1024,128]{1,0:T(8,128)} %slice.18), channel_id=1, source_target_pairs={{0,64},{1,65},{2,66},{3,67},{4,68},{5,69},{6,70},{7,71},{8,72},{9,... | collective-permute-start | bytes 1572872 | tf_op jit(solution)/shard_map/ppermute | solution.py:52
  109.0 0.0 all-gather.2.cloned.1.call-done.refs_0_
  109.0 2.1 %collective-permute-start.15 = (f32[6208,128]{1,0:T(8,128)}, f32[6208,128]{1,0:T(8,128)S(1)}, u32[]{:S(2)}, u32[]{:S(2)}) collective-permute-start(f32[6208,128]{1,0:T(8,128)} %all-gather.2.cloned.1.call-done.refs_0_), channel_id=1, source_target_pairs={{0,1},{1,0},{2,3},{3,2},{4,5},{5,4},{6,7},{7,6},{8,9},{9,8},{10,11... | collective-permute-start | bytes 9535496 | tf_op jit(solution)/shard_map/ppermute | solution.py:52
  111.1 0.0 collective-permute-done.12.refs_4_
  111.1 2.3 %collective-permute-done.11.refs_3_ = f32[1024,128]{1,0:T(8,128)} collective-permute-done((f32[1024,128]{1,0:T(8,128)}, f32[1024,128]{1,0:T(8,128)}, u32[]{:S(2)}, u32[]{:S(2)}) %collective-permute-start.11) | collective-permute-done | bytes 524320 | tf_op jit(solution)/shard_map/ppermute | solution.py:52
  113.4 1.2 copy-done.3
  114.7 2.2 %shard_map.84 = (bf16[1024,512]{1,0:T(8,128)(2,1)S(1)}, bf16[1024,512]{1,0:T(8,128)(2,1)S(1)}, bf16[1024,512]{1,0:T(8,128)(2,1)S(1)}, bf16[1024,512]{1,0:T(8,128)(2,1)S(1)}) custom-call(f32[2048,128]{1,0:T(8,128)S(1)} %copy-done.3, f32[2048,128]{1,0:T(8,128)S(1)} %collective-permute-done.9.refs_1_, f32[2048,128]{1,0:T(8,128)S(1)} %collective-permute-done.10.refs_2_, ...), custom_call_target="tpu_custom_call" | custom-call | tf_op jit(solution)/shard_map/pallas_call | solution.py:198
  116.8 6.0 %collective-permute-done.13.refs_3_ = f32[1024,128]{1,0:T(8,128)} collective-permute-done((f32[1024,128]{1,0:T(8,128)}, f32[1024,128]{1,0:T(8,128)}, u32[]{:S(2)}, u32[]{:S(2)}) %collective-permute-start.13) | collective-permute-done | bytes 524320 | tf_op jit(solution)/shard_map/ppermute | solution.py:52
  122.8 2.0 %shard_map.85 = (bf16[1024,512]{1,0:T(8,128)(2,1)S(1)}, bf16[1024,512]{1,0:T(8,128)(2,1)S(1)}, bf16[1024,512]{1,0:T(8,128)(2,1)S(1)}, bf16[1024,512]{1,0:T(8,128)(2,1)S(1)}) custom-call(f32[2048,128]{1,0:T(8,128)S(1)} %copy-done.5, f32[2048,128]{1,0:T(8,128)S(1)} %copy-done.1, f32[2048,128]{1,0:T(8,128)S(1)} %collective-permute-done.8.refs_2_, ...), custom_call_target="tpu_custom_call" | custom-call | tf_op jit(solution)/shard_map/pallas_call | solution.py:198
  124.8 0.0 copy-start.6
  124.9 4.7 %shard_map.86.refs_1_ = f32[512,512]{1,0:T(8,128)S(1)} custom-call(f32[6208,128]{1,0:T(8,128)S(1)} %copy-done.7, bf16[1024,512]{1,0:T(8,128)(2,1)S(1)} %get-tuple-element.35.refs_1_, bf16[1024,512]{1,0:T(8,128)(2,1)S(1)} %get-tuple-element.36.refs_2_, bf16[1024,512]{1,0:T(8,128)(2,1)S(1)} %get-tuple-element.39.refs_3_, ...), custom_call_target="tpu_custom_call" | custom-call | flops 32212254720 | bytes 4194304 | tf_op jit(solution)/shard_map/pallas_call | solution.py:175
  129.6 0.0 collective-permute-done.15.refs_2_
  129.6 6.2 %shard_map.87 = f32[4,4,128,128]{3,2,1,0:T(8,128)} custom-call(s32[4,4]{1,0:T(4,128)S(1)} %copy-done.6, f32[512,512]{1,0:T(8,128)S(1)} %shard_map.86.refs_1_, f32[6208,128]{1,0:T(8,128)S(1)} %collective-permute-done.15.refs_2_, bf16[1024,512]{1,0:T(8,128)(2,1)S(1)} %get-tuple-element.41.refs_3_, bf16[1024,512]{1,0:T(8,128)(2,1)S(1)} %get-tuple-element.42.refs_4_, ...), custom_call_target="tpu_custom_call" | custom-call | flops 1073741824 | bytes 4194304 | tf_op jit(solution)/shard_map/pallas_call | solution.py:175
  (21 shorter events, 0.2 us)
Async XLA Ops:
  6.5 102.5 %all-gather.2.cloned.1.call-start = ((), (), s32[]{:S(2)}) async-start(), calls=%async_computation | async-start | bytes 3575808 | tf_op jit(solution)/shard_map/all_gather | solution.py:223
  10.2 41.3 %collective-permute-start.3 = (f32[512,128]{1,0:T(8,128)}, f32[512,128]{1,0:T(8,128)S(1)}, u32[]{:S(2)}, u32[]{:S(2)}) collective-permute-start(f32[512,128]{1,0:T(8,128)} %shard_map.83), channel_id=1, source_target_pairs={{0,256},{1,257},{2,258},{3,259},{4,260},{5,261},{6,262},{7,263},{8... | collective-permute-start | bytes 786440 | tf_op jit(solution)/shard_map/ppermute | solution.py:52
  19.3 32.3 %collective-permute-start.2 = (f32[512,128]{1,0:T(8,128)}, f32[512,128]{1,0:T(8,128)S(1)}, u32[]{:S(2)}, u32[]{:S(2)}) collective-permute-start(f32[512,128]{1,0:T(8,128)} %shard_map.83), channel_id=1, source_target_pairs={{0,128},{1,129},{2,130},{3,131},{4,132},{5,133},{6,134},{7,135},{8... | collective-permute-start | bytes 786440 | tf_op jit(solution)/shard_map/ppermute | solution.py:52
  24.2 27.3 %collective-permute-start.1 = (f32[512,128]{1,0:T(8,128)}, f32[512,128]{1,0:T(8,128)S(1)}, u32[]{:S(2)}, u32[]{:S(2)}) collective-permute-start(f32[512,128]{1,0:T(8,128)} %shard_map.83), channel_id=1, source_target_pairs={{0,192},{1,193},{2,194},{3,195},{4,196},{5,197},{6,198},{7,199},{8... | collective-permute-start | bytes 786440 | tf_op jit(solution)/shard_map/ppermute | solution.py:52
  27.3 24.3 %collective-permute-start = (f32[512,128]{1,0:T(8,128)}, f32[512,128]{1,0:T(8,128)S(1)}, u32[]{:S(2)}, u32[]{:S(2)}) collective-permute-start(f32[512,128]{1,0:T(8,128)} %shard_map.83), channel_id=1, source_target_pairs={{0,64},{1,65},{2,66},{3,67},{4,68},{5,69},{6,70},{7,71},{8,72},{9,... | collective-permute-start | bytes 786440 | tf_op jit(solution)/shard_map/ppermute | solution.py:52
  51.6 18.0 %collective-permute-start.6 = (f32[512,128]{1,0:T(8,128)S(1)}, f32[512,128]{1,0:T(8,128)S(1)}, u32[]{:S(2)}, u32[]{:S(2)}) collective-permute-start(f32[512,128]{1,0:T(8,128)S(1)} %collective-permute-done.3), channel_id=1, source_target_pairs={{0,32},{1,33},{2,34},{3,35},{4,36},{5,37},{6,38},{7,39},{8,40},{9,... | collective-permute-start | bytes 786440 | tf_op jit(solution)/shard_map/ppermute | solution.py:52
  56.7 13.6 %collective-permute-start.5 = (f32[512,128]{1,0:T(8,128)S(1)}, f32[512,128]{1,0:T(8,128)S(1)}, u32[]{:S(2)}, u32[]{:S(2)}) collective-permute-start(f32[512,128]{1,0:T(8,128)S(1)} %collective-permute-done.3), channel_id=1, source_target_pairs={{0,48},{1,49},{2,50},{3,51},{4,52},{5,53},{6,54},{7,55},{8,56},{9,... | collective-permute-start | bytes 786440 | tf_op jit(solution)/shard_map/ppermute | solution.py:52
  59.5 10.8 %collective-permute-start.4 = (f32[512,128]{1,0:T(8,128)S(1)}, f32[512,128]{1,0:T(8,128)S(1)}, u32[]{:S(2)}, u32[]{:S(2)}) collective-permute-start(f32[512,128]{1,0:T(8,128)S(1)} %collective-permute-done.3), channel_id=1, source_target_pairs={{0,16},{1,17},{2,18},{3,19},{4,20},{5,21},{6,22},{7,23},{8,24},{9,... | collective-permute-start | bytes 786440 | tf_op jit(solution)/shard_map/ppermute | solution.py:52
  63.6 42.5 %copy-start.2 = (f32[2048,128]{1,0:T(8,128)}, f32[2048,128]{1,0:T(8,128)S(1)}, u32[]{:S(2)}) copy-start(f32[2048,128]{1,0:T(8,128)S(1)} %constant_dynamic-update-slice_fusion.4.refs_0_) | copy-start | bytes 3145732
  63.6 27.6 %collective-permute-start.10 = (f32[2048,128]{1,0:T(8,128)S(1)}, f32[2048,128]{1,0:T(8,128)S(1)}, u32[]{:S(2)}, u32[]{:S(2)}) collective-permute-start(f32[2048,128]{1,0:T(8,128)S(1)} %constant_dynamic-update-slice_fusion.4.refs_0_), channel_id=1, source_target_pairs={{0,48},{1,49},{2,50},{3,51},{4,52},{5,53},{6,54},{7,55},{8,56},{9,... | collective-permute-start | bytes 3145736 | tf_op jit(solution)/shard_map/ppermute | solution.py:52
  67.6 28.9 %collective-permute-start.9 = (f32[2048,128]{1,0:T(8,128)S(1)}, f32[2048,128]{1,0:T(8,128)S(1)}, u32[]{:S(2)}, u32[]{:S(2)}) collective-permute-start(f32[2048,128]{1,0:T(8,128)S(1)} %constant_dynamic-update-slice_fusion.4.refs_0_), channel_id=1, source_target_pairs={{0,16},{1,17},{2,18},{3,19},{4,20},{5,21},{6,22},{7,23},{8,24},{9,... | collective-permute-start | bytes 3145736 | tf_op jit(solution)/shard_map/ppermute | solution.py:52
  70.4 35.7 %copy-start.4 = (f32[2048,128]{1,0:T(8,128)}, f32[2048,128]{1,0:T(8,128)S(1)}, u32[]{:S(2)}) copy-start(f32[2048,128]{1,0:T(8,128)S(1)} %constant_dynamic-update-slice_fusion.refs_0_) | copy-start | bytes 3145732
  70.4 29.0 %collective-permute-start.8 = (f32[2048,128]{1,0:T(8,128)S(1)}, f32[2048,128]{1,0:T(8,128)S(1)}, u32[]{:S(2)}, u32[]{:S(2)}) collective-permute-start(f32[2048,128]{1,0:T(8,128)S(1)} %constant_dynamic-update-slice_fusion.refs_0_), channel_id=1, source_target_pairs={{0,192},{1,193},{2,194},{3,195},{4,196},{5,197},{6,198},{7,199},{8... | collective-permute-start | bytes 3145736 | tf_op jit(solution)/shard_map/ppermute | solution.py:52
  75.0 30.2 %collective-permute-start.7 = (f32[2048,128]{1,0:T(8,128)S(1)}, f32[2048,128]{1,0:T(8,128)S(1)}, u32[]{:S(2)}, u32[]{:S(2)}) collective-permute-start(f32[2048,128]{1,0:T(8,128)S(1)} %constant_dynamic-update-slice_fusion.refs_0_), channel_id=1, source_target_pairs={{0,64},{1,65},{2,66},{3,67},{4,68},{5,69},{6,70},{7,71},{8,72},{9,... | collective-permute-start | bytes 3145736 | tf_op jit(solution)/shard_map/ppermute | solution.py:52
  92.0 19.1 %collective-permute-start.12 = (f32[1024,128]{1,0:T(8,128)}, f32[1024,128]{1,0:T(8,128)}, u32[]{:S(2)}, u32[]{:S(2)}) collective-permute-start(f32[1024,128]{1,0:T(8,128)} %slice.17), channel_id=1, source_target_pairs={{0,48},{1,49},{2,50},{3,51},{4,52},{5,53},{6,54},{7,55},{8,56},{9,... | collective-permute-start | bytes 1572872 | tf_op jit(solution)/shard_map/ppermute | solution.py:52
  97.5 16.0 %collective-permute-start.11 = (f32[1024,128]{1,0:T(8,128)}, f32[1024,128]{1,0:T(8,128)}, u32[]{:S(2)}, u32[]{:S(2)}) collective-permute-start(f32[1024,128]{1,0:T(8,128)} %slice.16), channel_id=1, source_target_pairs={{0,16},{1,17},{2,18},{3,19},{4,20},{5,21},{6,22},{7,23},{8,24},{9,... | collective-permute-start | bytes 1572872 | tf_op jit(solution)/shard_map/ppermute | solution.py:52
  100.3 16.5 %collective-permute-start.14 = (f32[1024,128]{1,0:T(8,128)}, f32[1024,128]{1,0:T(8,128)}, u32[]{:S(2)}, u32[]{:S(2)}) collective-permute-start(f32[1024,128]{1,0:T(8,128)} %slice.19), channel_id=1, source_target_pairs={{0,192},{1,193},{2,194},{3,195},{4,196},{5,197},{6,198},{7,199},{8... | collective-permute-start | bytes 1572872 | tf_op jit(solution)/shard_map/ppermute | solution.py:52
  106.1 1.0 copy-start
  107.1 15.7 %collective-permute-start.13 = (f32[1024,128]{1,0:T(8,128)}, f32[1024,128]{1,0:T(8,128)}, u32[]{:S(2)}, u32[]{:S(2)}) collective-permute-start(f32[1024,128]{1,0:T(8,128)} %slice.18), channel_id=1, source_target_pairs={{0,64},{1,65},{2,66},{3,67},{4,68},{5,69},{6,70},{7,71},{8,72},{9,... | collective-permute-start | bytes 1572872 | tf_op jit(solution)/shard_map/ppermute | solution.py:52
  109.0 13.8 %copy-start.1 = (f32[2048,128]{1,0:T(8,128)S(1)}, f32[2048,128]{1,0:T(8,128)}, u32[]{:S(2)}) copy-start(f32[2048,128]{1,0:T(8,128)} %copy-done) | copy-start | bytes 3145732
  109.0 20.6 %collective-permute-start.15 = (f32[6208,128]{1,0:T(8,128)}, f32[6208,128]{1,0:T(8,128)S(1)}, u32[]{:S(2)}, u32[]{:S(2)}) collective-permute-start(f32[6208,128]{1,0:T(8,128)} %all-gather.2.cloned.1.call-done.refs_0_), channel_id=1, source_target_pairs={{0,1},{1,0},{2,3},{3,2},{4,5},{5,4},{6,7},{7,6},{8,9},{9,8},{10,11... | collective-permute-start | bytes 9535496 | tf_op jit(solution)/shard_map/ppermute | solution.py:52
  113.4 1.2 copy-start.3
  114.7 8.2 %copy-start.5 = (f32[2048,128]{1,0:T(8,128)S(1)}, f32[2048,128]{1,0:T(8,128)}, u32[]{:S(2)}) copy-start(f32[2048,128]{1,0:T(8,128)} %copy-done.4) | copy-start | bytes 3145732
  114.7 10.2 %copy-start.7 = (f32[6208,128]{1,0:T(8,128)S(1)}, f32[6208,128]{1,0:T(8,128)}, u32[]{:S(2)}) copy-start(f32[6208,128]{1,0:T(8,128)} %all-gather.2.cloned.1.call-done.refs_0_) | copy-start | bytes 9535492
  124.8 4.7 %copy-start.6 = (s32[4,4]{1,0:T(4,128)S(1)}, s32[4,4]{1,0:T(4,128)}, u32[]{:S(2)}) copy-start(s32[4,4]{1,0:T(4,128)} %refs_0_.1) | copy-start | bytes 196
Sparse Core Ops, SparseCore 0:
  9.4 92.9 all-gather.1

commit v7 on v6

--- a/solution.py
+++ b/solution.py
@@ -91,6 +91,11 @@
     for j in range(4):
         columns = jnp.where(occupied[0, j] > 0, col_sizes[j], 0)
         out[j * BS:(j + 1) * BS, :] = jnp.where((line < used) & (lane < columns), blocks[0, j], 0.0)
+
+
+def pack_both(a_blocks, b_blocks, a_occupied, b_occupied, row_sizes, k_sizes, col_sizes, left, right):
+    pack_left(a_blocks, a_occupied, row_sizes, k_sizes, left)
+    mask_right(b_blocks, b_occupied, k_sizes, col_sizes, right)
 
 
 def split(value):
@@ -205,20 +210,17 @@
 
 
 def on_device(a_blocks, b_blocks, a_occupied, b_occupied, c_filter, row_sizes, k_sizes, col_sizes):
-    right = pl.pallas_call(
-        mask_right,
-        out_shape=jax.ShapeDtypeStruct((4 * BS, BS), jnp.float32),
-        in_specs=[VMEM, SMEM, SMEM, SMEM],
-        out_specs=VMEM,
-    )(b_blocks, b_occupied, k_sizes, col_sizes)
+    left, right = pl.pallas_call(
+        pack_both,
+        out_shape=[
+            jax.ShapeDtypeStruct((PAY_ROWS, BS), jnp.float32),
+            jax.ShapeDtypeStruct((4 * BS, BS), jnp.float32),
+        ],
+        in_specs=[VMEM, VMEM] + [SMEM] * 5,
+        out_specs=[VMEM, VMEM],
+    )(a_blocks, b_blocks, a_occupied.T, b_occupied, row_sizes, k_sizes, col_sizes)
     first = [right, *near(right, along_x)]
     partner = send(right, other_half())
-    left = pl.pallas_call(
-        pack_left,
-        out_shape=jax.ShapeDtypeStruct((PAY_ROWS, BS), jnp.float32),
-        in_specs=[VMEM, SMEM, SMEM, SMEM],
-        out_specs=VMEM,
-    )(a_blocks, a_occupied.T, row_sizes, k_sizes)
     same_core = [[zl * NC + core for zl in range(NZL)] for core in range(NC)]
     own = lax.all_gather(left, "col", axis_index_groups=same_core, tiled=True)
     *first, partner = lax.optimization_barrier((*first, partner))

time: 143 us -> 142 us (level)
  the two profiles are of different devices: /device:TPU:192 before, /device:TPU:56 now
where the time goes in v7:
time: 142 us; the launch traced here: 141 us
  starting transfers between devices  65.1 us (46%)
  waiting for transfers between devices  38.3 us (27%)
  Pallas kernels  17.2 us (12%)
  between operations  13.8 us (10%)
  local copies, waits for them, and re-layouts  6.84 us (5%)
    ppermute x16, starting transfers between devices, send(): return lax.ppermute(value, AXES, pairs)  65.1 us
    ppermute x16, waiting for transfers between devices, send(): return lax.ppermute(value, AXES, pairs)  38.3 us
    pallas_call x2, Pallas kernels, add_products(): pl.pallas_call(functools.partial(multiply, last), out_shape=jax.ShapeDtyp...  11 us
    pallas_call x2, Pallas kernels, prepare(): pl.pallas_call(functools.partial(prepare_right, along_first), out_shape=[...  4.15 us
    unnamed x22, local copies, waits for them, and re-layouts  3.34 us
  transfers between devices with their start and end apart: 17, of which 3 were waited for; matrix products, arithmetic and copies ran while one was open for 3% of the time, Pallas kernels for 6%

profile of v7, /device:TPU:56, one launch (start us, length us, event | category | flops | bytes accessed | tf_op | source)
XLA Modules:
  0.0 141.1 jit_solution(8706879023369174064)
XLA Ops:
  6.5 2.1 %shard_map.82 = (f32[776,128]{1,0:T(8,128)}, f32[512,128]{1,0:T(8,128)}) custom-call(f32[4,2,128,128]{3,2,1,0:T(8,128)} %a_blocks.1, f32[1,4,128,128]{3,2,1,0:T(8,128)} %b_blocks.1, s32[2,4]{1,0:T(2,128)} %bitcast.1, s32[1,4]{1,0:T(1,128)} %b_occupied.1, s32[4]{0:T(128)} %row_sizes.1, s32[32]{0:T(128)} %k_sizes.1, s32[4]{0:T(128)} %col_sizes.1), custom_call_target="tpu_custom_call" | custom-call | tf_op jit(solution)/shard_map/pallas_call | solution.py:213
  8.6 0.0 all-gather.2.cloned.1.call-update
  8.6 14.8 %collective-permute-start.3 = (f32[512,128]{1,0:T(8,128)}, f32[512,128]{1,0:T(8,128)S(1)}, u32[]{:S(2)}, u32[]{:S(2)}) collective-permute-start(f32[512,128]{1,0:T(8,128)} %get-tuple-element.35), channel_id=1, source_target_pairs={{0,256},{1,257},{2,258},{3,259},{4,260},{5,261},{6,262},{7,263},{8... | collective-permute-start | bytes 786440 | tf_op jit(solution)/shard_map/ppermute | solution.py:52
  23.5 4.9 %collective-permute-start.2 = (f32[512,128]{1,0:T(8,128)}, f32[512,128]{1,0:T(8,128)S(1)}, u32[]{:S(2)}, u32[]{:S(2)}) collective-permute-start(f32[512,128]{1,0:T(8,128)} %get-tuple-element.35), channel_id=1, source_target_pairs={{0,128},{1,129},{2,130},{3,131},{4,132},{5,133},{6,134},{7,135},{8... | collective-permute-start | bytes 786440 | tf_op jit(solution)/shard_map/ppermute | solution.py:52
  28.4 3.1 %collective-permute-start.1 = (f32[512,128]{1,0:T(8,128)}, f32[512,128]{1,0:T(8,128)S(1)}, u32[]{:S(2)}, u32[]{:S(2)}) collective-permute-start(f32[512,128]{1,0:T(8,128)} %get-tuple-element.35), channel_id=1, source_target_pairs={{0,192},{1,193},{2,194},{3,195},{4,196},{5,197},{6,198},{7,199},{8... | collective-permute-start | bytes 786440 | tf_op jit(solution)/shard_map/ppermute | solution.py:52
  31.5 2.8 %collective-permute-start = (f32[512,128]{1,0:T(8,128)}, f32[512,128]{1,0:T(8,128)S(1)}, u32[]{:S(2)}, u32[]{:S(2)}) collective-permute-start(f32[512,128]{1,0:T(8,128)} %get-tuple-element.35), channel_id=1, source_target_pairs={{0,64},{1,65},{2,66},{3,67},{4,68},{5,69},{6,70},{7,71},{8,72},{9,... | collective-permute-start | bytes 786440 | tf_op jit(solution)/shard_map/ppermute | solution.py:52
  34.2 22.7 %collective-permute-done.3 = f32[512,128]{1,0:T(8,128)S(1)} collective-permute-done((f32[512,128]{1,0:T(8,128)}, f32[512,128]{1,0:T(8,128)S(1)}, u32[]{:S(2)}, u32[]{:S(2)}) %collective-permute-start.3) | collective-permute-done | bytes 262176 | tf_op jit(solution)/shard_map/ppermute | solution.py:52
  56.9 0.0 collective-permute-done.2
  56.9 0.0 collective-permute-done.1
  56.9 0.0 collective-permute-done
  56.9 3.1 %collective-permute-start.6 = (f32[512,128]{1,0:T(8,128)S(1)}, f32[512,128]{1,0:T(8,128)S(1)}, u32[]{:S(2)}, u32[]{:S(2)}) collective-permute-start(f32[512,128]{1,0:T(8,128)S(1)} %collective-permute-done.3), channel_id=1, source_target_pairs={{0,32},{1,33},{2,34},{3,35},{4,36},{5,37},{6,38},{7,39},{8,40},{9,... | collective-permute-start | bytes 786440 | tf_op jit(solution)/shard_map/ppermute | solution.py:52
  60.1 1.9 %collective-permute-start.5 = (f32[512,128]{1,0:T(8,128)S(1)}, f32[512,128]{1,0:T(8,128)S(1)}, u32[]{:S(2)}, u32[]{:S(2)}) collective-permute-start(f32[512,128]{1,0:T(8,128)S(1)} %collective-permute-done.3), channel_id=1, source_target_pairs={{0,48},{1,49},{2,50},{3,51},{4,52},{5,53},{6,54},{7,55},{8,56},{9,... | collective-permute-start | bytes 786440 | tf_op jit(solution)/shard_map/ppermute | solution.py:52
  62.0 5.1 %collective-permute-start.4 = (f32[512,128]{1,0:T(8,128)S(1)}, f32[512,128]{1,0:T(8,128)S(1)}, u32[]{:S(2)}, u32[]{:S(2)}) collective-permute-start(f32[512,128]{1,0:T(8,128)S(1)} %collective-permute-done.3), channel_id=1, source_target_pairs={{0,16},{1,17},{2,18},{3,19},{4,20},{5,21},{6,22},{7,23},{8,24},{9,... | collective-permute-start | bytes 786440 | tf_op jit(solution)/shard_map/ppermute | solution.py:52
  67.2 1.0 constant_dynamic-update-slice_fusion.7
  68.2 0.0 copy-start.2
  68.2 1.9 %collective-permute-start.10 = (f32[2048,128]{1,0:T(8,128)S(1)}, f32[2048,128]{1,0:T(8,128)S(1)}, u32[]{:S(2)}, u32[]{:S(2)}) collective-permute-start(f32[2048,128]{1,0:T(8,128)S(1)} %constant_dynamic-update-slice_fusion.4.refs_0_), channel_id=1, source_target_pairs={{0,48},{1,49},{2,50},{3,51},{4,52},{5,53},{6,54},{7,55},{8,56},{9,... | collective-permute-start | bytes 3145736 | tf_op jit(solution)/shard_map/ppermute | solution.py:52
  70.2 5.1 %collective-permute-start.9 = (f32[2048,128]{1,0:T(8,128)S(1)}, f32[2048,128]{1,0:T(8,128)S(1)}, u32[]{:S(2)}, u32[]{:S(2)}) collective-permute-start(f32[2048,128]{1,0:T(8,128)S(1)} %constant_dynamic-update-slice_fusion.4.refs_0_), channel_id=1, source_target_pairs={{0,16},{1,17},{2,18},{3,19},{4,20},{5,21},{6,22},{7,23},{8,24},{9,... | collective-permute-start | bytes 3145736 | tf_op jit(solution)/shard_map/ppermute | solution.py:52
  75.3 0.0 collective-permute-done.6
  75.3 0.0 collective-permute-done.5
  75.3 0.0 collective-permute-done.4
  75.4 4.7 %collective-permute-start.8 = (f32[2048,128]{1,0:T(8,128)S(1)}, f32[2048,128]{1,0:T(8,128)S(1)}, u32[]{:S(2)}, u32[]{:S(2)}) collective-permute-start(f32[2048,128]{1,0:T(8,128)S(1)} %constant_dynamic-update-slice_fusion.refs_0_), channel_id=1, source_target_pairs={{0,192},{1,193},{2,194},{3,195},{4,196},{5,197},{6,198},{7,199},{8... | collective-permute-start | bytes 3145736 | tf_op jit(solution)/shard_map/ppermute | solution.py:52
  80.1 1.9 %collective-permute-start.7 = (f32[2048,128]{1,0:T(8,128)S(1)}, f32[2048,128]{1,0:T(8,128)S(1)}, u32[]{:S(2)}, u32[]{:S(2)}) collective-permute-start(f32[2048,128]{1,0:T(8,128)S(1)} %constant_dynamic-update-slice_fusion.refs_0_), channel_id=1, source_target_pairs={{0,64},{1,65},{2,66},{3,67},{4,68},{5,69},{6,70},{7,71},{8,72},{9,... | collective-permute-start | bytes 3145736 | tf_op jit(solution)/shard_map/ppermute | solution.py:52
  82.0 10.4 %collective-permute-done.10.refs_2_ = f32[2048,128]{1,0:T(8,128)S(1)} collective-permute-done((f32[2048,128]{1,0:T(8,128)S(1)}, f32[2048,128]{1,0:T(8,128)S(1)}, u32[]{:S(2)}, u32[]{:S(2)}) %collective-permute-start.10) | collective-permute-done | bytes 1048608 | tf_op jit(solution)/shard_map/ppermute | solution.py:52
  92.4 0.8 slice.17
  93.3 1.9 %collective-permute-start.12 = (f32[1024,128]{1,0:T(8,128)}, f32[1024,128]{1,0:T(8,128)}, u32[]{:S(2)}, u32[]{:S(2)}) collective-permute-start(f32[1024,128]{1,0:T(8,128)} %slice.17), channel_id=1, source_target_pairs={{0,48},{1,49},{2,50},{3,51},{4,52},{5,53},{6,54},{7,55},{8,56},{9,... | collective-permute-start | bytes 1572872 | tf_op jit(solution)/shard_map/ppermute | solution.py:52
  95.2 0.0 collective-permute-done.9.refs_1_
  95.2 0.9 slice.16
  96.1 5.1 %collective-permute-start.11 = (f32[1024,128]{1,0:T(8,128)}, f32[1024,128]{1,0:T(8,128)}, u32[]{:S(2)}, u32[]{:S(2)}) collective-permute-start(f32[1024,128]{1,0:T(8,128)} %slice.16), channel_id=1, source_target_pairs={{0,16},{1,17},{2,18},{3,19},{4,20},{5,21},{6,22},{7,23},{8,24},{9,... | collective-permute-start | bytes 1572872 | tf_op jit(solution)/shard_map/ppermute | solution.py:52
  101.2 0.0 collective-permute-done.8.refs_2_
  101.3 0.9 slice.19
  102.1 4.7 %collective-permute-start.14 = (f32[1024,128]{1,0:T(8,128)}, f32[1024,128]{1,0:T(8,128)}, u32[]{:S(2)}, u32[]{:S(2)}) collective-permute-start(f32[1024,128]{1,0:T(8,128)} %slice.19), channel_id=1, source_target_pairs={{0,192},{1,193},{2,194},{3,195},{4,196},{5,197},{6,198},{7,199},{8... | collective-permute-start | bytes 1572872 | tf_op jit(solution)/shard_map/ppermute | solution.py:52
  106.8 0.0 collective-permute-done.7.refs_1_
  106.8 0.8 slice.18
  107.6 1.0 copy-done
  108.7 1.9 %collective-permute-start.13 = (f32[1024,128]{1,0:T(8,128)}, f32[1024,128]{1,0:T(8,128)}, u32[]{:S(2)}, u32[]{:S(2)}) collective-permute-start(f32[1024,128]{1,0:T(8,128)} %slice.18), channel_id=1, source_target_pairs={{0,64},{1,65},{2,66},{3,67},{4,68},{5,69},{6,70},{7,71},{8,72},{9,... | collective-permute-start | bytes 1572872 | tf_op jit(solution)/shard_map/ppermute | solution.py:52
  110.6 0.0 all-gather.2.cloned.1.call-done.refs_0_
  110.6 2.1 %collective-permute-start.15 = (f32[6208,128]{1,0:T(8,128)}, f32[6208,128]{1,0:T(8,128)S(1)}, u32[]{:S(2)}, u32[]{:S(2)}) collective-permute-start(f32[6208,128]{1,0:T(8,128)} %all-gather.2.cloned.1.call-done.refs_0_), channel_id=1, source_target_pairs={{0,1},{1,0},{2,3},{3,2},{4,5},{5,4},{6,7},{7,6},{8,9},{9,8},{10,11... | collective-permute-start | bytes 9535496 | tf_op jit(solution)/shard_map/ppermute | solution.py:52
  112.7 0.0 collective-permute-done.12.refs_4_
  112.7 0.0 collective-permute-done.11.refs_3_
  112.7 0.0 copy-start.3
  112.7 1.2 copy-done.3
  113.9 2.1 %shard_map.83 = (bf16[1024,512]{1,0:T(8,128)(2,1)S(1)}, bf16[1024,512]{1,0:T(8,128)(2,1)S(1)}, bf16[1024,512]{1,0:T(8,128)(2,1)S(1)}, bf16[1024,512]{1,0:T(8,128)(2,1)S(1)}) custom-call(f32[2048,128]{1,0:T(8,128)S(1)} %copy-done.3, f32[2048,128]{1,0:T(8,128)S(1)} %collective-permute-done.9.refs_1_, f32[2048,128]{1,0:T(8,128)S(1)} %collective-permute-done.10.refs_2_, ...), custom_call_target="tpu_custom_call" | custom-call | tf_op jit(solution)/shard_map/pallas_call | solution.py:203
  116.1 0.0 collective-permute-done.14.refs_4_
  116.1 5.2 %collective-permute-done.13.refs_3_ = f32[1024,128]{1,0:T(8,128)} collective-permute-done((f32[1024,128]{1,0:T(8,128)}, f32[1024,128]{1,0:T(8,128)}, u32[]{:S(2)}, u32[]{:S(2)}) %collective-permute-start.13) | collective-permute-done | bytes 524320 | tf_op jit(solution)/shard_map/ppermute | solution.py:52
  121.3 2.0 %shard_map.84 = (bf16[1024,512]{1,0:T(8,128)(2,1)S(1)}, bf16[1024,512]{1,0:T(8,128)(2,1)S(1)}, bf16[1024,512]{1,0:T(8,128)(2,1)S(1)}, bf16[1024,512]{1,0:T(8,128)(2,1)S(1)}) custom-call(f32[2048,128]{1,0:T(8,128)S(1)} %copy-done.5, f32[2048,128]{1,0:T(8,128)S(1)} %copy-done.1, f32[2048,128]{1,0:T(8,128)S(1)} %collective-permute-done.8.refs_2_, ...), custom_call_target="tpu_custom_call" | custom-call | tf_op jit(solution)/shard_map/pallas_call | solution.py:203
  123.3 0.0 copy-start.6
  123.3 4.7 %shard_map.85.refs_1_ = f32[512,512]{1,0:T(8,128)S(1)} custom-call(f32[6208,128]{1,0:T(8,128)S(1)} %copy-done.7, bf16[1024,512]{1,0:T(8,128)(2,1)S(1)} %get-tuple-element.39.refs_1_, bf16[1024,512]{1,0:T(8,128)(2,1)S(1)} %get-tuple-element.40.refs_2_, bf16[1024,512]{1,0:T(8,128)(2,1)S(1)} %get-tuple-element.43.refs_3_, ...), custom_call_target="tpu_custom_call" | custom-call | flops 32212254720 | bytes 4194304 | tf_op jit(solution)/shard_map/pallas_call | solution.py:180
  128.0 6.2 %shard_map.86 = f32[4,4,128,128]{3,2,1,0:T(8,128)} custom-call(s32[4,4]{1,0:T(4,128)S(1)} %copy-done.6, f32[512,512]{1,0:T(8,128)S(1)} %shard_map.85.refs_1_, f32[6208,128]{1,0:T(8,128)S(1)} %collective-permute-done.15.refs_2_, bf16[1024,512]{1,0:T(8,128)(2,1)S(1)} %get-tuple-element.45.refs_3_, bf16[1024,512]{1,0:T(8,128)(2,1)S(1)} %get-tuple-element.46.refs_4_, ...), custom_call_target="tpu_custom_call" | custom-call | flops 1073741824 | bytes 4194304 | tf_op jit(solution)/shard_map/pallas_call | solution.py:180
  (20 shorter events, 0.2 us)
Async XLA Ops:
  6.5 104.1 %all-gather.2.cloned.1.call-start = ((), (), s32[]{:S(2)}) async-start(), calls=%async_computation | async-start | bytes 3575808 | tf_op jit(solution)/shard_map/all_gather | solution.py:225
  8.6 48.3 %collective-permute-start.3 = (f32[512,128]{1,0:T(8,128)}, f32[512,128]{1,0:T(8,128)S(1)}, u32[]{:S(2)}, u32[]{:S(2)}) collective-permute-start(f32[512,128]{1,0:T(8,128)} %get-tuple-element.35), channel_id=1, source_target_pairs={{0,256},{1,257},{2,258},{3,259},{4,260},{5,261},{6,262},{7,263},{8... | collective-permute-start | bytes 786440 | tf_op jit(solution)/shard_map/ppermute | solution.py:52
  23.5 33.5 %collective-permute-start.2 = (f32[512,128]{1,0:T(8,128)}, f32[512,128]{1,0:T(8,128)S(1)}, u32[]{:S(2)}, u32[]{:S(2)}) collective-permute-start(f32[512,128]{1,0:T(8,128)} %get-tuple-element.35), channel_id=1, source_target_pairs={{0,128},{1,129},{2,130},{3,131},{4,132},{5,133},{6,134},{7,135},{8... | collective-permute-start | bytes 786440 | tf_op jit(solution)/shard_map/ppermute | solution.py:52
  28.4 28.6 %collective-permute-start.1 = (f32[512,128]{1,0:T(8,128)}, f32[512,128]{1,0:T(8,128)S(1)}, u32[]{:S(2)}, u32[]{:S(2)}) collective-permute-start(f32[512,128]{1,0:T(8,128)} %get-tuple-element.35), channel_id=1, source_target_pairs={{0,192},{1,193},{2,194},{3,195},{4,196},{5,197},{6,198},{7,199},{8... | collective-permute-start | bytes 786440 | tf_op jit(solution)/shard_map/ppermute | solution.py:52
  31.5 25.5 %collective-permute-start = (f32[512,128]{1,0:T(8,128)}, f32[512,128]{1,0:T(8,128)S(1)}, u32[]{:S(2)}, u32[]{:S(2)}) collective-permute-start(f32[512,128]{1,0:T(8,128)} %get-tuple-element.35), channel_id=1, source_target_pairs={{0,64},{1,65},{2,66},{3,67},{4,68},{5,69},{6,70},{7,71},{8,72},{9,... | collective-permute-start | bytes 786440 | tf_op jit(solution)/shard_map/ppermute | solution.py:52
  56.9 18.4 %collective-permute-start.6 = (f32[512,128]{1,0:T(8,128)S(1)}, f32[512,128]{1,0:T(8,128)S(1)}, u32[]{:S(2)}, u32[]{:S(2)}) collective-permute-start(f32[512,128]{1,0:T(8,128)S(1)} %collective-permute-done.3), channel_id=1, source_target_pairs={{0,32},{1,33},{2,34},{3,35},{4,36},{5,37},{6,38},{7,39},{8,40},{9,... | collective-permute-start | bytes 786440 | tf_op jit(solution)/shard_map/ppermute | solution.py:52
  60.1 15.2 %collective-permute-start.5 = (f32[512,128]{1,0:T(8,128)S(1)}, f32[512,128]{1,0:T(8,128)S(1)}, u32[]{:S(2)}, u32[]{:S(2)}) collective-permute-start(f32[512,128]{1,0:T(8,128)S(1)} %collective-permute-done.3), channel_id=1, source_target_pairs={{0,48},{1,49},{2,50},{3,51},{4,52},{5,53},{6,54},{7,55},{8,56},{9,... | collective-permute-start | bytes 786440 | tf_op jit(solution)/shard_map/ppermute | solution.py:52
  62.0 13.3 %collective-permute-start.4 = (f32[512,128]{1,0:T(8,128)S(1)}, f32[512,128]{1,0:T(8,128)S(1)}, u32[]{:S(2)}, u32[]{:S(2)}) collective-permute-start(f32[512,128]{1,0:T(8,128)S(1)} %collective-permute-done.3), channel_id=1, source_target_pairs={{0,16},{1,17},{2,18},{3,19},{4,20},{5,21},{6,22},{7,23},{8,24},{9,... | collective-permute-start | bytes 786440 | tf_op jit(solution)/shard_map/ppermute | solution.py:52
  68.2 39.4 %copy-start.2 = (f32[2048,128]{1,0:T(8,128)}, f32[2048,128]{1,0:T(8,128)S(1)}, u32[]{:S(2)}) copy-start(f32[2048,128]{1,0:T(8,128)S(1)} %constant_dynamic-update-slice_fusion.4.refs_0_) | copy-start | bytes 3145732
  68.2 24.2 %collective-permute-start.10 = (f32[2048,128]{1,0:T(8,128)S(1)}, f32[2048,128]{1,0:T(8,128)S(1)}, u32[]{:S(2)}, u32[]{:S(2)}) collective-permute-start(f32[2048,128]{1,0:T(8,128)S(1)} %constant_dynamic-update-slice_fusion.4.refs_0_), channel_id=1, source_target_pairs={{0,48},{1,49},{2,50},{3,51},{4,52},{5,53},{6,54},{7,55},{8,56},{9,... | collective-permute-start | bytes 3145736 | tf_op jit(solution)/shard_map/ppermute | solution.py:52
  70.2 25.1 %collective-permute-start.9 = (f32[2048,128]{1,0:T(8,128)S(1)}, f32[2048,128]{1,0:T(8,128)S(1)}, u32[]{:S(2)}, u32[]{:S(2)}) collective-permute-start(f32[2048,128]{1,0:T(8,128)S(1)} %constant_dynamic-update-slice_fusion.4.refs_0_), channel_id=1, source_target_pairs={{0,16},{1,17},{2,18},{3,19},{4,20},{5,21},{6,22},{7,23},{8,24},{9,... | collective-permute-start | bytes 3145736 | tf_op jit(solution)/shard_map/ppermute | solution.py:52
  75.4 32.2 %copy-start.4 = (f32[2048,128]{1,0:T(8,128)}, f32[2048,128]{1,0:T(8,128)S(1)}, u32[]{:S(2)}) copy-start(f32[2048,128]{1,0:T(8,128)S(1)} %constant_dynamic-update-slice_fusion.refs_0_) | copy-start | bytes 3145732
  75.4 25.8 %collective-permute-start.8 = (f32[2048,128]{1,0:T(8,128)S(1)}, f32[2048,128]{1,0:T(8,128)S(1)}, u32[]{:S(2)}, u32[]{:S(2)}) collective-permute-start(f32[2048,128]{1,0:T(8,128)S(1)} %constant_dynamic-update-slice_fusion.refs_0_), channel_id=1, source_target_pairs={{0,192},{1,193},{2,194},{3,195},{4,196},{5,197},{6,198},{7,199},{8... | collective-permute-start | bytes 3145736 | tf_op jit(solution)/shard_map/ppermute | solution.py:52
  80.1 26.7 %collective-permute-start.7 = (f32[2048,128]{1,0:T(8,128)S(1)}, f32[2048,128]{1,0:T(8,128)S(1)}, u32[]{:S(2)}, u32[]{:S(2)}) collective-permute-start(f32[2048,128]{1,0:T(8,128)S(1)} %constant_dynamic-update-slice_fusion.refs_0_), channel_id=1, source_target_pairs={{0,64},{1,65},{2,66},{3,67},{4,68},{5,69},{6,70},{7,71},{8,72},{9,... | collective-permute-start | bytes 3145736 | tf_op jit(solution)/shard_map/ppermute | solution.py:52
  93.3 19.4 %collective-permute-start.12 = (f32[1024,128]{1,0:T(8,128)}, f32[1024,128]{1,0:T(8,128)}, u32[]{:S(2)}, u32[]{:S(2)}) collective-permute-start(f32[1024,128]{1,0:T(8,128)} %slice.17), channel_id=1, source_target_pairs={{0,48},{1,49},{2,50},{3,51},{4,52},{5,53},{6,54},{7,55},{8,56},{9,... | collective-permute-start | bytes 1572872 | tf_op jit(solution)/shard_map/ppermute | solution.py:52
  96.1 16.6 %collective-permute-start.11 = (f32[1024,128]{1,0:T(8,128)}, f32[1024,128]{1,0:T(8,128)}, u32[]{:S(2)}, u32[]{:S(2)}) collective-permute-start(f32[1024,128]{1,0:T(8,128)} %slice.16), channel_id=1, source_target_pairs={{0,16},{1,17},{2,18},{3,19},{4,20},{5,21},{6,22},{7,23},{8,24},{9,... | collective-permute-start | bytes 1572872 | tf_op jit(solution)/shard_map/ppermute | solution.py:52
  102.1 14.0 %collective-permute-start.14 = (f32[1024,128]{1,0:T(8,128)}, f32[1024,128]{1,0:T(8,128)}, u32[]{:S(2)}, u32[]{:S(2)}) collective-permute-start(f32[1024,128]{1,0:T(8,128)} %slice.19), channel_id=1, source_target_pairs={{0,192},{1,193},{2,194},{3,195},{4,196},{5,197},{6,198},{7,199},{8... | collective-permute-start | bytes 1572872 | tf_op jit(solution)/shard_map/ppermute | solution.py:52
  107.6 1.0 copy-start
  108.7 12.6 %collective-permute-start.13 = (f32[1024,128]{1,0:T(8,128)}, f32[1024,128]{1,0:T(8,128)}, u32[]{:S(2)}, u32[]{:S(2)}) collective-permute-start(f32[1024,128]{1,0:T(8,128)} %slice.18), channel_id=1, source_target_pairs={{0,64},{1,65},{2,66},{3,67},{4,68},{5,69},{6,70},{7,71},{8,72},{9,... | collective-permute-start | bytes 1572872 | tf_op jit(solution)/shard_map/ppermute | solution.py:52
  110.6 10.6 %copy-start.1 = (f32[2048,128]{1,0:T(8,128)S(1)}, f32[2048,128]{1,0:T(8,128)}, u32[]{:S(2)}) copy-start(f32[2048,128]{1,0:T(8,128)} %copy-done) | copy-start | bytes 3145732
  110.6 17.4 %collective-permute-start.15 = (f32[6208,128]{1,0:T(8,128)}, f32[6208,128]{1,0:T(8,128)S(1)}, u32[]{:S(2)}, u32[]{:S(2)}) collective-permute-start(f32[6208,128]{1,0:T(8,128)} %all-gather.2.cloned.1.call-done.refs_0_), channel_id=1, source_target_pairs={{0,1},{1,0},{2,3},{3,2},{4,5},{5,4},{6,7},{7,6},{8,9},{9,8},{10,11... | collective-permute-start | bytes 9535496 | tf_op jit(solution)/shard_map/ppermute | solution.py:52
  112.7 1.2 copy-start.3
  113.9 7.3 %copy-start.5 = (f32[2048,128]{1,0:T(8,128)S(1)}, f32[2048,128]{1,0:T(8,128)}, u32[]{:S(2)}) copy-start(f32[2048,128]{1,0:T(8,128)} %copy-done.4) | copy-start | bytes 3145732
  113.9 9.3 %copy-start.7 = (f32[6208,128]{1,0:T(8,128)S(1)}, f32[6208,128]{1,0:T(8,128)}, u32[]{:S(2)}) copy-start(f32[6208,128]{1,0:T(8,128)} %all-gather.2.cloned.1.call-done.refs_0_) | copy-start | bytes 9535492
  123.3 4.8 %copy-start.6 = (s32[4,4]{1,0:T(4,128)S(1)}, s32[4,4]{1,0:T(4,128)}, u32[]{:S(2)}) copy-start(s32[4,4]{1,0:T(4,128)} %refs_0_.1) | copy-start | bytes 196
Sparse Core Ops, SparseCore 0:
  9.4 97.7 all-gather.1
